TPU v7x, 32 devices: a whole 2x2x4 slice. The times are simulated.
32 devices in a mesh: shard: 2 (over y), ctx: 4 (over z), tp: 4 (over x, core).
Axes of the slice: x: 2, y: 2, z: 4, core: 2. Of those that a mesh axis runs over, the one named last changes fastest.
Arguments:
- hidden_in: bfloat16 [4, 1024, 2560], P('shard', 'ctx'), may hold values from -6 to 6
- cotangent: bfloat16 [4, 1024, 2560], P('shard', 'ctx'), may hold values from -6 to 6
- doc_lengths: int32 [4, 4], P('shard'), may hold values from 1 to 896, as said below
- attn_gain: bfloat16 [2560], P(('shard', 'ctx', 'tp')), may hold values from 0.5 to 1.5
- q_gain: bfloat16 [768], P(('shard', 'ctx', 'tp')), may hold values from 0.5 to 1.5
- kv_gain: bfloat16 [256], P(('shard', 'ctx', 'tp')), may hold values from 0.5 to 1.5
- ffn_gain: bfloat16 [2560], P(('shard', 'ctx', 'tp')), may hold values from 0.5 to 1.5
- q_down: bfloat16 [2560, 768], P(('shard', 'ctx', 'tp')), may hold values from -0.125 to 0.125
- kv_down: bfloat16 [2560, 288], P(('shard', 'ctx', 'tp')), may hold values from -0.125 to 0.125
- q_up: bfloat16 [768, 3840], P(('shard', 'ctx'), 'tp'), may hold values from -0.4375 to 0.4375
- kv_up: bfloat16 [256, 5120], P(('shard', 'ctx'), 'tp'), may hold values from -0.375 to 0.375
- out_proj: bfloat16 [2560, 2560], P('tp', ('shard', 'ctx')), may hold values from -3 to 3
- gate_proj: bfloat16 [2560, 6400], P(('shard', 'ctx'), 'tp'), may hold values from -0.125 to 0.125
- up_proj: bfloat16 [2560, 6400], P(('shard', 'ctx'), 'tp'), may hold values from -0.125 to 0.125
- down_proj: bfloat16 [6400, 2560], P('tp', ('shard', 'ctx')), may hold values from -0.75 to 0.75
Outputs:
- output: float32 [4, 1024, 2560], P('shard', 'ctx')
- grad_input: float32 [4, 1024, 2560], P('shard', 'ctx')
- grad_attn_gain: float32 [2560], P(('shard', 'ctx', 'tp'))
- grad_q_gain: float32 [768], P(('shard', 'ctx', 'tp'))
- grad_kv_gain: float32 [256], P(('shard', 'ctx', 'tp'))
- grad_ffn_gain: float32 [2560], P(('shard', 'ctx', 'tp'))
- grad_q_down: float32 [2560, 768], P(('shard', 'ctx', 'tp'))
- grad_kv_down: float32 [2560, 288], P(('shard', 'ctx', 'tp'))
- grad_q_up: float32 [768, 3840], P(('shard', 'ctx'), 'tp')
- grad_kv_up: float32 [256, 5120], P(('shard', 'ctx'), 'tp')
- grad_out_proj: float32 [2560, 2560], P('tp', ('shard', 'ctx'))
- grad_gate_proj: float32 [2560, 6400], P(('shard', 'ctx'), 'tp')
- grad_up_proj: float32 [2560, 6400], P(('shard', 'ctx'), 'tp')
- grad_down_proj: float32 [6400, 2560], P('tp', ('shard', 'ctx'))
Inputs may be any that keep to these rules, and one draw needn't show every extreme that they name: `doc_lengths`: in every sequence the 4 lengths are positive and sum to 1024; exactly one of them, at a place drawn for each sequence, is 896.
All inputs are finite; a program needn't handle non-finite values.
Results may differ from a plain program's by a relative error of at most 0.02.
Values may be sent and summed in bfloat16 or wider, within the bound.
No kernel may reach another device: no remote copies, remote signals or barrier semaphores. Data moves between devices by JAX's collectives and lax.ppermute only.
A program may use at most 320 MiB of HBM per device.

v0:
```python
import math

import jax
import jax.numpy as jnp
from jax import lax
from jax.sharding import PartitionSpec as P

NOPE = 64
ROPE = 32
VDIM = 64
KVRANK = 256


eps = 1e-05
res_scale = 1.4 / math.sqrt(62.0)
big_negative = -1e30
highest = lax.Precision.HIGHEST


def rope_tables(positions):
    half = ROPE // 2
    inverse = jnp.exp(-math.log(10000.0) * jnp.arange(half, dtype=jnp.float32) * 2.0 / ROPE)
    angles = positions.astype(jnp.float32)[:, None] * inverse[None, :]
    angles = jnp.concatenate([angles, angles], axis=-1)
    return (jnp.cos(angles), jnp.sin(angles))


def rotate_half(values):
    half = values.shape[-1] // 2
    return jnp.concatenate([-values[..., half:], values[..., :half]], axis=-1)


def rotate(values, cosine, sine):
    return values * cosine + rotate_half(values) * sine


def unrotate(grads, cosine, sine):
    return grads * cosine - rotate_half(grads) * sine


def norm_forward(values, gain):
    inverse_rms = lax.rsqrt(jnp.mean(values * values, axis=-1, keepdims=True) + eps)
    normed = values * inverse_rms
    return (normed, inverse_rms, normed * gain)


def norm_backward(grad_out, normed, inverse_rms, gain):
    scaled = grad_out * gain
    grad_values = inverse_rms * (
        scaled - normed * jnp.mean(scaled * normed, axis=-1, keepdims=True)
    )
    return (grad_values, jnp.sum(grad_out * normed, axis=0))


def head_total(partial_sum):
    return lax.psum(partial_sum, "tp")


def on_device(
    hidden_in,
    cotangent,
    doc_lengths,
    attn_gain,
    q_gain,
    kv_gain,
    ffn_gain,
    q_down,
    kv_down,
    q_up,
    kv_up,
    out_proj,
    gate_proj,
    up_proj,
    down_proj,
):
    f32 = jnp.float32
    bf16 = jnp.bfloat16
    seqs_here, piece_len, width = hidden_in.shape
    rows = seqs_here * piece_len
    seq_len = piece_len * lax.axis_size("ctx")
    offset = lax.axis_index("ctx") * piece_len
    scale = 1.0 / math.sqrt(NOPE + ROPE)
    small_full = (
        lax.all_gather(attn_gain, ("shard", "ctx", "tp"), axis=0, tiled=True),
        lax.all_gather(ffn_gain, ("shard", "ctx", "tp"), axis=0, tiled=True),
        lax.all_gather(q_gain, ("shard", "ctx", "tp"), axis=0, tiled=True),
        lax.all_gather(kv_gain, ("shard", "ctx", "tp"), axis=0, tiled=True),
        lax.all_gather(q_down, ("shard", "ctx", "tp"), axis=0, tiled=True),
        lax.all_gather(kv_down, ("shard", "ctx", "tp"), axis=0, tiled=True),
    )
    gain_attn = small_full[0].astype(f32)
    gain_ffn = small_full[1].astype(f32)
    gain_query = small_full[2].astype(f32)
    gain_latent = small_full[3].astype(f32)
    down_query = small_full[4]
    down_latent = small_full[5]
    up_query, up_latent, gate_full, upward_full = (
        lax.all_gather(q_up, ("shard", "ctx"), axis=0, tiled=True),
        lax.all_gather(kv_up, ("shard", "ctx"), axis=0, tiled=True),
        lax.all_gather(gate_proj, ("shard", "ctx"), axis=0, tiled=True),
        lax.all_gather(up_proj, ("shard", "ctx"), axis=0, tiled=True),
    )
    out_full, down_full = (
        lax.all_gather(out_proj, ("shard", "ctx"), axis=1, tiled=True),
        lax.all_gather(down_proj, ("shard", "ctx"), axis=1, tiled=True),
    )
    heads_here = up_query.shape[1] // (NOPE + ROPE)
    positions_all = jnp.arange(seq_len, dtype=jnp.int32)
    positions_here = offset + jnp.arange(piece_len, dtype=jnp.int32)
    cosine_all, sine_all = rope_tables(positions_all)
    cosine_here = lax.dynamic_slice_in_dim(cosine_all, offset, piece_len, 0)
    sine_here = lax.dynamic_slice_in_dim(sine_all, offset, piece_len, 0)
    doc_ends = jnp.cumsum(doc_lengths, axis=-1)
    segment_all = jnp.sum(
        (positions_all[None, :, None] >= doc_ends[:, None, :]).astype(jnp.int32), axis=-1
    )
    segment_here = lax.dynamic_slice_in_dim(segment_all, offset, piece_len, 1)
    causal = positions_here[:, None] >= positions_all[None, :]
    allowed = (causal[None] & (segment_here[:, :, None] == segment_all[:, None, :]))[:, None]
    stream = hidden_in.astype(f32).reshape(rows, width)
    normed_one, inverse_one, pre_one = norm_forward(stream, gain_attn)
    input_low = pre_one.astype(bf16)
    query_latent = jnp.dot(input_low, down_query, preferred_element_type=f32)
    normed_query, inverse_query, pre_query = norm_forward(query_latent, gain_query)
    query_low = pre_query.astype(bf16)
    latent_raw = jnp.dot(input_low, down_latent, preferred_element_type=f32)
    normed_latent, inverse_latent, pre_latent = norm_forward(latent_raw[:, :KVRANK], gain_latent)
    latent_low = pre_latent.astype(bf16).reshape(seqs_here, piece_len, KVRANK)
    rotary_key = rotate(
        latent_raw[:, KVRANK:].reshape(seqs_here, piece_len, ROPE), cosine_here, sine_here
    ).astype(bf16)
    latent_all, rotary_all = (
        lax.all_gather(latent_low, "ctx", axis=1, tiled=True),
        lax.all_gather(rotary_key, "ctx", axis=1, tiled=True),
    )
    key_value = jnp.einsum("slr,rf->slf", latent_all, up_latent, preferred_element_type=f32)
    key_value = key_value.reshape(seqs_here, seq_len, heads_here, NOPE + VDIM)
    key_nope = key_value[..., :NOPE].astype(bf16)
    value_low = key_value[..., NOPE:].astype(bf16)
    query = jnp.dot(query_low, up_query, preferred_element_type=f32).reshape(
        seqs_here, piece_len, heads_here, NOPE + ROPE
    )
    query_nope = query[..., :NOPE].astype(bf16)
    query_rope = rotate(query[..., NOPE:], cosine_here[:, None, :], sine_here[:, None, :]).astype(
        bf16
    )

    def masked_scores():
        raw = jnp.einsum("sqhd,skhd->shqk", query_nope, key_nope, preferred_element_type=f32)
        raw = raw + jnp.einsum("sqhd,skd->shqk", query_rope, rotary_all, preferred_element_type=f32)
        return jnp.where(allowed, raw * scale, big_negative)

    scores = masked_scores()
    row_max = jnp.max(scores, axis=-1, keepdims=True)
    weights = jnp.exp(scores - row_max)
    row_total = jnp.sum(weights, axis=-1, keepdims=True)
    log_total = row_max + jnp.log(row_total)
    prob_low = (weights / row_total).astype(bf16)
    attended = jnp.einsum("shqk,skhd->sqhd", prob_low, value_low, preferred_element_type=f32)
    attended_low = attended.reshape(rows, heads_here * VDIM).astype(bf16)
    attn_out = head_total(jnp.dot(attended_low, out_full, preferred_element_type=f32))
    middle = stream + res_scale * attn_out
    normed_two, inverse_two, pre_two = norm_forward(middle, gain_ffn)
    ffn_low = pre_two.astype(bf16)
    gate_value = jnp.dot(ffn_low, gate_full, preferred_element_type=f32)
    up_value = jnp.dot(ffn_low, upward_full, preferred_element_type=f32)
    gate_act = jax.nn.silu(gate_value)
    hidden_low = (gate_act * up_value).astype(bf16)
    ffn_out = head_total(jnp.dot(hidden_low, down_full, preferred_element_type=f32))
    output = middle + res_scale * ffn_out
    grad_out = cotangent.astype(f32).reshape(rows, width)
    grad_ffn = (res_scale * grad_out).astype(bf16)
    grad_down_w = jnp.einsum("rf,rd->fd", hidden_low, grad_ffn, preferred_element_type=f32)
    grad_hidden = jnp.einsum("rd,fd->rf", grad_ffn, down_full, preferred_element_type=f32)
    sigma = jax.nn.sigmoid(gate_value)
    grad_gate = (grad_hidden * up_value * sigma * (1.0 + gate_value * (1.0 - sigma))).astype(bf16)
    grad_upward = (grad_hidden * gate_act).astype(bf16)
    grad_gate_w = jnp.einsum("rd,rf->df", ffn_low, grad_gate, preferred_element_type=f32)
    grad_upward_w = jnp.einsum("rd,rf->df", ffn_low, grad_upward, preferred_element_type=f32)
    grad_pre_two = jnp.einsum("rf,df->rd", grad_gate, gate_full, preferred_element_type=f32)
    grad_pre_two = grad_pre_two + jnp.einsum(
        "rf,df->rd", grad_upward, upward_full, preferred_element_type=f32
    )
    grad_middle_part, grad_gain_ffn = norm_backward(grad_pre_two, normed_two, inverse_two, gain_ffn)
    grad_middle = grad_out + head_total(grad_middle_part)
    grad_attn = (res_scale * grad_middle).astype(bf16)
    grad_out_w = jnp.einsum("ro,rd->od", attended_low, grad_attn, preferred_element_type=f32)
    grad_attended = jnp.einsum("rd,od->ro", grad_attn, out_full, preferred_element_type=f32)
    grad_attended = grad_attended.astype(bf16).reshape(seqs_here, piece_len, heads_here, VDIM)
    grad_value = jnp.einsum("shqk,sqhd->skhd", prob_low, grad_attended, preferred_element_type=f32)
    grad_prob = jnp.einsum("sqhd,skhd->shqk", grad_attended, value_low, preferred_element_type=f32)
    prob_again = jnp.exp(masked_scores() - log_total)
    grad_scores = prob_again * (grad_prob - jnp.sum(prob_again * grad_prob, axis=-1, keepdims=True))
    grad_scores = grad_scores.astype(bf16)
    grad_qnope = (
        jnp.einsum("shqk,skhd->sqhd", grad_scores, key_nope, preferred_element_type=f32) * scale
    )
    grad_qrope = (
        jnp.einsum("shqk,skd->sqhd", grad_scores, rotary_all, preferred_element_type=f32) * scale
    )
    grad_qrope = unrotate(grad_qrope, cosine_here[:, None, :], sine_here[:, None, :])
    grad_knope = (
        jnp.einsum("shqk,sqhd->skhd", grad_scores, query_nope, preferred_element_type=f32) * scale
    )
    grad_krope = (
        jnp.einsum("shqk,sqhd->skd", grad_scores, query_rope, preferred_element_type=f32) * scale
    )
    grad_query = (
        jnp.concatenate([grad_qnope, grad_qrope], axis=-1)
        .reshape(rows, heads_here * (NOPE + ROPE))
        .astype(bf16)
    )
    grad_up_query = jnp.einsum("rq,rf->qf", query_low, grad_query, preferred_element_type=f32)
    grad_pre_query = jnp.einsum("rf,qf->rq", grad_query, up_query, preferred_element_type=f32)
    grad_key_value = jnp.concatenate([grad_knope, grad_value], axis=-1).reshape(
        seqs_here, seq_len, heads_here * (NOPE + VDIM)
    )
    grad_up_latent = jnp.einsum(
        "slr,slf->rf", latent_all.astype(f32), grad_key_value, precision=highest
    )
    grad_latent_all = jnp.einsum(
        "slf,rf->slr", grad_key_value, up_latent.astype(f32), precision=highest
    )
    grad_latent, grad_rotary = (
        lax.psum_scatter(
            grad_latent_all.astype(jnp.bfloat16), "ctx", scatter_dimension=1, tiled=True
        ).astype(jnp.float32),
        lax.psum_scatter(
            grad_krope.astype(jnp.bfloat16), "ctx", scatter_dimension=1, tiled=True
        ).astype(jnp.float32),
    )
    grad_query_latent, grad_gain_query = norm_backward(
        grad_pre_query, normed_query, inverse_query, gain_query
    )
    grad_compressed, grad_gain_latent = norm_backward(
        grad_latent.reshape(rows, KVRANK), normed_latent, inverse_latent, gain_latent
    )
    grad_rotary_raw = unrotate(grad_rotary, cosine_here, sine_here).reshape(rows, ROPE)
    grad_latent_raw = jnp.concatenate([grad_compressed, grad_rotary_raw], axis=-1)
    input_wide = input_low.astype(f32)
    grad_pre_one = jnp.einsum(
        "rq,dq->rd", grad_query_latent, down_query.astype(f32), precision=highest
    )
    grad_pre_one = grad_pre_one + jnp.einsum(
        "rq,dq->rd", grad_latent_raw, down_latent.astype(f32), precision=highest
    )
    grad_stream_part, grad_gain_attn = norm_backward(
        grad_pre_one, normed_one, inverse_one, gain_attn
    )
    grad_down_query = jnp.einsum("rd,rq->dq", input_wide, grad_query_latent, precision=highest)
    grad_down_latent = jnp.einsum("rd,rq->dq", input_wide, grad_latent_raw, precision=highest)
    grad_input = grad_middle + head_total(grad_stream_part)
    small_grads = (
        lax.psum_scatter(grad_gain_attn, ("shard", "ctx", "tp"), scatter_dimension=0, tiled=True),
        lax.psum_scatter(grad_gain_ffn, ("shard", "ctx", "tp"), scatter_dimension=0, tiled=True),
        lax.psum_scatter(grad_gain_query, ("shard", "ctx", "tp"), scatter_dimension=0, tiled=True),
        lax.psum_scatter(grad_gain_latent, ("shard", "ctx", "tp"), scatter_dimension=0, tiled=True),
        lax.psum_scatter(grad_down_query, ("shard", "ctx", "tp"), scatter_dimension=0, tiled=True),
        lax.psum_scatter(grad_down_latent, ("shard", "ctx", "tp"), scatter_dimension=0, tiled=True),
    )
    inner_grads = (
        lax.psum_scatter(
            grad_up_query.astype(jnp.bfloat16), ("shard", "ctx"), scatter_dimension=0, tiled=True
        ).astype(jnp.float32),
        lax.psum_scatter(
            grad_up_latent.astype(jnp.bfloat16), ("shard", "ctx"), scatter_dimension=0, tiled=True
        ).astype(jnp.float32),
        lax.psum_scatter(
            grad_gate_w.astype(jnp.bfloat16), ("shard", "ctx"), scatter_dimension=0, tiled=True
        ).astype(jnp.float32),
        lax.psum_scatter(
            grad_upward_w.astype(jnp.bfloat16), ("shard", "ctx"), scatter_dimension=0, tiled=True
        ).astype(jnp.float32),
    )
    outer_grads = (
        lax.psum_scatter(
            grad_out_w.astype(jnp.bfloat16), ("shard", "ctx"), scatter_dimension=1, tiled=True
        ).astype(jnp.float32),
        lax.psum_scatter(
            grad_down_w.astype(jnp.bfloat16), ("shard", "ctx"), scatter_dimension=1, tiled=True
        ).astype(jnp.float32),
    )
    return (
        output.reshape(seqs_here, piece_len, width),
        grad_input.reshape(seqs_here, piece_len, width),
        small_grads[0],
        small_grads[2],
        small_grads[3],
        small_grads[1],
        small_grads[4],
        small_grads[5],
        inner_grads[0],
        inner_grads[1],
        outer_grads[0],
        inner_grads[2],
        inner_grads[3],
        outer_grads[1],
    )


def solution(mesh):
    placed = (
        P("shard", "ctx", None),
        P("shard", "ctx", None),
        P("shard", None),
        P(("shard", "ctx", "tp")),
        P(("shard", "ctx", "tp")),
        P(("shard", "ctx", "tp")),
        P(("shard", "ctx", "tp")),
        P(("shard", "ctx", "tp"), None),
        P(("shard", "ctx", "tp"), None),
        P(("shard", "ctx"), "tp"),
        P(("shard", "ctx"), "tp"),
        P("tp", ("shard", "ctx")),
        P(("shard", "ctx"), "tp"),
        P(("shard", "ctx"), "tp"),
        P("tp", ("shard", "ctx")),
    )
    return jax.shard_map(
        on_device,
        mesh=mesh,
        in_specs=placed,
        out_specs=(
            P("shard", "ctx", None),
            P("shard", "ctx", None),
            P(("shard", "ctx", "tp")),
            P(("shard", "ctx", "tp")),
            P(("shard", "ctx", "tp")),
            P(("shard", "ctx", "tp")),
            P(("shard", "ctx", "tp"), None),
            P(("shard", "ctx", "tp"), None),
            P(("shard", "ctx"), "tp"),
            P(("shard", "ctx"), "tp"),
            P("tp", ("shard", "ctx")),
            P(("shard", "ctx"), "tp"),
            P(("shard", "ctx"), "tp"),
            P("tp", ("shard", "ctx")),
        ),
        check_vma=False,
    )
```

profile of v0, /device:TPU:0, one launch (start us, length us, event | category | flops | bytes accessed | tf_op | source)
XLA Modules:
  0.0 2134.8 jit_solution(11234434157566794903)
XLA Ops:
  13.7 42.3 %all-reduce.10 = (bf16[2560]{0:T(1024)(128)(2,1)S(1)}, bf16[768]{0:T(1024)(128)(2,1)}, bf16[256]{0:T(256)(128)(2,1)S(1)}, bf16[2560]{0:T(1024)(128)(2,1)}) all-reduce(bf16[2560]{0:T(1024)(128)(2,1)S(1)} %dynamic-update-slice, bf16[768]{0:T(1024)(128)(2,1)S(1)} %dynamic-update-slice.2, ...), channel_id=1, replica_groups=mesh['shard'=2,'ctx'=4,'tp'=4] {'shard','ctx','tp'}, use_global_device_ids=true, to_apply=%add | all-reduce | flops 6144 | bytes 24576
  59.4 10.4 all-gather.9.cloned.1.call-done
  69.7 3.3 fusion.68
  79.5 37.9 %all_gather.46 = bf16[256,1280]{1,0:T(8,128)(2,1)} all-gather(bf16[32,1280]{1,0:T(8,128)(2,1)S(1)} %copy-done.37), channel_id=1, replica_groups=mesh['shard'=2,'ctx'=4,'tp'=4] {'shard','ctx'}, dimensions={0}, use_global_device_ids=true | all-gather | bytes 737280 | tf_op jit(solution)/shard_map/all_gather | solution.py:99
  118.6 14.2 all_gather.50
  132.8 5.3 convolution_convert_fusion.3
  138.1 8.1 copy.88
  146.2 29.7 %all-gather.13.cloned.1.call-done = bf16[2560,768]{1,0:T(8,128)(2,1)} async-done(((bf16[80,768]{1,0:T(8,128)(2,1)}), bf16[2560,768]{1,0:T(8,128)(2,1)}) %all-gather.13.cloned.1.call-update) | async-done | bytes 3932176 | tf_op jit(solution)/shard_map/all_gather | solution.py:88
  175.9 6.3 multiply_reduce_fusion.6
  182.2 38.6 %all-gather.15.cloned.1.call-done = bf16[768,960]{1,0:T(8,128)(2,1)} async-done(((bf16[96,960]{1,0:T(8,128)(2,1)}), bf16[768,960]{1,0:T(8,128)(2,1)}) %all-gather.15.cloned.1.call-update) | async-done | bytes 1474576 | tf_op jit(solution)/shard_map/all_gather | solution.py:98
  220.8 4.2 fusion.62
  225.0 3.4 reshape.192
  228.4 2.8 slice.63
  232.9 8.7 fusion.51
  241.6 14.9 fusion.67
  256.5 10.0 fusion.2
  266.5 3.1 copy-done
  269.6 4.1 divide_convert_fusion
  273.7 7.8 fusion.36
  284.3 6.7 fusion.69
  293.4 3.7 fusion.3
  297.1 95.5 %all-reduce.15.cloned.1.call-done = f32[512,2560]{1,0:T(8,128)} async-done(((f32[512,2560]{1,0:T(8,128)}), f32[512,2560]{1,0:T(8,128)}) %all-reduce.15.cloned.1.call-update) | async-done | bytes 5242896 | tf_op jit(solution)/shard_map/psum | solution.py:56
  392.6 3.4 multiply_reduce_fusion.3
  398.9 122.7 %all-gather.21.cloned.1.call-done = bf16[2560,1600]{1,0:T(8,128)(2,1)} async-done(((bf16[320,1600]{1,0:T(8,128)(2,1)}), bf16[2560,1600]{1,0:T(8,128)(2,1)}) %all-gather.21.cloned.1.call-update) | async-done | bytes 8192016 | tf_op jit(solution)/shard_map/all_gather | solution.py:101
  521.5 8.7 fusion.71
  530.3 118.2 %all-gather.19.cloned.1.call-done = bf16[2560,1600]{1,0:T(8,128)(2,1)} async-done(((bf16[320,1600]{1,0:T(8,128)(2,1)}), bf16[2560,1600]{1,0:T(8,128)(2,1)}) %all-gather.19.cloned.1.call-update) | async-done | bytes 8192016 | tf_op jit(solution)/shard_map/all_gather | solution.py:100
  648.5 8.6 fusion.70
  657.1 118.4 %all-gather.23.cloned.1.call-done = bf16[1600,2560]{0,1:T(8,128)(2,1)} async-done(((bf16[1600,320]{0,1:T(8,128)(2,1)}), bf16[1600,2560]{0,1:T(8,128)(2,1)}) %all-gather.23.cloned.1.call-update) | async-done | bytes 8192016 | tf_op jit(solution)/shard_map/all_gather | solution.py:105
  775.5 13.7 multiply_convert_fusion.3
  789.1 11.2 fusion.73
  800.3 12.1 multiply_reduce_fusion.1
  812.4 3.5 subtract_multiply_fusion
  816.5 100.4 %all-reduce.17.cloned.1.call-done = f32[512,2560]{1,0:T(8,128)} async-done(((f32[512,2560]{1,0:T(8,128)}), f32[512,2560]{1,0:T(8,128)}) %all-reduce.17.cloned.1.call-update) | async-done | bytes 5242896 | tf_op jit(solution)/shard_map/psum | solution.py:56
  916.9 3.5 multiply_convert_fusion.1
  924.4 8.2 convolution_bitcast_fusion.1
  932.6 14.4 multiply_reduce_fusion
  947.0 14.1 multiply_convert_fusion
  961.2 4.0 copy-done.1
  967.8 8.3 multiply_bitcast_fusion
  976.3 10.1 pad_maximum_fusion
  986.4 13.4 convolution_convert_fusion.6
  1000.1 7.3 broadcast_multiply_fusion
  1007.5 6.6 fusion.16
  1014.8 8.1 fusion.33
  1026.8 5.7 convolution_convert_fusion.4
  1032.6 11.4 fusion.72
  1046.6 8.9 fusion.64
  1064.4 9.8 fusion.12
  1074.3 3.6 fusion.11
  1079.6 8.7 convolution_convert_fusion
  1090.1 8.9 convolution_convert_fusion.1
  1099.1 8.6 convolution_convert_fusion.2
  1109.5 7.0 fusion.49
  1116.6 11.5 fusion.63
  1129.8 40.2 %all-reduce.8 = (f32[2560]{0:T(1024)S(1)}, f32[768]{0:T(1024)S(1)}, f32[256]{0:T(256)S(1)}, f32[2560]{0:T(1024)S(1)}) all-reduce(f32[2560]{0:T(1024)S(1)} %get-tuple-element.16, f32[768]{0:T(1024)S(1)} %get-tuple-element.18, f32[256]{0:T(256)S(1)} %get-tuple-element.20, ...), channel_id=4, replica_groups=mesh['shard'=2,'ctx'=4,'tp'=4] {'shard','ctx','tp'}, use_global_device_ids=true, to_apply=%region_20.21.clone | all-reduce | flops 6144 | bytes 49152
  1174.1 64.1 %reduce-scatter.23.cloned.1.call-done = bf16[640,320]{0,1:T(8,128)(2,1)} async-done(((bf16[640,2560]{0,1:T(8,128)(2,1)}), bf16[640,320]{0,1:T(8,128)(2,1)}) %reduce-scatter.23.cloned.1.call-update) | async-done | bytes 409616 | tf_op jit(solution)/shard_map/reduce_scatter | solution.py:276
  1240.2 187.4 %all-reduce.19.cloned.1.call-done = (f32[512,2560]{1,0:T(8,128)}, f32[512,2560]{1,0:T(8,128)}) async-done(((f32[512,2560]{1,0:T(8,128)}, f32[512,2560]{1,0:T(8,128)}), (f32[512,2560]{1,0:T(8,128)}, f32[512,2560]{1,0:T(8,128)})) %all-reduce.19.cloned.1.call-update) | async-done | bytes 10485776 | tf_op jit(solution)/shard_map/psum | solution.py:56
  1427.6 7.9 multiply_add_fusion
  1437.0 3.8 fusion.14
  1440.8 142.2 %reduce-scatter.29.cloned.1.call-done = bf16[1600,320]{0,1:T(8,128)(2,1)} async-done(((bf16[1600,2560]{0,1:T(8,128)(2,1)}), bf16[1600,320]{0,1:T(8,128)(2,1)}) %reduce-scatter.29.cloned.1.call-update) | async-done | bytes 1024016 | tf_op jit(solution)/shard_map/reduce_scatter | solution.py:279
  1585.6 151.1 %reduce-scatter.27.cloned.1.call-done = bf16[320,1600]{1,0:T(8,128)(2,1)} async-done(((bf16[2560,1600]{1,0:T(8,128)(2,1)}), bf16[320,1600]{1,0:T(8,128)(2,1)}) %reduce-scatter.27.cloned.1.call-update) | async-done | bytes 1024016 | tf_op jit(solution)/shard_map/reduce_scatter | solution.py:271
  1739.5 151.6 %reduce-scatter.25.cloned.1.call-done = bf16[320,1600]{1,0:T(8,128)(2,1)} async-done(((bf16[2560,1600]{1,0:T(8,128)(2,1)}), bf16[320,1600]{1,0:T(8,128)(2,1)}) %reduce-scatter.25.cloned.1.call-update) | async-done | bytes 1024016 | tf_op jit(solution)/shard_map/reduce_scatter | solution.py:268
  1893.8 106.1 %reduce-scatter.17.cloned.1.call-done = f32[80,288]{1,0:T(8,128)} async-done(((f32[2560,288]{1,0:T(8,128)}), f32[80,288]{1,0:T(8,128)}) %reduce-scatter.17.cloned.1.call-update) | async-done | bytes 92176 | tf_op jit(solution)/shard_map/reduce_scatter | solution.py:259
  1999.9 127.6 %reduce-scatter.15.cloned.1.call-done = f32[80,768]{1,0:T(8,128)} async-done(((f32[2560,768]{1,0:T(8,128)}), f32[80,768]{1,0:T(8,128)}) %reduce-scatter.15.cloned.1.call-update) | async-done | bytes 245776 | tf_op jit(solution)/shard_map/reduce_scatter | solution.py:258
  (242 shorter events, 73.1 us)
Async XLA Ops:
  7.2 50.0 %copy-start.5 = (bf16[2,256,2560]{2,1,0:T(8,128)(2,1)S(1)}, bf16[2,256,2560]{2,1,0:T(8,128)(2,1)}, u32[]{:S(2)}) copy-start(bf16[2,256,2560]{2,1,0:T(8,128)(2,1)} %param.15) | copy-start | bytes 7864324
  7.2 62.5 %all-gather.9.cloned.1.call-start = ((), (), s32[]{:S(2)}) async-start(), calls=%async_computation.10 | async-start | bytes 2027520 | tf_op jit(solution)/shard_map/all_gather | solution.py:89
  7.9 124.9 %all-gather.11.cloned.1.call-start = ((), (), s32[]{:S(2)}) async-start(), calls=%async_computation.11 | async-start | bytes 1310720 | tf_op jit(solution)/shard_map/all_gather | solution.py:133
  10.3 49.1 %copy-start.40 = (f32[1,2,2,128]{3,1,2,0:T(2,128)}, f32[1,2,2,128]{3,1,2,0:T(2,128)S(1)}, u32[]{:S(2)}) copy-start(f32[1,2,2,128]{3,1,2,0:T(2,128)S(1)} %copy.121) | copy-start | bytes 6148
  59.4 20.1 copy-start.37
  69.7 4.1 copy-start.47
  73.1 65.0 %copy-start.11 = (f32[512,288]{0,1:T(8,128)}, f32[512,288]{0,1:T(8,128)S(1)}, u32[]{:S(2)}) copy-start(f32[512,288]{0,1:T(8,128)S(1)} %fusion.68) | copy-start | bytes 1769476
  74.8 101.1 %all-gather.13.cloned.1.call-start = ((), (), s32[]{:S(2)}) async-start(), calls=%async_computation.12 | async-start | bytes 4055040 | tf_op jit(solution)/shard_map/all_gather | solution.py:88
  75.6 145.2 %all-gather.15.cloned.1.call-start = ((), (), s32[]{:S(2)}) async-start(), calls=%async_computation.13 | async-start | bytes 1769472 | tf_op jit(solution)/shard_map/all_gather | solution.py:98
  76.1 208.2 %all-gather.17.cloned.1.call-start = ((), (), s32[]{:S(2)}) async-start(), calls=%async_computation.14 | async-start | bytes 3686400 | tf_op jit(solution)/shard_map/all_gather | solution.py:104
  76.7 315.9 %all-reduce.15.cloned.1.call-start = ((), (), s32[]{:S(2)}) async-start(), calls=%async_computation.15 | async-start | bytes 10485760 | tf_op jit(solution)/shard_map/psum | solution.py:56
  78.3 142.5 %copy-start.38 = (f32[768]{0:T(1024)}, f32[768]{0:T(1024)S(1)}, u32[]{:S(2)}) copy-start(f32[768]{0:T(1024)S(1)} %convert_element_type.143) | copy-start | bytes 9220
  79.2 153.5 %copy-start.29 = (f32[256,32]{0,1:T(8,128)}, f32[256,32]{0,1:T(8,128)S(1)}, u32[]{:S(2)}) copy-start(f32[256,32]{0,1:T(8,128)S(1)} %get-tuple-element.45) | copy-start | bytes 98308
  79.2 153.5 %copy-start.32 = (f32[256,32]{0,1:T(8,128)}, f32[256,32]{0,1:T(8,128)S(1)}, u32[]{:S(2)}) copy-start(f32[256,32]{0,1:T(8,128)S(1)} %get-tuple-element.33) | copy-start | bytes 98308
  182.2 46.2 %copy-start.44 = (f32[512]{0:T(512)}, f32[512]{0:T(512)S(1)}, u32[]{:S(2)}) copy-start(f32[512]{0:T(512)S(1)} %add_rsqrt_fusion.1) | copy-start | bytes 6148
  228.4 4.3 slice-start.4
  228.4 4.4 copy-start.27
  232.9 8.7 copy-start.23
  256.5 13.1 copy-start
  273.7 7.9 copy-start.2
  291.1 230.4 %all-gather.21.cloned.1.call-start = ((), (), s32[]{:S(2)}) async-start(), calls=%async_computation.17 | async-start | bytes 9584640 | tf_op jit(solution)/shard_map/all_gather | solution.py:101
  291.8 356.6 %all-gather.19.cloned.1.call-start = ((), (), s32[]{:S(2)}) async-start(), calls=%async_computation.16 | async-start | bytes 9584640 | tf_op jit(solution)/shard_map/all_gather | solution.py:100
  292.6 482.9 %all-gather.23.cloned.1.call-start = ((), (), s32[]{:S(2)}) async-start(), calls=%async_computation.18 | async-start | bytes 9584640 | tf_op jit(solution)/shard_map/all_gather | solution.py:105
  293.3 623.5 %all-reduce.17.cloned.1.call-start = ((), (), s32[]{:S(2)}) async-start(), calls=%async_computation.19 | async-start | bytes 10485760 | tf_op jit(solution)/shard_map/psum | solution.py:56
  398.9 249.6 %copy-start.19 = (bf16[512,2560]{1,0:T(8,128)(2,1)}, bf16[512,2560]{1,0:T(8,128)(2,1)S(1)}, u32[]{:S(2)}) copy-start(bf16[512,2560]{1,0:T(8,128)(2,1)S(1)} %multiply_convert_fusion.2) | copy-start | bytes 7864324
  775.5 24.9 %slice-start = ((s8[5242880]{0:T(1024)(128)(4,1)}), s8[1048576]{0:T(1024)(128)(4,1)S(1)}, s32[]{:S(2)}) async-start(s8[5242880]{0:T(1024)(128)(4,1)} %bitcast.152), calls=%async_computation.31 | async-start | bytes 2097152
  789.1 11.2 copy-start.52
  789.1 11.2 slice-start.1
  816.0 100.9 %copy-start.8 = (bf16[2,256,2560]{2,1,0:T(8,128)(2,1)S(1)}, bf16[2,256,2560]{2,1,0:T(8,128)(2,1)}, u32[]{:S(2)}) copy-start(bf16[2,256,2560]{2,1,0:T(8,128)(2,1)} %param.16) | copy-start | bytes 7864324
  816.0 239.5 %reduce-scatter.13.cloned.1.call-start = ((), (), s32[]{:S(2)}) async-start(), calls=%async_computation.21 | async-start | bytes 163840 | tf_op jit(solution)/shard_map/reduce_scatter | solution.py:228
  916.8 4.9 copy-start.51
  961.2 4.0 copy-start.1
  965.2 2.6 copy-start.10
  976.1 10.4 copy-start.14
  976.1 81.9 %reduce-scatter.11.cloned.1.call-start = ((), (), s32[]{:S(2)}) async-start(), calls=%async_computation.20 | async-start | bytes 1310720 | tf_op jit(solution)/shard_map/reduce_scatter | solution.py:225
  986.4 13.7 copy-start.28
  999.8 7.7 copy-start.18
  999.8 128.3 %reduce-scatter.21.cloned.1.call-start = ((), (), s32[]{:S(2)}) async-start(), calls=%async_computation.25 | async-start | bytes 737280 | tf_op jit(solution)/shard_map/reduce_scatter | solution.py:265
  1000.1 7.4 copy-start.3
  1007.5 7.2 copy-start.30
  1007.5 7.1 copy-start.36
  1014.2 158.2 %reduce-scatter.19.cloned.1.call-start = ((), (), s32[]{:S(2)}) async-start(), calls=%async_computation.24 | async-start | bytes 1769472 | tf_op jit(solution)/shard_map/reduce_scatter | solution.py:262
  1024.1 2.7 copy-start.31
  1026.8 211.4 %reduce-scatter.23.cloned.1.call-start = ((), (), s32[]{:S(2)}) async-start(), calls=%async_computation.26 | async-start | bytes 3686400 | tf_op jit(solution)/shard_map/reduce_scatter | solution.py:276
  1032.6 395.0 %all-reduce.19.cloned.1.call-start = ((), (), s32[]{:S(2)}) async-start(), calls=%async_computation.30 | async-start | bytes 20971520 | tf_op jit(solution)/shard_map/psum | solution.py:56
  1032.6 11.4 copy-start.25
  1046.5 10.6 copy-start.33
  1046.5 15.3 copy-start.12
  1046.5 15.3 copy-start.43
  1046.5 15.3 copy-start.48
  1055.5 8.9 copy-start.6
  1055.5 8.9 copy-start.35
  1055.5 8.9 copy-start.41
  1061.8 2.6 copy-start.24
  1064.4 9.9 copy-start.16
  1077.9 505.0 %reduce-scatter.29.cloned.1.call-start = ((), (), s32[]{:S(2)}) async-start(), calls=%async_computation.29 | async-start | bytes 9584640 | tf_op jit(solution)/shard_map/reduce_scatter | solution.py:279
  1088.4 648.4 %reduce-scatter.27.cloned.1.call-start = ((), (), s32[]{:S(2)}) async-start(), calls=%async_computation.28 | async-start | bytes 9584640 | tf_op jit(solution)/shard_map/reduce_scatter | solution.py:271
  1099.0 792.1 %reduce-scatter.25.cloned.1.call-start = ((), (), s32[]{:S(2)}) async-start(), calls=%async_computation.27 | async-start | bytes 9584640 | tf_op jit(solution)/shard_map/reduce_scatter | solution.py:268
  1107.7 892.2 %reduce-scatter.17.cloned.1.call-start = ((), (), s32[]{:S(2)}) async-start(), calls=%async_computation.23 | async-start | bytes 4055040 | tf_op jit(solution)/shard_map/reduce_scatter | solution.py:259
  1116.6 1010.9 %reduce-scatter.15.cloned.1.call-start = ((), (), s32[]{:S(2)}) async-start(), calls=%async_computation.22 | async-start | bytes 8110080 | tf_op jit(solution)/shard_map/reduce_scatter | solution.py:258
  1128.1 307.4 %slice-start.2 = ((s8[5242880]{0:T(1024)(128)(4,1)}), s8[1048576]{0:T(1024)(128)(4,1)S(1)}, s32[]{:S(2)}) async-start(s8[5242880]{0:T(1024)(128)(4,1)} %bitcast.158), calls=%async_computation.33 | async-start | bytes 2097152
  1427.6 7.9 copy-start.9
  1427.6 7.9 slice-start.3
  1427.6 9.4 copy-start.15
  (15 other events, 24.1 us)
Sparse Core Ops, SparseCore 0:
  10.9 58.7 all-gather.8
  74.9 36.4 all-gather.10
  114.3 61.6 all-gather.12
  177.9 42.8 all-gather.14
  222.7 60.7 all-gather.16
  291.2 101.3 all-reduce.14
  394.7 126.8 all-gather.20
  523.6 124.8 all-gather.18
  650.6 124.8 all-gather.22
  816.1 100.6 all-reduce.16
  976.2 19.3 reduce-scatter.12
  1000.0 27.2 reduce-scatter.10
  1031.1 60.7 reduce-scatter.20
  1095.6 64.1 reduce-scatter.18
  1163.3 74.9 reduce-scatter.22
  1241.4 186.1 all-reduce.18
  1431.5 151.4 reduce-scatter.28
  1586.4 150.3 reduce-scatter.26
  1740.8 150.2 reduce-scatter.24
  1896.9 102.9 reduce-scatter.16
  2006.1 121.3 reduce-scatter.14
where the time goes:
time: 2140 us; the launch traced here: 2130 us
  waiting for transfers between devices  1570 us (73%)
  matrix products  267 us (12%)
  blocking collectives  135 us (6%)
  other arithmetic  97.1 us (5%)
  local copies, waits for them, and re-layouts  49.8 us (2%)
    psum x3, waiting for transfers between devices, head_total(): return lax.psum(partial_sum, 'tp')  383 us
    reduce_scatter x1, waiting for transfers between devices, on_device(): lax.psum_scatter(grad_gate_w.astype(jnp.bfloat16), ('shard', 'ctx'), scat...  152 us
    reduce_scatter x1, waiting for transfers between devices, on_device(): lax.psum_scatter(grad_upward_w.astype(jnp.bfloat16), ('shard', 'ctx'), sc...  151 us
    reduce_scatter x1, waiting for transfers between devices, on_device(): lax.psum_scatter(grad_down_w.astype(jnp.bfloat16), ('shard', 'ctx'), scat...  142 us
    reduce_scatter x1, waiting for transfers between devices, on_device(): lax.psum_scatter(grad_down_query, ('shard', 'ctx', 'tp'), scatter_dimensi...  128 us
    all_gather x1, waiting for transfers between devices, on_device(): lax.all_gather(up_proj, ('shard', 'ctx'), axis=0, tiled=True)  123 us
    all_gather x1, waiting for transfers between devices, on_device(): lax.all_gather(down_proj, ('shard', 'ctx'), axis=1, tiled=True)  118 us
    all_gather x1, waiting for transfers between devices, on_device(): lax.all_gather(gate_proj, ('shard', 'ctx'), axis=0, tiled=True)  118 us
  transfers between devices with their start and end apart: 21, of which 15 were waited for; matrix products, arithmetic and copies ran while one was open for 14% of the time, Pallas kernels for 0%

commit v1 on v0

v1 whole, which is shorter than its diff:
```python
import math

import jax
import jax.numpy as jnp
from jax import lax
from jax.sharding import PartitionSpec as P

NOPE = 64
ROPE = 32
VDIM = 64
KVRANK = 256
QRANK = 768
PAD = 16

eps = 1e-05
res_scale = 1.4 / math.sqrt(62.0)
big_negative = -1e30
f32 = jnp.float32
bf16 = jnp.bfloat16


def rope_tables(positions):
    half = ROPE // 2
    inverse = jnp.exp(-math.log(10000.0) * jnp.arange(half, dtype=f32) * 2.0 / ROPE)
    angles = positions.astype(f32)[:, None] * inverse[None, :]
    angles = jnp.concatenate([angles, angles], axis=-1)
    return (jnp.cos(angles), jnp.sin(angles))


def rotate_half(values):
    half = values.shape[-1] // 2
    return jnp.concatenate([-values[..., half:], values[..., :half]], axis=-1)


def rotate(values, cosine, sine):
    return values * cosine + rotate_half(values) * sine


def unrotate(grads, cosine, sine):
    return grads * cosine - rotate_half(grads) * sine


def rms_inverse(values):
    return lax.rsqrt(jnp.mean(values * values, axis=-1, keepdims=True) + eps)


def norm_backward(grad_out, normed, inverse_rms, gain):
    scaled = grad_out * gain
    return inverse_rms * (scaled - normed * jnp.mean(scaled * normed, axis=-1, keepdims=True))


def dot(left, right, dims):
    return lax.dot_general(left, right, (dims, ((), ())), preferred_element_type=f32)


def round_low(values):
    return lax.reduce_precision(values, 8, 7)


def tp_xor(values, mask):
    size = lax.axis_size("tp")
    return lax.ppermute(values, "tp", [(i, i ^ mask) for i in range(size)])


def from_ctx(values, shift):
    size = lax.axis_size("ctx")
    return lax.ppermute(values, "ctx", [((i + shift) % size, i) for i in range(size)])


def gather_ctx(values):
    size = lax.axis_size("ctx")
    spread = jnp.broadcast_to(values[None], (size,) + values.shape)
    return lax.all_to_all(spread, "ctx", 0, 0)


def pair_order(own, other, second, axis):
    return jnp.concatenate(
        [jnp.where(second, other, own), jnp.where(second, own, other)], axis=axis
    )


def gather_shard(values, axis):
    if lax.axis_size("shard") == 2:
        other = lax.ppermute(values, "shard", [(0, 1), (1, 0)])
        return pair_order(values, other, lax.axis_index("shard") == 1, axis)
    return lax.all_gather(values, "shard", axis=axis, tiled=True)


def scatter_shard(values, axis):
    size = lax.axis_size("shard")
    if size == 2:
        length = values.shape[axis] // 2
        low = lax.slice_in_dim(values, 0, length, axis=axis)
        high = lax.slice_in_dim(values, length, 2 * length, axis=axis)
        second = lax.axis_index("shard") == 1
        keep = jnp.where(second, high, low)
        send = jnp.where(second, low, high).astype(bf16)
        return keep + lax.ppermute(send, "shard", [(0, 1), (1, 0)]).astype(f32)
    return lax.psum_scatter(
        values.astype(bf16), "shard", scatter_dimension=axis, tiled=True
    ).astype(f32)


def scatter_ctx(values):
    came = lax.all_to_all(values.astype(bf16), "ctx", 0, 0)
    return jnp.sum(came.astype(f32), axis=0)


def gather_tp(chunk):
    rank = lax.axis_index("tp")
    low_bit, high_bit = (rank & 1) == 1, (rank >> 1) == 1
    other = tp_xor(chunk, 2)
    pair = jnp.stack([jnp.where(high_bit, other, chunk), jnp.where(high_bit, chunk, other)])
    across = tp_xor(pair, 1)
    both = jnp.stack(
        [jnp.where(low_bit, across, pair), jnp.where(low_bit, pair, across)], axis=1
    )
    return both.reshape((4,) + chunk.shape)


def scatter_tp(partial_sum):
    rank = lax.axis_index("tp")
    low_bit, high_bit = (rank & 1) == 1, (rank >> 1) == 1
    parts = partial_sum.reshape((2, 2) + partial_sum.shape[1:])
    keep = jnp.where(low_bit, parts[:, 1], parts[:, 0])
    send = jnp.where(low_bit, parts[:, 0], parts[:, 1]).astype(bf16)
    summed = keep + tp_xor(send, 1).astype(f32)
    keep = jnp.where(high_bit, summed[1], summed[0])
    send = jnp.where(high_bit, summed[0], summed[1]).astype(bf16)
    return keep + tp_xor(send, 2).astype(f32)


def gather_tokens(chunk, own):
    groups = []
    for shift in range(lax.axis_size("ctx")):
        if shift == 0 and own is not None:
            groups.append(own)
            continue
        here = from_ctx(chunk, shift) if shift else chunk
        far = tp_xor(here, 2)
        near, near_far = tp_xor(here, 1), tp_xor(far, 1)
        groups.append(jnp.concatenate([here, near, far, near_far], axis=0))
    return groups


def scatter_tokens(partial_sums):
    size = lax.axis_size("ctx")
    total = None
    for shift in reversed(range(size)):
        parts = partial_sums[shift].reshape((4, -1, partial_sums[shift].shape[-1]))
        came = tp_xor(jnp.stack([parts[1], parts[3]]).astype(bf16), 1).astype(f32)
        near, far = parts[0] + came[0], parts[2] + came[1]
        summed = near + tp_xor(far.astype(bf16), 2).astype(f32)
        if shift:
            summed = lax.ppermute(
                summed.astype(bf16), "ctx", [(i, (i + shift) % size) for i in range(size)]
            ).astype(f32)
        total = summed if total is None else total + summed
    return total


def on_device(
    hidden_in,
    cotangent,
    doc_lengths,
    attn_gain,
    q_gain,
    kv_gain,
    ffn_gain,
    q_down,
    kv_down,
    q_up,
    kv_up,
    out_proj,
    gate_proj,
    up_proj,
    down_proj,
):
    seqs, piece, width = hidden_in.shape
    n_shard, n_ctx, n_tp = lax.axis_size("shard"), lax.axis_size("ctx"), lax.axis_size("tp")
    rank = lax.axis_index("tp")
    low_bit = (rank & 1) == 1
    rows = seqs * piece
    chunk_rows = rows // n_tp
    seq_len = piece * n_ctx
    offset = lax.axis_index("ctx") * piece
    scale = 1.0 / math.sqrt(NOPE + ROPE)
    q_part, kv_part = QRANK // n_tp, (KVRANK + ROPE) // n_tp
    part = q_part + kv_part
    block = q_down.shape[0]
    n_gain = 2 * attn_gain.shape[0] + q_gain.shape[0] + kv_gain.shape[0]

    gain_row = jnp.concatenate([attn_gain, ffn_gain, q_gain, kv_gain])
    gain_rows = jnp.pad(gain_row[None], ((0, PAD - 1), (0, part - n_gain)))
    small = jnp.stack(
        [
            jnp.concatenate(
                [
                    jnp.concatenate(
                        [
                            q_down[:, i * q_part : (i + 1) * q_part],
                            kv_down[:, i * kv_part : (i + 1) * kv_part],
                        ],
                        axis=1,
                    ),
                    gain_rows,
                ],
                axis=0,
            )
            for i in range(n_tp)
        ]
    )
    small = lax.all_to_all(small, "tp", 0, 0)
    small = gather_shard(gather_ctx(small), 0)
    small = small.reshape(n_shard * n_ctx * n_tp, block + PAD, part)
    gains = small[:, block, :].astype(f32)
    cut = attn_gain.shape[0]
    gain_attn = gains[:, :cut].reshape(1, -1)
    gain_ffn = gains[:, cut : 2 * cut].reshape(1, -1)
    gain_query = gains[:, 2 * cut : 2 * cut + q_gain.shape[0]].reshape(1, -1)
    gain_latent = gains[:, 2 * cut + q_gain.shape[0] : n_gain].reshape(1, -1)
    down_part = small[:, :block, :].reshape(width, part)

    up_query = gather_shard(gather_ctx(q_up).reshape(-1, q_up.shape[1]), 0)
    up_latent = gather_shard(gather_ctx(kv_up).reshape(-1, kv_up.shape[1]), 0)
    out_full = gather_shard(
        gather_ctx(out_proj).transpose(1, 0, 2).reshape(out_proj.shape[0], -1), 1
    )

    gate_full = gather_shard(lax.all_to_all(gate_proj, "ctx", 1, 0, tiled=True), 0)
    upward_full = gather_shard(lax.all_to_all(up_proj, "ctx", 1, 0, tiled=True), 0)
    down_full = gather_shard(lax.all_to_all(down_proj, "ctx", 0, 1, tiled=True), 1)

    down_all = gather_tp(down_part)
    down_query = down_all[:, :, :q_part].transpose(1, 0, 2).reshape(width, QRANK)
    down_latent = down_all[:, :, q_part:].transpose(1, 0, 2).reshape(width, KVRANK + ROPE)

    heads = up_query.shape[1] // (NOPE + ROPE)
    positions_all = jnp.arange(seq_len, dtype=jnp.int32)
    positions_here = offset + jnp.arange(piece, dtype=jnp.int32)
    cosine_here, sine_here = rope_tables(positions_here)
    ends = jnp.stack(
        [jnp.sum(doc_lengths[:, : i + 1], axis=1) for i in range(doc_lengths.shape[1])], axis=1
    )

    def segments(positions):
        return jnp.sum((positions[None, :, None] >= ends[:, None, :]).astype(jnp.int32), axis=-1)

    segment_all, segment_here = segments(positions_all), segments(positions_here)
    causal = positions_here[:, None] >= positions_all[None, :]
    allowed = (causal[None] & (segment_here[:, :, None] == segment_all[:, None, :]))[:, None]

    stream = hidden_in.astype(f32).reshape(rows, width)
    grad_out = cotangent.astype(f32).reshape(rows, width)
    chunk_start = rank * chunk_rows

    def own_chunk(values):
        return lax.dynamic_slice_in_dim(values, chunk_start, chunk_rows, 0)

    def rank_groups(values):
        grouped = values.reshape(n_tp, chunk_rows, values.shape[-1])
        return jnp.concatenate(
            [lax.dynamic_index_in_dim(grouped, rank ^ i, 0, False) for i in range(n_tp)], axis=0
        )

    grad_ffn = (res_scale * grad_out).astype(bf16)
    grad_ffn_groups = gather_tokens(own_chunk(grad_ffn), rank_groups(grad_ffn))

    inverse_one = rms_inverse(stream)
    normed_one = stream * inverse_one
    input_low = (normed_one * gain_attn).astype(bf16)
    low_rank = gather_tp(dot(input_low, down_part, ((1,), (0,))))
    query_latent = low_rank[:, :, :q_part].transpose(1, 0, 2).reshape(rows, QRANK)
    latent_raw = low_rank[:, :, q_part:].transpose(1, 0, 2).reshape(rows, KVRANK + ROPE)
    inverse_latent = rms_inverse(latent_raw[:, :KVRANK])
    normed_latent = latent_raw[:, :KVRANK] * inverse_latent
    latent_low = (normed_latent * gain_latent).astype(bf16).reshape(seqs, piece, KVRANK)
    rotary_key = rotate(
        latent_raw[:, KVRANK:].reshape(seqs, piece, ROPE), cosine_here, sine_here
    ).astype(bf16)
    keys_here = jnp.concatenate([latent_low, rotary_key], axis=-1)
    keys_half = keys_here.reshape(seqs, 2, piece // 2, KVRANK + ROPE)
    keys_half = gather_ctx(jnp.where(low_bit, keys_half[:, 1], keys_half[:, 0]))
    keys_other = tp_xor(keys_half, 1)
    keys_all = jnp.stack(
        [
            jnp.where(low_bit, keys_other, keys_half),
            jnp.where(low_bit, keys_half, keys_other),
        ],
        axis=2,
    )
    keys_all = keys_all.transpose(1, 0, 2, 3, 4).reshape(seqs, seq_len, KVRANK + ROPE)
    latent_all, rotary_all = keys_all[..., :KVRANK], keys_all[..., KVRANK:]

    inverse_query = rms_inverse(query_latent)
    normed_query = query_latent * inverse_query
    query_low = (normed_query * gain_query).astype(bf16)
    key_value = jnp.einsum("slr,rf->slf", latent_all, up_latent, preferred_element_type=f32)
    key_value = key_value.reshape(seqs, seq_len, heads, NOPE + VDIM)
    key_nope = key_value[..., :NOPE].astype(bf16)
    value_low = key_value[..., NOPE:].astype(bf16)
    query = dot(query_low, up_query, ((1,), (0,))).reshape(seqs, piece, heads, NOPE + ROPE)
    query_nope = query[..., :NOPE].astype(bf16)
    query_rope = rotate(query[..., NOPE:], cosine_here[:, None, :], sine_here[:, None, :]).astype(
        bf16
    )

    def masked_scores():
        raw = jnp.einsum("sqhd,skhd->shqk", query_nope, key_nope, preferred_element_type=f32)
        raw = raw + jnp.einsum("sqhd,skd->shqk", query_rope, rotary_all, preferred_element_type=f32)
        return jnp.where(allowed, raw * scale, big_negative)

    scores = masked_scores()
    row_max = jnp.max(scores, axis=-1, keepdims=True)
    weights = jnp.exp(scores - row_max)
    row_total = jnp.sum(weights, axis=-1, keepdims=True)
    log_total = row_max + jnp.log(row_total)
    prob_low = (weights / row_total).astype(bf16)
    attended = jnp.einsum("shqk,skhd->sqhd", prob_low, value_low, preferred_element_type=f32)
    attended_low = attended.reshape(rows, heads * VDIM).astype(bf16)

    attn_out = scatter_tp(
        dot(attended_low, out_full, ((1,), (0,))).reshape(n_tp, chunk_rows, width)
    )
    middle = own_chunk(stream) + res_scale * attn_out
    inverse_two = rms_inverse(middle)
    normed_two = middle * inverse_two
    ffn_groups = gather_tokens((normed_two * gain_ffn).astype(bf16), None)

    ffn_parts, grad_two_parts = [], []
    grad_gate_w = grad_upward_w = grad_down_w = 0.0
    for ffn_low, grad_low in zip(ffn_groups, grad_ffn_groups):
        gate_value = dot(ffn_low, gate_full, ((1,), (0,)))
        up_value = dot(ffn_low, upward_full, ((1,), (0,)))
        sigma = jax.nn.sigmoid(gate_value)
        gate_act = gate_value * sigma
        hidden_low = (gate_act * up_value).astype(bf16)
        grad_hidden = dot(grad_low, down_full, ((1,), (1,)))
        grad_gate = (grad_hidden * up_value * sigma * (1.0 + gate_value * (1.0 - sigma))).astype(
            bf16
        )
        grad_upward = (grad_hidden * gate_act).astype(bf16)
        grad_two_parts.append(
            dot(grad_gate, gate_full, ((1,), (1,))) + dot(grad_upward, upward_full, ((1,), (1,)))
        )
        ffn_parts.append(dot(hidden_low, down_full, ((1,), (0,))))
        grad_gate_w += dot(ffn_low, grad_gate, ((0,), (0,)))
        grad_upward_w += dot(ffn_low, grad_upward, ((0,), (0,)))
        grad_down_w += dot(hidden_low, grad_low, ((0,), (0,)))

    grad_two = scatter_tokens(grad_two_parts)
    grad_middle = own_chunk(grad_out) + norm_backward(grad_two, normed_two, inverse_two, gain_ffn)
    grad_gain_ffn = jnp.sum(grad_two * normed_two, axis=0)
    grad_attn = gather_tp((res_scale * grad_middle).astype(bf16)).reshape(rows, width)

    output = round_low(middle + res_scale * scatter_tokens(ffn_parts))
    output = gather_tp(output.astype(bf16)).astype(f32)

    grad_attended = dot(grad_attn, out_full, ((1,), (1,)))
    grad_attended = grad_attended.astype(bf16).reshape(seqs, piece, heads, VDIM)
    grad_value = jnp.einsum("shqk,sqhd->skhd", prob_low, grad_attended, preferred_element_type=f32)
    grad_prob = jnp.einsum("sqhd,skhd->shqk", grad_attended, value_low, preferred_element_type=f32)
    prob_again = jnp.exp(masked_scores() - log_total)
    grad_scores = prob_again * (grad_prob - jnp.sum(prob_again * grad_prob, axis=-1, keepdims=True))
    grad_scores = grad_scores.astype(bf16)
    grad_qnope = (
        jnp.einsum("shqk,skhd->sqhd", grad_scores, key_nope, preferred_element_type=f32) * scale
    )
    grad_qrope = (
        jnp.einsum("shqk,skd->sqhd", grad_scores, rotary_all, preferred_element_type=f32) * scale
    )
    grad_qrope = unrotate(grad_qrope, cosine_here[:, None, :], sine_here[:, None, :])
    grad_knope = (
        jnp.einsum("shqk,sqhd->skhd", grad_scores, query_nope, preferred_element_type=f32) * scale
    )
    grad_krope = (
        jnp.einsum("shqk,sqhd->skd", grad_scores, query_rope, preferred_element_type=f32) * scale
    )
    grad_query = (
        jnp.concatenate([grad_qnope, grad_qrope], axis=-1)
        .reshape(rows, heads * (NOPE + ROPE))
        .astype(bf16)
    )
    grad_key_value = jnp.concatenate([grad_knope, grad_value], axis=-1).astype(bf16)
    grad_key_value = grad_key_value.reshape(seqs * seq_len, heads * (NOPE + VDIM))

    grad_latent_all = dot(grad_key_value, up_latent, ((1,), (1,))).reshape(seqs, seq_len, KVRANK)
    grad_keys = jnp.concatenate([grad_latent_all, grad_krope], axis=-1)
    grad_keys = grad_keys.reshape(seqs, n_ctx, 2, piece // 2, KVRANK + ROPE).transpose(
        1, 2, 0, 3, 4
    )
    send = jnp.where(low_bit, grad_keys[:, 0], grad_keys[:, 1]).astype(bf16)
    grad_keys = jnp.where(low_bit, grad_keys[:, 1], grad_keys[:, 0]) + tp_xor(send, 1).astype(f32)
    grad_keys = scatter_ctx(grad_keys)
    grad_pre_query = dot(grad_query, up_query, ((1,), (1,)))
    grad_pre_query = grad_pre_query.reshape(seqs, 2, piece // 2, QRANK)
    send = jnp.where(low_bit, grad_pre_query[:, 0], grad_pre_query[:, 1]).astype(bf16)
    grad_pre_query = jnp.where(low_bit, grad_pre_query[:, 1], grad_pre_query[:, 0])
    grad_pre_query = grad_pre_query + tp_xor(send, 1).astype(f32)
    grad_low = jnp.concatenate([grad_pre_query, grad_keys], axis=-1).astype(bf16)
    grad_low = (grad_low.astype(f32) + tp_xor(grad_low, 2).astype(f32)).astype(bf16)
    grad_low = pair_order(grad_low[:, None], tp_xor(grad_low, 1)[:, None], low_bit, 1)
    grad_low = grad_low.reshape(rows, QRANK + KVRANK + ROPE).astype(f32)

    grad_out_query, grad_out_latent = grad_low[:, :QRANK], grad_low[:, QRANK : QRANK + KVRANK]
    grad_query_latent = norm_backward(grad_out_query, normed_query, inverse_query, gain_query)
    grad_compressed = norm_backward(grad_out_latent, normed_latent, inverse_latent, gain_latent)
    grad_gain_query = jnp.sum(own_chunk(grad_out_query * normed_query), axis=0)
    grad_gain_latent = jnp.sum(own_chunk(grad_out_latent * normed_latent), axis=0)
    grad_rotary = grad_low[:, QRANK + KVRANK :].reshape(seqs, piece, ROPE)
    grad_rotary = unrotate(grad_rotary, cosine_here, sine_here).reshape(rows, ROPE)
    grad_query_latent = grad_query_latent.astype(bf16)
    grad_latent_raw = jnp.concatenate([grad_compressed, grad_rotary], axis=-1).astype(bf16)

    grad_pre_one = dot(own_chunk(grad_query_latent), down_query, ((1,), (1,)))
    grad_pre_one = grad_pre_one + dot(own_chunk(grad_latent_raw), down_latent, ((1,), (1,)))
    normed_own = own_chunk(normed_one)
    grad_input = grad_middle + norm_backward(
        grad_pre_one, normed_own, own_chunk(inverse_one), gain_attn
    )
    grad_gain_attn = jnp.sum(grad_pre_one * normed_own, axis=0)
    grad_input = gather_tp(round_low(grad_input).astype(bf16)).astype(f32)

    grad_part = jnp.concatenate(
        [
            lax.dynamic_slice_in_dim(grad_query_latent, rank * q_part, q_part, 1),
            lax.dynamic_slice_in_dim(grad_latent_raw, rank * kv_part, kv_part, 1),
        ],
        axis=1,
    )
    n_blocks = n_shard * n_ctx * n_tp
    grad_small = dot(input_low, grad_part, ((0,), (0,))).reshape(n_blocks, block, part)
    grad_gains = jnp.concatenate(
        [
            grad_gain_attn.reshape(n_blocks, -1),
            grad_gain_ffn.reshape(n_blocks, -1),
            grad_gain_query.reshape(n_blocks, -1),
            grad_gain_latent.reshape(n_blocks, -1),
        ],
        axis=1,
    )
    grad_gains = jnp.pad(grad_gains[:, None], ((0, 0), (0, PAD - 1), (0, part - n_gain)))
    grad_small = jnp.concatenate([grad_small, grad_gains], axis=1)
    grad_small = scatter_ctx(
        scatter_shard(grad_small, 0).reshape(n_ctx, n_tp, block + PAD, part)
    )
    grad_small = lax.all_to_all(grad_small.astype(bf16), "tp", 0, 0).astype(f32)
    grad_gains = jnp.sum(grad_small[:, block, :], axis=0)
    grad_small = grad_small[:, :block].transpose(1, 0, 2)
    grad_down_query = grad_small[:, :, :q_part].reshape(block, QRANK)
    grad_down_latent = grad_small[:, :, q_part:].reshape(block, KVRANK + ROPE)

    def rows_grad(grad):
        mine = scatter_shard(grad, 0)
        return scatter_ctx(mine.reshape(n_ctx, -1, mine.shape[-1]))

    grad_up_query = rows_grad(dot(query_low, grad_query, ((0,), (0,))))
    grad_up_latent = rows_grad(
        dot(latent_all.reshape(-1, KVRANK), grad_key_value, ((0,), (0,)))
    )
    grad_out_w = scatter_shard(dot(attended_low, grad_attn, ((0,), (0,))), 1)
    grad_out_w = scatter_ctx(
        grad_out_w.reshape(grad_out_w.shape[0], n_ctx, -1).transpose(1, 0, 2)
    )

    def hidden_grad(grad):
        mine = scatter_shard(grad, 0).astype(bf16)
        return lax.all_to_all(mine, "ctx", 0, 1, tiled=True).astype(f32)

    grad_gate_w, grad_upward_w = hidden_grad(grad_gate_w), hidden_grad(grad_upward_w)
    grad_down_w = scatter_shard(grad_down_w, 1).astype(bf16)
    grad_down_w = lax.all_to_all(grad_down_w, "ctx", 1, 0, tiled=True).astype(f32)
    return (
        output.reshape(seqs, piece, width),
        grad_input.reshape(seqs, piece, width),
        grad_gains[:cut],
        grad_gains[2 * cut : 2 * cut + q_gain.shape[0]],
        grad_gains[2 * cut + q_gain.shape[0] : n_gain],
        grad_gains[cut : 2 * cut],
        grad_down_query,
        grad_down_latent,
        grad_up_query,
        grad_up_latent,
        grad_out_w,
        grad_gate_w,
        grad_upward_w,
        grad_down_w,
    )


def solution(mesh):
    all_axes = ("shard", "ctx", "tp")
    tokens, vector, square = P("shard", "ctx", None), P(all_axes), P(all_axes, None)
    inner, outer = P(("shard", "ctx"), "tp"), P("tp", ("shard", "ctx"))
    weights = (
        vector,
        vector,
        vector,
        vector,
        square,
        square,
        inner,
        inner,
        outer,
        inner,
        inner,
        outer,
    )
    return jax.shard_map(
        on_device,
        mesh=mesh,
        in_specs=(tokens, tokens, P("shard", None)) + weights,
        out_specs=(tokens, tokens) + weights,
        check_vma=False,
    )
```

time: 2140 us -> 1280 us (0.60)
  waiting for transfers between devices: 1570 us -> 474 us
  local copies, waits for them, and re-layouts: 49.8 us -> 227 us
  starting transfers between devices: 2.04 us -> 149 us
  blocking collectives: 135 us -> 0 us
  other arithmetic: 97.1 us -> 216 us
  matrix products: 267 us -> 195 us
    reduce_scatter x10 -> x0, waiting for transfers between devices: 743 us -> none  [the longest x1 152 us: on_device(): lax.psum_scatter(grad_gate_w.astype(jnp.bfloat16), ('shard', 'ctx'), scat...]
    all_gather x8 -> x0, waiting for transfers between devices: 438 us -> none  [the longest x1 123 us: on_device(): lax.all_gather(up_proj, ('shard', 'ctx'), axis=0, tiled=True)]
    psum x3 -> x0, waiting for transfers between devices: 383 us -> none  [head_total(): return lax.psum(partial_sum, 'tp')]
    ppermute x0 -> x80, waiting for transfers between devices: none -> 287 us  [the longest x54 122 us: tp_xor(): return lax.ppermute(values, 'tp', [(i, i ^ mask) for i in range(size)])]
    all_to_all x0 -> x18, waiting for transfers between devices: none -> 187 us  [the longest x5 73.1 us: gather_ctx(): return lax.all_to_all(spread, 'ctx', 0, 0)]
    all_to_all x0 -> x18, starting transfers between devices: none -> 93.2 us  [the longest x5 36.6 us: gather_ctx(): return lax.all_to_all(spread, 'ctx', 0, 0)]
    unnamed x2 -> x0, blocking collectives: 82.5 us -> none
    convert_element_type x17 -> x61, other arithmetic: 21.7 us -> 88.2 us  [the longest x8 16.4 us: scatter_tokens(): came = tp_xor(jnp.stack([parts[1], parts[3]]).astype(bf16), 1).astype(f32)]
  transfers between devices with their start and end apart: 21 -> 98, of which waited for: 15 -> 33; matrix products, arithmetic and copies ran while one was open for 14% -> 45% of each run, Pallas kernels for 0% -> 0%
where the time goes in v1:
time: 1280 us; the launch traced here: 1270 us
  waiting for transfers between devices  474 us (37%)
  local copies, waits for them, and re-layouts  227 us (18%)
  other arithmetic  216 us (17%)
  matrix products  195 us (15%)
  starting transfers between devices  149 us (12%)
    ppermute x54, waiting for transfers between devices, tp_xor(): return lax.ppermute(values, 'tp', [(i, i ^ mask) for i in range(size)])  122 us
    dot_general x48, matrix products, dot(): lax.dot_general(left, right, (dims, ((), ())), preferred_element_type=f32)  119 us
    ppermute x6, waiting for transfers between devices, scatter_tokens(): lax.ppermute(summed.astype(bf16), 'ctx', [(i, (i + shift) % size) for i i...  102 us
    unnamed x369, local copies, waits for them, and re-layouts  86.7 us
    all_to_all x5, waiting for transfers between devices, gather_ctx(): return lax.all_to_all(spread, 'ctx', 0, 0)  73.1 us
    all_to_all x5, waiting for transfers between devices, scatter_ctx(): came = lax.all_to_all(values.astype(bf16), 'ctx', 0, 0)  53.4 us
    ppermute x6, waiting for transfers between devices, from_ctx(): lax.ppermute(values, 'ctx', [((i + shift) % size, i) for i in range(size)])  42.6 us
    all_to_all x5, starting transfers between devices, gather_ctx(): return lax.all_to_all(spread, 'ctx', 0, 0)  36.6 us
  transfers between devices with their start and end apart: 98, of which 33 were waited for; matrix products, arithmetic and copies ran while one was open for 45% of the time, Pallas kernels for 0%

profile of v1, /device:TPU:0, one launch (start us, length us, event | category | flops | bytes accessed | tf_op | source)
XLA Modules:
  0.0 1265.3 jit_solution(17319673651149224054)
XLA Ops:
  16.6 5.7 all-to-all-start.3
  34.5 16.6 %all-to-all-start.4 = ((bf16[4,96,960]{2,1,0:T(8,128)(2,1)}), bf16[4,96,960]{2,1,0:T(8,128)(2,1)S(1)}, u32[]{:S(2)}, u32[]{:S(2)}) async-start(bf16[4,96,960]{2,1,0:T(8,128)(2,1)} %broadcast_in_dim.31), calls=%async_computation.4 | async-start | bytes 1572864 | tf_op jit(solution)/shard_map/all_to_all | solution.py:73
  53.0 52.4 %all-to-all-done.4 = bf16[4,96,960]{2,1,0:T(8,128)(2,1)S(1)} async-done(((bf16[4,96,960]{2,1,0:T(8,128)(2,1)}), bf16[4,96,960]{2,1,0:T(8,128)(2,1)S(1)}, u32[]{:S(2)}, u32[]{:S(2)}) %all-to-all-start.4) | async-done | bytes 737312 | tf_op jit(solution)/shard_map/all_to_all | solution.py:73
  107.5 4.3 all-to-all-start.1
  128.6 9.2 all-to-all-done.1
  137.8 4.3 all-to-all-start.7
  151.4 19.8 %all-to-all-done.7 = bf16[320,4,400]{0,2,1:T(8,128)(2,1)} async-done(((bf16[320,4,400]{0,2,1:T(8,128)(2,1)}), bf16[320,4,400]{0,2,1:T(8,128)(2,1)}, u32[]{:S(2)}, u32[]{:S(2)}) %all-to-all-start.7) | async-done | bytes 1024032 | tf_op jit(solution)/shard_map/all_to_all | solution.py:231
  171.2 4.3 all-to-all-start.8
  186.6 18.1 %all-to-all-done.8 = bf16[4,400,320]{2,1,0:T(8,128)(2,1)} async-done(((bf16[4,400,320]{2,1,0:T(8,128)(2,1)}), bf16[4,400,320]{2,1,0:T(8,128)(2,1)}, u32[]{:S(2)}, u32[]{:S(2)}) %all-to-all-start.8) | async-done | bytes 1024032 | tf_op jit(solution)/shard_map/all_to_all | solution.py:232
  204.7 4.3 all-to-all-start.6
  233.5 4.6 all-to-all-done.6
  240.4 4.6 all-to-all-start.5
  268.3 5.2 reshape.617
  282.6 9.2 collective-permute-done.1
  299.3 4.5 copy.663
  321.5 5.5 all-to-all-start.2
  335.2 8.3 all-to-all-done.2
  343.4 10.5 collective-permute-done.6
  362.6 9.8 fusion.105
  376.3 7.9 copy.624
  384.2 15.0 %fusion.174 = (f32[2,10,256]{2,1,0:T(8,128)S(1)}, f32[2,10,256,1024]{3,2,1,0:T(8,128)}) fusion(f32[2,1024,256,10]{1,2,3,0:T(8,128)} %fusion.105, bf16[2,1024,10,128]{1,3,2,0:T(8,128)(2,1)} %bitcast.549, f32[2,256,10,96]{1,3,2,0:T(8,128)} %copy-done.26, pred[2,256,1024]{2,1,0:T(8,128)(4,1)} %compare_and_fusion), kind=kOutput, calls=%fused_computation.448 | convolution fusion | flops 692055040 | bytes 45764608 | tf_op jit(solution)/shard_map/sqhd,skhd->shqk/dot_general | solution.py:309
  399.2 9.9 fusion.2
  420.0 5.9 fusion.81
  428.4 4.4 fusion.6
  447.8 8.4 collective-permute-done.8
  472.8 5.2 collective-permute-done.26
  479.7 13.4 %collective-permute-done.9 = bf16[128,2560]{1,0:T(8,128)(2,1)S(1)} collective-permute-done((bf16[128,2560]{1,0:T(8,128)(2,1)S(1)}, bf16[128,2560]{1,0:T(8,128)(2,1)S(1)}, u32[]{:S(2)}, u32[]{:S(2)}) %collective-permute-start.9) | collective-permute-done | bytes 655392 | tf_op jit(solution)/shard_map/ppermute | solution.py:67
  493.2 23.9 %collective-permute-done.19 = bf16[128,2560]{1,0:T(8,128)(2,1)S(1)} collective-permute-done((bf16[128,2560]{1,0:T(8,128)(2,1)S(1)}, bf16[128,2560]{1,0:T(8,128)(2,1)S(1)}, u32[]{:S(2)}, u32[]{:S(2)}) %collective-permute-start.19) | collective-permute-done | bytes 655392 | tf_op jit(solution)/shard_map/ppermute | solution.py:67
  536.9 11.9 collective-permute-done.11
  555.0 5.8 collective-permute-done.21
  570.0 4.8 fusion.182
  579.7 4.7 fusion.180
  592.1 4.8 fusion.181
  631.5 4.3 fusion.176
  659.9 6.5 all-to-all-start.17
  689.4 16.8 %collective-permute-done.17 = bf16[128,2560]{1,0:T(8,128)(2,1)} collective-permute-done((bf16[128,2560]{1,0:T(8,128)(2,1)}, bf16[128,2560]{1,0:T(8,128)(2,1)}, u32[]{:S(2)}, u32[]{:S(2)}) %collective-permute-start.17) | collective-permute-done | bytes 655392 | tf_op jit(solution)/shard_map/ppermute | solution.py:62
  709.0 11.2 collective-permute-done.24
  723.0 24.6 %collective-permute-done.45 = bf16[128,2560]{1,0:T(8,128)(2,1)S(1)} collective-permute-done((bf16[128,2560]{1,0:T(8,128)(2,1)S(1)}, bf16[128,2560]{1,0:T(8,128)(2,1)S(1)}, u32[]{:S(2)}, u32[]{:S(2)}) %collective-permute-start.45) | collective-permute-done | bytes 655392 | tf_op jit(solution)/shard_map/ppermute | solution.py:62
  748.5 15.3 %collective-permute-done.52 = bf16[128,2560]{1,0:T(8,128)(2,1)S(1)} collective-permute-done((bf16[128,2560]{1,0:T(8,128)(2,1)S(1)}, bf16[128,2560]{1,0:T(8,128)(2,1)S(1)}, u32[]{:S(2)}, u32[]{:S(2)}) %collective-permute-start.52) | collective-permute-done | bytes 655392 | tf_op jit(solution)/shard_map/ppermute | solution.py:62
  764.7 14.4 %collective-permute-done.59 = bf16[128,2560]{1,0:T(8,128)(2,1)S(1)} collective-permute-done((bf16[128,2560]{1,0:T(8,128)(2,1)S(1)}, bf16[128,2560]{1,0:T(8,128)(2,1)S(1)}, u32[]{:S(2)}, u32[]{:S(2)}) %collective-permute-start.59) | collective-permute-done | bytes 655392 | tf_op jit(solution)/shard_map/ppermute | solution.py:62
  787.1 11.0 collective-permute-done.46
  798.1 4.3 collective-permute-start.18
  802.5 59.0 %collective-permute-done.53 = bf16[128,2560]{1,0:T(8,128)(2,1)S(1)} collective-permute-done((bf16[128,2560]{1,0:T(8,128)(2,1)S(1)}, bf16[128,2560]{1,0:T(8,128)(2,1)S(1)}, u32[]{:S(2)}, u32[]{:S(2)}) %collective-permute-start.53) | collective-permute-done | bytes 655392 | tf_op jit(solution)/shard_map/ppermute | solution.py:155
  873.2 4.3 all-to-all-start.16
  877.5 32.4 %collective-permute-done.25 = bf16[128,2560]{1,0:T(8,128)(2,1)} collective-permute-done((bf16[128,2560]{1,0:T(8,128)(2,1)}, bf16[128,2560]{1,0:T(8,128)(2,1)}, u32[]{:S(2)}, u32[]{:S(2)}) %collective-permute-start.25) | collective-permute-done | bytes 655392 | tf_op jit(solution)/shard_map/ppermute | solution.py:155
  909.8 5.3 multiply_convert_fusion.5
  929.7 4.4 all-to-all-start.15
  948.4 12.0 all-to-all-done.15
  974.7 7.4 convolution_bitcast_fusion
  982.1 14.3 %multiply_reduce_fusion = (f32[2,10,256]{2,1,0:T(8,128)S(1)}, f32[2,10,256,1024]{3,2,1,0:T(8,128)}) fusion(f32[2,10,256,1024]{3,2,1,0:T(8,128)} %get-tuple-element.248, f32[2,10,256]{2,1,0:T(8,128)S(1)} %copy-done.122, bf16[2,1024,10,128]{1,3,2,0:T(8,128)(2,1)} %bitcast.551, bf16[2,256,10,64]{1,0,3,2:T(2,128)(2,1)S(1)} %reshape.628), kind=kOutput, calls=%fused_computation.4 | convolution fusion | flops 686812160 | bytes 45260800 | tf_op jit(solution)/shard_map/sqhd,skhd->shqk/dot_general | solution.py:362
  996.4 14.5 %multiply_convert_fusion = bf16[2,10,256,1024]{3,2,1,0:T(8,128)(2,1)S(1)} fusion(f32[2,10,256,1024]{3,2,1,0:T(8,128)} %get-tuple-element.266, f32[2,10,256,1024]{3,2,1,0:T(8,128)} %get-tuple-element.248, f32[2,10,256]{2,1,0:T(8,128)S(1)} %get-tuple-element.265, f32[2,10,256]{2,1,0:T(8,128)S(1)} %copy-done.122), kind=kLoop, calls=%fused_computation.3 | loop fusion | flops 20971520 | bytes 52469760 | tf_op jit(solution)/shard_map/convert_element_type | solution.py:365
  1012.9 7.5 fusion.27
  1032.2 6.0 fusion.85
  1048.3 10.3 copy.671
  1058.7 7.1 copy.723
  1094.1 11.1 all-to-all-done.9
  1110.0 4.3 all-to-all-start.13
  1129.1 7.0 copy.660
  1151.6 4.4 all-to-all-start.12
  1156.8 4.3 fusion.108
  1172.4 4.7 all-to-all-done.12
  1188.0 9.5 collective-permute-done.73
  1200.2 19.0 %all-to-all-done.14 = bf16[4,640,320]{1,2,0:T(8,128)(2,1)S(1)} async-done(((bf16[4,640,320]{1,2,0:T(8,128)(2,1)}), bf16[4,640,320]{1,2,0:T(8,128)(2,1)S(1)}, u32[]{:S(2)}, u32[]{:S(2)}) %all-to-all-start.14) | async-done | bytes 1638432 | tf_op jit(solution)/shard_map/all_to_all | solution.py:105
  1230.8 18.6 %all-to-all-done.10 = bf16[4,4,96,264]{2,3,1,0:T(8,128)(2,1)} async-done(((bf16[4,4,96,264]{2,3,1,0:T(8,128)(2,1)}), bf16[4,4,96,264]{2,3,1,0:T(8,128)(2,1)}, u32[]{:S(2)}, u32[]{:S(2)}) %all-to-all-start.10) | async-done | bytes 811040 | tf_op jit(solution)/shard_map/all_to_all | solution.py:105
  (832 shorter events, 558.6 us)
Async XLA Ops:
  24.6 124.0 %collective-permute-start.54 = (bf16[128,2560]{1,0:T(8,128)(2,1)}, bf16[128,2560]{1,0:T(8,128)(2,1)}, u32[]{:S(2)}, u32[]{:S(2)}) collective-permute-start(bf16[128,2560]{1,0:T(8,128)(2,1)} %multiply_convert_fusion.6), channel_id=1, source_target_pairs={{4,0},{8,4},{12,8},{0,12},{5,1},{9,5},{13,9},{1,13},{6,2},{10,6},{... | collective-permute-start | bytes 1966088 | tf_op jit(solution)/shard_map/ppermute | solution.py:67
  28.4 120.8 %collective-permute-start.40 = (bf16[128,2560]{1,0:T(8,128)(2,1)}, bf16[128,2560]{1,0:T(8,128)(2,1)}, u32[]{:S(2)}, u32[]{:S(2)}) collective-permute-start(bf16[128,2560]{1,0:T(8,128)(2,1)} %multiply_convert_fusion.6), channel_id=1, source_target_pairs={{12,0},{0,4},{4,8},{8,12},{13,1},{1,5},{5,9},{9,13},{14,2},{2,6},{... | collective-permute-start | bytes 1966088 | tf_op jit(solution)/shard_map/ppermute | solution.py:67
  28.4 149.1 %collective-permute-start.47 = (bf16[128,2560]{1,0:T(8,128)(2,1)}, bf16[128,2560]{1,0:T(8,128)(2,1)}, u32[]{:S(2)}, u32[]{:S(2)}) collective-permute-start(bf16[128,2560]{1,0:T(8,128)(2,1)} %multiply_convert_fusion.6), channel_id=1, source_target_pairs={{8,0},{12,4},{0,8},{4,12},{9,1},{13,5},{1,9},{5,13},{10,2},{14,6},... | collective-permute-start | bytes 1966088 | tf_op jit(solution)/shard_map/ppermute | solution.py:67
  34.5 70.9 %all-to-all-start.4 = ((bf16[4,96,960]{2,1,0:T(8,128)(2,1)}), bf16[4,96,960]{2,1,0:T(8,128)(2,1)S(1)}, u32[]{:S(2)}, u32[]{:S(2)}) async-start(bf16[4,96,960]{2,1,0:T(8,128)(2,1)} %broadcast_in_dim.31), calls=%async_computation.4 | async-start | bytes 1572864 | tf_op jit(solution)/shard_map/all_to_all | solution.py:73
  107.5 30.3 %all-to-all-start.1 = ((bf16[4,4,96,264]{2,3,1,0:T(8,128)(2,1)}), bf16[4,4,96,264]{2,3,1,0:T(8,128)(2,1)}, u32[]{:S(2)}, u32[]{:S(2)}) async-start(bf16[4,4,96,264]{2,3,1,0:T(8,128)(2,1)} %broadcast_in_dim.27), calls=%async_computation.1 | async-start | bytes 2162688 | tf_op jit(solution)/shard_map/all_to_all | solution.py:73
  137.8 33.4 %all-to-all-start.7 = ((bf16[320,4,400]{0,2,1:T(8,128)(2,1)}), bf16[320,4,400]{0,2,1:T(8,128)(2,1)}, u32[]{:S(2)}, u32[]{:S(2)}) async-start(bf16[320,4,400]{0,2,1:T(8,128)(2,1)} %bitcast.604), calls=%async_computation.7 | async-start | bytes 2457600 | tf_op jit(solution)/shard_map/all_to_all | solution.py:231
  147.0 33.1 %collective-permute-start.4 = (bf16[128,1280]{1,0:T(8,128)(2,1)}, bf16[128,1280]{1,0:T(8,128)(2,1)}, u32[]{:S(2)}, u32[]{:S(2)}) collective-permute-start(bf16[128,1280]{1,0:T(8,128)(2,1)} %bitcast.20), channel_id=1, source_target_pairs={{0,16},{16,0},{1,17},{17,1},{2,18},{18,2},{3,19},{19,3},{4,20},{20... | collective-permute-start | bytes 983048 | tf_op jit(solution)/shard_map/ppermute | solution.py:84
  148.5 34.7 %collective-permute-start.55 = (bf16[128,2560]{1,0:T(8,128)(2,1)}, bf16[128,2560]{1,0:T(8,128)(2,1)}, u32[]{:S(2)}, u32[]{:S(2)}) collective-permute-start(bf16[128,2560]{1,0:T(8,128)(2,1)} %collective-permute-done.54), channel_id=1, source_target_pairs={{0,1},{1,0},{2,3},{3,2},{4,5},{5,4},{6,7},{7,6},{8,9},{9,8},{10,11... | collective-permute-start | bytes 1966088 | tf_op jit(solution)/shard_map/ppermute | solution.py:62
  148.5 60.5 %collective-permute-start.56 = (bf16[128,2560]{1,0:T(8,128)(2,1)}, bf16[128,2560]{1,0:T(8,128)(2,1)}, u32[]{:S(2)}, u32[]{:S(2)}) collective-permute-start(bf16[128,2560]{1,0:T(8,128)(2,1)} %collective-permute-done.54), channel_id=1, source_target_pairs={{0,2},{1,3},{2,0},{3,1},{4,6},{5,7},{6,4},{7,5},{8,10},{9,11},{10,... | collective-permute-start | bytes 1966088 | tf_op jit(solution)/shard_map/ppermute | solution.py:62
  149.2 63.4 %collective-permute-start.41 = (bf16[128,2560]{1,0:T(8,128)(2,1)}, bf16[128,2560]{1,0:T(8,128)(2,1)}, u32[]{:S(2)}, u32[]{:S(2)}) collective-permute-start(bf16[128,2560]{1,0:T(8,128)(2,1)} %collective-permute-done.40), channel_id=1, source_target_pairs={{0,1},{1,0},{2,3},{3,2},{4,5},{5,4},{6,7},{7,6},{8,9},{9,8},{10,11... | collective-permute-start | bytes 1966088 | tf_op jit(solution)/shard_map/ppermute | solution.py:62
  171.2 33.4 %all-to-all-start.8 = ((bf16[4,400,320]{2,1,0:T(8,128)(2,1)}), bf16[4,400,320]{2,1,0:T(8,128)(2,1)}, u32[]{:S(2)}, u32[]{:S(2)}) async-start(bf16[4,400,320]{2,1,0:T(8,128)(2,1)} %bitcast.603), calls=%async_computation.8 | async-start | bytes 2457600 | tf_op jit(solution)/shard_map/all_to_all | solution.py:232
  177.5 35.1 %collective-permute-start.42 = (bf16[128,2560]{1,0:T(8,128)(2,1)}, bf16[128,2560]{1,0:T(8,128)(2,1)}, u32[]{:S(2)}, u32[]{:S(2)}) collective-permute-start(bf16[128,2560]{1,0:T(8,128)(2,1)} %collective-permute-done.40), channel_id=1, source_target_pairs={{0,2},{1,3},{2,0},{3,1},{4,6},{5,7},{6,4},{7,5},{8,10},{9,11},{10,... | collective-permute-start | bytes 1966088 | tf_op jit(solution)/shard_map/ppermute | solution.py:62
  180.1 37.0 %collective-permute-start.48 = (bf16[128,2560]{1,0:T(8,128)(2,1)}, bf16[128,2560]{1,0:T(8,128)(2,1)}, u32[]{:S(2)}, u32[]{:S(2)}) collective-permute-start(bf16[128,2560]{1,0:T(8,128)(2,1)} %collective-permute-done.47), channel_id=1, source_target_pairs={{0,1},{1,0},{2,3},{3,2},{4,5},{5,4},{6,7},{7,6},{8,9},{9,8},{10,11... | collective-permute-start | bytes 1966088 | tf_op jit(solution)/shard_map/ppermute | solution.py:62
  183.3 33.8 %collective-permute-start.49 = (bf16[128,2560]{1,0:T(8,128)(2,1)}, bf16[128,2560]{1,0:T(8,128)(2,1)}, u32[]{:S(2)}, u32[]{:S(2)}) collective-permute-start(bf16[128,2560]{1,0:T(8,128)(2,1)} %collective-permute-done.47), channel_id=1, source_target_pairs={{0,2},{1,3},{2,0},{3,1},{4,6},{5,7},{6,4},{7,5},{8,10},{9,11},{10,... | collective-permute-start | bytes 1966088 | tf_op jit(solution)/shard_map/ppermute | solution.py:62
  204.7 33.4 %all-to-all-start.6 = ((bf16[320,4,400]{0,2,1:T(8,128)(2,1)}), bf16[320,4,400]{0,2,1:T(8,128)(2,1)}, u32[]{:S(2)}, u32[]{:S(2)}) async-start(bf16[320,4,400]{0,2,1:T(8,128)(2,1)} %bitcast.602), calls=%async_computation.6 | async-start | bytes 2457600 | tf_op jit(solution)/shard_map/all_to_all | solution.py:230
  209.0 42.0 %collective-permute-start.5 = (bf16[384,960]{0,1:T(8,128)(2,1)S(1)}, bf16[384,960]{0,1:T(8,128)(2,1)}, u32[]{:S(2)}, u32[]{:S(2)}) collective-permute-start(bf16[384,960]{0,1:T(8,128)(2,1)S(1)} %copy-done.84), channel_id=1, source_target_pairs={{0,16},{16,0},{1,17},{17,1},{2,18},{18,2},{3,19},{19,3},{4,20},{20... | collective-permute-start | bytes 2211848 | tf_op jit(solution)/shard_map/ppermute | solution.py:84
  212.6 42.6 %collective-permute-start.57 = (bf16[128,2560]{1,0:T(8,128)(2,1)}, bf16[128,2560]{1,0:T(8,128)(2,1)}, u32[]{:S(2)}, u32[]{:S(2)}) collective-permute-start(bf16[128,2560]{1,0:T(8,128)(2,1)} %collective-permute-done.56), channel_id=1, source_target_pairs={{0,1},{1,0},{2,3},{3,2},{4,5},{5,4},{6,7},{7,6},{8,9},{9,8},{10,11... | collective-permute-start | bytes 1966088 | tf_op jit(solution)/shard_map/ppermute | solution.py:62
  212.6 63.9 %collective-permute-start.43 = (bf16[128,2560]{1,0:T(8,128)(2,1)}, bf16[128,2560]{1,0:T(8,128)(2,1)}, u32[]{:S(2)}, u32[]{:S(2)}) collective-permute-start(bf16[128,2560]{1,0:T(8,128)(2,1)} %collective-permute-done.42), channel_id=1, source_target_pairs={{0,1},{1,0},{2,3},{3,2},{4,5},{5,4},{6,7},{7,6},{8,9},{9,8},{10,11... | collective-permute-start | bytes 1966088 | tf_op jit(solution)/shard_map/ppermute | solution.py:62
  217.0 62.2 %collective-permute-start.50 = (bf16[128,2560]{1,0:T(8,128)(2,1)}, bf16[128,2560]{1,0:T(8,128)(2,1)}, u32[]{:S(2)}, u32[]{:S(2)}) collective-permute-start(bf16[128,2560]{1,0:T(8,128)(2,1)} %collective-permute-done.49), channel_id=1, source_target_pairs={{0,1},{1,0},{2,3},{3,2},{4,5},{5,4},{6,7},{7,6},{8,9},{9,8},{10,11... | collective-permute-start | bytes 1966088 | tf_op jit(solution)/shard_map/ppermute | solution.py:62
  219.1 38.6 %collective-permute-start = (bf16[4,4,96,264]{2,3,1,0:T(8,128)(2,1)}, bf16[4,4,96,264]{2,3,1,0:T(8,128)(2,1)}, u32[]{:S(2)}, u32[]{:S(2)}) collective-permute-start(bf16[4,4,96,264]{2,3,1,0:T(8,128)(2,1)} %all-to-all-done.1), channel_id=1, source_target_pairs={{0,16},{16,0},{1,17},{17,1},{2,18},{18,2},{3,19},{19,3},{4,20},{20... | collective-permute-start | bytes 2433032 | tf_op jit(solution)/shard_map/ppermute | solution.py:84
  240.4 63.4 %all-to-all-start.5 = ((bf16[4,640,320]{1,2,0:T(8,128)(2,1)}), bf16[4,640,320]{1,2,0:T(8,128)(2,1)}, u32[]{:S(2)}, u32[]{:S(2)}) async-start(bf16[4,640,320]{1,2,0:T(8,128)(2,1)} %broadcast_in_dim.33), calls=%async_computation.5 | async-start | bytes 3276800 | tf_op jit(solution)/shard_map/all_to_all | solution.py:73
  251.0 186.0 %collective-permute-start.14 = (bf16[1280,400]{0,1:T(8,128)(2,1)}, bf16[1280,400]{0,1:T(8,128)(2,1)}, u32[]{:S(2)}, u32[]{:S(2)}) collective-permute-start(bf16[1280,400]{0,1:T(8,128)(2,1)} %all_to_all.121), channel_id=1, source_target_pairs={{0,16},{16,0},{1,17},{17,1},{2,18},{18,2},{3,19},{19,3},{4,20},{20... | collective-permute-start | bytes 3072008 | tf_op jit(solution)/shard_map/ppermute | solution.py:84
  255.2 52.2 %collective-permute-start.15 = (bf16[400,1280]{1,0:T(8,128)(2,1)}, bf16[400,1280]{1,0:T(8,128)(2,1)}, u32[]{:S(2)}, u32[]{:S(2)}) collective-permute-start(bf16[400,1280]{1,0:T(8,128)(2,1)} %all_to_all.125), channel_id=1, source_target_pairs={{0,16},{16,0},{1,17},{17,1},{2,18},{18,2},{3,19},{19,3},{4,20},{20... | collective-permute-start | bytes 3072008 | tf_op jit(solution)/shard_map/ppermute | solution.py:84
  257.6 180.7 %collective-permute-start.13 = (bf16[1280,400]{0,1:T(8,128)(2,1)}, bf16[1280,400]{0,1:T(8,128)(2,1)}, u32[]{:S(2)}, u32[]{:S(2)}) collective-permute-start(bf16[1280,400]{0,1:T(8,128)(2,1)} %all_to_all.117), channel_id=1, source_target_pairs={{0,16},{16,0},{1,17},{17,1},{2,18},{18,2},{3,19},{19,3},{4,20},{20... | collective-permute-start | bytes 3072008 | tf_op jit(solution)/shard_map/ppermute | solution.py:84
  281.3 181.6 %collective-permute-start.69 = (bf16[2560,264]{0,1:T(8,128)(2,1)}, bf16[2560,264]{0,1:T(8,128)(2,1)}, u32[]{:S(2)}, u32[]{:S(2)}) collective-permute-start(bf16[2560,264]{0,1:T(8,128)(2,1)} %reshape.617), channel_id=1, source_target_pairs={{0,2},{1,3},{2,0},{3,1},{4,6},{5,7},{6,4},{7,5},{8,10},{9,11},{10,... | collective-permute-start | bytes 4055048 | tf_op jit(solution)/shard_map/ppermute | solution.py:62
  307.4 46.5 %collective-permute-start.6 = (bf16[640,1280]{1,0:T(8,128)(2,1)}, bf16[640,1280]{1,0:T(8,128)(2,1)}, u32[]{:S(2)}, u32[]{:S(2)}) collective-permute-start(bf16[640,1280]{1,0:T(8,128)(2,1)} %copy.634), channel_id=1, source_target_pairs={{0,16},{16,0},{1,17},{17,1},{2,18},{18,2},{3,19},{19,3},{4,20},{20... | collective-permute-start | bytes 4915208 | tf_op jit(solution)/shard_map/ppermute | solution.py:84
  465.5 27.7 %collective-permute-start.9 = (bf16[128,2560]{1,0:T(8,128)(2,1)S(1)}, bf16[128,2560]{1,0:T(8,128)(2,1)S(1)}, u32[]{:S(2)}, u32[]{:S(2)}) collective-permute-start(bf16[128,2560]{1,0:T(8,128)(2,1)S(1)} %multiply_convert_fusion.7), channel_id=1, source_target_pairs={{12,0},{0,4},{4,8},{8,12},{13,1},{1,5},{5,9},{9,13},{14,2},{2,6},{... | collective-permute-start | bytes 1966088 | tf_op jit(solution)/shard_map/ppermute | solution.py:67
  467.5 448.3 %collective-permute-start.70 = (bf16[2,2560,264]{1,2,0:T(8,128)(2,1)}, bf16[2,2560,264]{1,2,0:T(8,128)(2,1)}, u32[]{:S(2)}, u32[]{:S(2)}) collective-permute-start(bf16[2,2560,264]{1,2,0:T(8,128)(2,1)} %pad_maximum_fusion.2), channel_id=1, source_target_pairs={{0,1},{1,0},{2,3},{3,2},{4,5},{5,4},{6,7},{7,6},{8,9},{9,8},{10,11... | collective-permute-start | bytes 8110088 | tf_op jit(solution)/shard_map/ppermute | solution.py:62
  472.3 45.4 %collective-permute-start.33 = (bf16[128,2560]{1,0:T(8,128)(2,1)S(1)}, bf16[128,2560]{1,0:T(8,128)(2,1)S(1)}, u32[]{:S(2)}, u32[]{:S(2)}) collective-permute-start(bf16[128,2560]{1,0:T(8,128)(2,1)S(1)} %multiply_convert_fusion.7), channel_id=1, source_target_pairs={{0,1},{1,0},{2,3},{3,2},{4,5},{5,4},{6,7},{7,6},{8,9},{9,8},{10,11... | collective-permute-start | bytes 1966088 | tf_op jit(solution)/shard_map/ppermute | solution.py:62
  478.0 39.1 %collective-permute-start.19 = (bf16[128,2560]{1,0:T(8,128)(2,1)S(1)}, bf16[128,2560]{1,0:T(8,128)(2,1)S(1)}, u32[]{:S(2)}, u32[]{:S(2)}) collective-permute-start(bf16[128,2560]{1,0:T(8,128)(2,1)S(1)} %multiply_convert_fusion.7), channel_id=1, source_target_pairs={{8,0},{12,4},{0,8},{4,12},{9,1},{13,5},{1,9},{5,13},{10,2},{14,6},... | collective-permute-start | bytes 1966088 | tf_op jit(solution)/shard_map/ppermute | solution.py:67
  479.6 49.3 %collective-permute-start.27 = (bf16[128,2560]{1,0:T(8,128)(2,1)S(1)}, bf16[128,2560]{1,0:T(8,128)(2,1)S(1)}, u32[]{:S(2)}, u32[]{:S(2)}) collective-permute-start(bf16[128,2560]{1,0:T(8,128)(2,1)S(1)} %collective-permute-done.26), channel_id=1, source_target_pairs={{0,1},{1,0},{2,3},{3,2},{4,5},{5,4},{6,7},{7,6},{8,9},{9,8},{10,11... | collective-permute-start | bytes 1966088 | tf_op jit(solution)/shard_map/ppermute | solution.py:62
  517.9 30.9 %collective-permute-start.11 = (bf16[128,2560]{1,0:T(8,128)(2,1)S(1)}, bf16[128,2560]{1,0:T(8,128)(2,1)S(1)}, u32[]{:S(2)}, u32[]{:S(2)}) collective-permute-start(bf16[128,2560]{1,0:T(8,128)(2,1)S(1)} %collective-permute-done.9), channel_id=1, source_target_pairs={{0,2},{1,3},{2,0},{3,1},{4,6},{5,7},{6,4},{7,5},{8,10},{9,11},{10,... | collective-permute-start | bytes 1966088 | tf_op jit(solution)/shard_map/ppermute | solution.py:62
  534.8 26.1 %collective-permute-start.21 = (bf16[128,2560]{1,0:T(8,128)(2,1)S(1)}, bf16[128,2560]{1,0:T(8,128)(2,1)S(1)}, u32[]{:S(2)}, u32[]{:S(2)}) collective-permute-start(bf16[128,2560]{1,0:T(8,128)(2,1)S(1)} %collective-permute-done.19), channel_id=1, source_target_pairs={{0,2},{1,3},{2,0},{3,1},{4,6},{5,7},{6,4},{7,5},{8,10},{9,11},{10,... | collective-permute-start | bytes 1966088 | tf_op jit(solution)/shard_map/ppermute | solution.py:62
  535.6 108.8 %collective-permute-start.36 = (bf16[2,128,2560]{2,1,0:T(8,128)(2,1)}, bf16[2,128,2560]{2,1,0:T(8,128)(2,1)}, u32[]{:S(2)}, u32[]{:S(2)}) collective-permute-start(bf16[2,128,2560]{2,1,0:T(8,128)(2,1)} %pad_maximum_fusion.20), channel_id=1, source_target_pairs={{0,1},{1,0},{2,3},{3,2},{4,5},{5,4},{6,7},{7,6},{8,9},{9,8},{10,11... | collective-permute-start | bytes 3932168 | tf_op jit(solution)/shard_map/ppermute | solution.py:62
  548.8 101.0 %collective-permute-start.61 = (bf16[2,128,2560]{2,1,0:T(8,128)(2,1)}, bf16[2,128,2560]{2,1,0:T(8,128)(2,1)}, u32[]{:S(2)}, u32[]{:S(2)}) collective-permute-start(bf16[2,128,2560]{2,1,0:T(8,128)(2,1)} %pad_maximum_fusion.25), channel_id=1, source_target_pairs={{0,1},{1,0},{2,3},{3,2},{4,5},{5,4},{6,7},{7,6},{8,9},{9,8},{10,11... | collective-permute-start | bytes 3932168 | tf_op jit(solution)/shard_map/ppermute | solution.py:62
  601.0 54.3 %collective-permute-start.79 = (bf16[400,1280]{1,0:T(8,128)(2,1)}, bf16[400,1280]{1,0:T(8,128)(2,1)}, u32[]{:S(2)}, u32[]{:S(2)}) collective-permute-start(bf16[400,1280]{1,0:T(8,128)(2,1)} %select_convert_fusion.3), channel_id=1, source_target_pairs={{0,16},{16,0},{1,17},{17,1},{2,18},{18,2},{3,19},{19,3},{4,20},{20... | collective-permute-start | bytes 3072008 | tf_op jit(solution)/shard_map/ppermute | solution.py:98
  615.5 50.9 %collective-permute-start.16 = (bf16[2,128,2560]{2,1,0:T(8,128)(2,1)}, bf16[2,128,2560]{2,1,0:T(8,128)(2,1)}, u32[]{:S(2)}, u32[]{:S(2)}) collective-permute-start(bf16[2,128,2560]{2,1,0:T(8,128)(2,1)} %pad_maximum_fusion.17), channel_id=1, source_target_pairs={{0,1},{1,0},{2,3},{3,2},{4,5},{5,4},{6,7},{7,6},{8,9},{9,8},{10,11... | collective-permute-start | bytes 3932168 | tf_op jit(solution)/shard_map/ppermute | solution.py:62
  659.9 213.3 %all-to-all-start.17 = ((bf16[400,4,320]{2,0,1:T(8,128)(2,1)}), bf16[400,4,320]{2,0,1:T(8,128)(2,1)}, u32[]{:S(2)}, u32[]{:S(2)}) async-start(bf16[400,4,320]{2,0,1:T(8,128)(2,1)} %copy.676), calls=%async_computation.17 | async-start | bytes 2457600 | tf_op jit(solution)/shard_map/all_to_all | solution.py:472
  666.4 116.7 %collective-permute-start.78 = (bf16[1280,400]{0,1:T(8,128)(2,1)S(1)}, bf16[1280,400]{0,1:T(8,128)(2,1)}, u32[]{:S(2)}, u32[]{:S(2)}) collective-permute-start(bf16[1280,400]{0,1:T(8,128)(2,1)S(1)} %copy-done.97), channel_id=1, source_target_pairs={{0,16},{16,0},{1,17},{17,1},{2,18},{18,2},{3,19},{19,3},{4,20},{20... | collective-permute-start | bytes 3072008 | tf_op jit(solution)/shard_map/ppermute | solution.py:98
  674.2 112.3 %collective-permute-start.62 = (bf16[128,2560]{1,0:T(8,128)(2,1)}, bf16[128,2560]{1,0:T(8,128)(2,1)S(1)}, u32[]{:S(2)}, u32[]{:S(2)}) collective-permute-start(bf16[128,2560]{1,0:T(8,128)(2,1)} %fusion.36), channel_id=1, source_target_pairs={{0,2},{1,3},{2,0},{3,1},{4,6},{5,7},{6,4},{7,5},{8,10},{9,11},{10,... | collective-permute-start | bytes 1966088 | tf_op jit(solution)/shard_map/ppermute | solution.py:62
  678.8 27.4 %collective-permute-start.17 = (bf16[128,2560]{1,0:T(8,128)(2,1)}, bf16[128,2560]{1,0:T(8,128)(2,1)}, u32[]{:S(2)}, u32[]{:S(2)}) collective-permute-start(bf16[128,2560]{1,0:T(8,128)(2,1)} %fusion.75), channel_id=1, source_target_pairs={{0,2},{1,3},{2,0},{3,1},{4,6},{5,7},{6,4},{7,5},{8,10},{9,11},{10,... | collective-permute-start | bytes 1966088 | tf_op jit(solution)/shard_map/ppermute | solution.py:62
  685.1 35.1 %collective-permute-start.24 = (bf16[128,2560]{1,0:T(8,128)(2,1)S(1)}, bf16[128,2560]{1,0:T(8,128)(2,1)}, u32[]{:S(2)}, u32[]{:S(2)}) collective-permute-start(bf16[128,2560]{1,0:T(8,128)(2,1)S(1)} %copy-done.115), channel_id=1, source_target_pairs={{0,2},{1,3},{2,0},{3,1},{4,6},{5,7},{6,4},{7,5},{8,10},{9,11},{10,... | collective-permute-start | bytes 1966088 | tf_op jit(solution)/shard_map/ppermute | solution.py:62
  706.2 77.0 %collective-permute-start.31 = (bf16[128,2560]{1,0:T(8,128)(2,1)}, bf16[128,2560]{1,0:T(8,128)(2,1)}, u32[]{:S(2)}, u32[]{:S(2)}) collective-permute-start(bf16[128,2560]{1,0:T(8,128)(2,1)} %fusion.65), channel_id=1, source_target_pairs={{0,2},{1,3},{2,0},{3,1},{4,6},{5,7},{6,4},{7,5},{8,10},{9,11},{10,... | collective-permute-start | bytes 1966088 | tf_op jit(solution)/shard_map/ppermute | solution.py:62
  720.2 27.4 %collective-permute-start.45 = (bf16[128,2560]{1,0:T(8,128)(2,1)S(1)}, bf16[128,2560]{1,0:T(8,128)(2,1)S(1)}, u32[]{:S(2)}, u32[]{:S(2)}) collective-permute-start(bf16[128,2560]{1,0:T(8,128)(2,1)S(1)} %fusion.51), channel_id=1, source_target_pairs={{0,2},{1,3},{2,0},{3,1},{4,6},{5,7},{6,4},{7,5},{8,10},{9,11},{10,... | collective-permute-start | bytes 1966088 | tf_op jit(solution)/shard_map/ppermute | solution.py:62
  783.1 78.3 %collective-permute-start.53 = (bf16[128,2560]{1,0:T(8,128)(2,1)S(1)}, bf16[128,2560]{1,0:T(8,128)(2,1)S(1)}, u32[]{:S(2)}, u32[]{:S(2)}) collective-permute-start(bf16[128,2560]{1,0:T(8,128)(2,1)S(1)} %fusion.49), channel_id=1, source_target_pairs={{0,8},{4,12},{8,0},{12,4},{1,9},{5,13},{9,1},{13,5},{2,10},{6,14},... | collective-permute-start | bytes 1966088 | tf_op jit(solution)/shard_map/ppermute | solution.py:155
  783.2 78.3 %collective-permute-start.60 = (bf16[128,2560]{1,0:T(8,128)(2,1)S(1)}, bf16[128,2560]{1,0:T(8,128)(2,1)S(1)}, u32[]{:S(2)}, u32[]{:S(2)}) collective-permute-start(bf16[128,2560]{1,0:T(8,128)(2,1)S(1)} %fusion.44), channel_id=1, source_target_pairs={{0,4},{4,8},{8,12},{12,0},{1,5},{5,9},{9,13},{13,1},{2,6},{6,10},{... | collective-permute-start | bytes 1966088 | tf_op jit(solution)/shard_map/ppermute | solution.py:155
  786.5 86.2 %collective-permute-start.37 = (bf16[128,2560]{1,0:T(8,128)(2,1)}, bf16[128,2560]{1,0:T(8,128)(2,1)}, u32[]{:S(2)}, u32[]{:S(2)}) collective-permute-start(bf16[128,2560]{1,0:T(8,128)(2,1)} %fusion.56), channel_id=1, source_target_pairs={{0,2},{1,3},{2,0},{3,1},{4,6},{5,7},{6,4},{7,5},{8,10},{9,11},{10,... | collective-permute-start | bytes 1966088 | tf_op jit(solution)/shard_map/ppermute | solution.py:62
  798.1 79.4 %collective-permute-start.18 = (bf16[128,2560]{1,0:T(8,128)(2,1)}, bf16[128,2560]{1,0:T(8,128)(2,1)}, u32[]{:S(2)}, u32[]{:S(2)}) collective-permute-start(bf16[128,2560]{1,0:T(8,128)(2,1)} %fusion.78), channel_id=1, source_target_pairs={{0,12},{4,0},{8,4},{12,8},{1,13},{5,1},{9,5},{13,9},{2,14},{6,2},{... | collective-permute-start | bytes 1966088 | tf_op jit(solution)/shard_map/ppermute | solution.py:155
  861.5 48.4 %collective-permute-start.25 = (bf16[128,2560]{1,0:T(8,128)(2,1)}, bf16[128,2560]{1,0:T(8,128)(2,1)}, u32[]{:S(2)}, u32[]{:S(2)}) collective-permute-start(bf16[128,2560]{1,0:T(8,128)(2,1)} %fusion.73), channel_id=1, source_target_pairs={{0,8},{4,12},{8,0},{12,4},{1,9},{5,13},{9,1},{13,5},{2,10},{6,14},... | collective-permute-start | bytes 1966088 | tf_op jit(solution)/shard_map/ppermute | solution.py:155
  861.5 48.4 %collective-permute-start.32 = (bf16[128,2560]{1,0:T(8,128)(2,1)}, bf16[128,2560]{1,0:T(8,128)(2,1)}, u32[]{:S(2)}, u32[]{:S(2)}) collective-permute-start(bf16[128,2560]{1,0:T(8,128)(2,1)} %fusion.68), channel_id=1, source_target_pairs={{0,4},{4,8},{8,12},{12,0},{1,5},{5,9},{9,13},{13,1},{2,6},{6,10},{... | collective-permute-start | bytes 1966088 | tf_op jit(solution)/shard_map/ppermute | solution.py:155
  872.6 46.3 %collective-permute-start.77 = (bf16[1280,400]{0,1:T(8,128)(2,1)}, bf16[1280,400]{0,1:T(8,128)(2,1)}, u32[]{:S(2)}, u32[]{:S(2)}) collective-permute-start(bf16[1280,400]{0,1:T(8,128)(2,1)} %select_convert_fusion.5), channel_id=1, source_target_pairs={{0,16},{16,0},{1,17},{17,1},{2,18},{18,2},{3,19},{19,3},{4,20},{20... | collective-permute-start | bytes 3072008 | tf_op jit(solution)/shard_map/ppermute | solution.py:98
  873.2 56.5 %all-to-all-start.16 = ((bf16[4,320,400]{1,2,0:T(8,128)(2,1)}), bf16[4,320,400]{1,2,0:T(8,128)(2,1)}, u32[]{:S(2)}, u32[]{:S(2)}) async-start(bf16[4,320,400]{1,2,0:T(8,128)(2,1)} %copy.675), calls=%async_computation.16 | async-start | bytes 2457600 | tf_op jit(solution)/shard_map/all_to_all | solution.py:468
  928.3 35.6 %collective-permute-start.38 = (bf16[128,2560]{1,0:T(8,128)(2,1)}, bf16[128,2560]{1,0:T(8,128)(2,1)}, u32[]{:S(2)}, u32[]{:S(2)}) collective-permute-start(bf16[128,2560]{1,0:T(8,128)(2,1)} %get-tuple-element.206), channel_id=1, source_target_pairs={{0,2},{1,3},{2,0},{3,1},{4,6},{5,7},{6,4},{7,5},{8,10},{9,11},{10,... | collective-permute-start | bytes 1966088 | tf_op jit(solution)/shard_map/ppermute | solution.py:62
  929.7 30.7 %all-to-all-start.15 = ((bf16[4,320,400]{1,2,0:T(8,128)(2,1)}), bf16[4,320,400]{1,2,0:T(8,128)(2,1)}, u32[]{:S(2)}, u32[]{:S(2)}) async-start(bf16[4,320,400]{1,2,0:T(8,128)(2,1)} %copy.674), calls=%async_computation.15 | async-start | bytes 2457600 | tf_op jit(solution)/shard_map/all_to_all | solution.py:468
  937.0 30.4 %collective-permute-start.64 = (bf16[2,128,2560]{2,1,0:T(8,128)(2,1)}, bf16[2,128,2560]{2,1,0:T(8,128)(2,1)}, u32[]{:S(2)}, u32[]{:S(2)}) collective-permute-start(bf16[2,128,2560]{2,1,0:T(8,128)(2,1)} %pad_maximum_fusion.26), channel_id=1, source_target_pairs={{0,1},{1,0},{2,3},{3,2},{4,5},{5,4},{6,7},{7,6},{8,9},{9,8},{10,11... | collective-permute-start | bytes 3932168 | tf_op jit(solution)/shard_map/ppermute | solution.py:62
  967.4 216.0 %collective-permute-start.39 = (bf16[2,128,2560]{2,1,0:T(8,128)(2,1)}, bf16[2,128,2560]{2,1,0:T(8,128)(2,1)}, u32[]{:S(2)}, u32[]{:S(2)}) collective-permute-start(bf16[2,128,2560]{2,1,0:T(8,128)(2,1)} %pad_maximum_fusion.21), channel_id=1, source_target_pairs={{0,1},{1,0},{2,3},{3,2},{4,5},{5,4},{6,7},{7,6},{8,9},{9,8},{10,11... | collective-permute-start | bytes 3932168 | tf_op jit(solution)/shard_map/ppermute | solution.py:62
  1044.4 78.3 %collective-permute-start.76 = (bf16[640,1280]{1,0:T(8,128)(2,1)}, bf16[640,1280]{1,0:T(8,128)(2,1)}, u32[]{:S(2)}, u32[]{:S(2)}) collective-permute-start(bf16[640,1280]{1,0:T(8,128)(2,1)} %select_convert_fusion), channel_id=1, source_target_pairs={{0,16},{16,0},{1,17},{17,1},{2,18},{18,2},{3,19},{19,3},{4,20},{20... | collective-permute-start | bytes 4915208 | tf_op jit(solution)/shard_map/ppermute | solution.py:98
  1078.7 29.1 %collective-permute-start.75 = (bf16[128,1280]{1,0:T(8,128)(2,1)}, bf16[128,1280]{1,0:T(8,128)(2,1)}, u32[]{:S(2)}, u32[]{:S(2)}) collective-permute-start(bf16[128,1280]{1,0:T(8,128)(2,1)} %select_convert_fusion.10), channel_id=1, source_target_pairs={{0,16},{16,0},{1,17},{17,1},{2,18},{18,2},{3,19},{19,3},{4,20},{20... | collective-permute-start | bytes 983048 | tf_op jit(solution)/shard_map/ppermute | solution.py:98
  1110.0 41.5 %all-to-all-start.13 = ((bf16[4,32,1280]{2,1,0:T(8,128)(2,1)}), bf16[4,32,1280]{2,1,0:T(8,128)(2,1)}, u32[]{:S(2)}, u32[]{:S(2)}) async-start(bf16[4,32,1280]{2,1,0:T(8,128)(2,1)} %bitcast.615), calls=%async_computation.13 | async-start | bytes 655360 | tf_op jit(solution)/shard_map/all_to_all | solution.py:105
  1151.6 25.5 %all-to-all-start.12 = ((bf16[4,96,960]{2,1,0:T(8,128)(2,1)}), bf16[4,96,960]{2,1,0:T(8,128)(2,1)}, u32[]{:S(2)}, u32[]{:S(2)}) async-start(bf16[4,96,960]{2,1,0:T(8,128)(2,1)} %bitcast.609), calls=%async_computation.12 | async-start | bytes 1572864 | tf_op jit(solution)/shard_map/all_to_all | solution.py:105
  1171.3 26.3 %collective-permute-start.73 = (bf16[16,96,264]{1,2,0:T(8,128)(2,1)}, bf16[16,96,264]{1,2,0:T(8,128)(2,1)}, u32[]{:S(2)}, u32[]{:S(2)}) collective-permute-start(bf16[16,96,264]{1,2,0:T(8,128)(2,1)} %select_convert_fusion.2), channel_id=1, source_target_pairs={{0,16},{16,0},{1,17},{17,1},{2,18},{18,2},{3,19},{19,3},{4,20},{20... | collective-permute-start | bytes 2433032 | tf_op jit(solution)/shard_map/ppermute | solution.py:98
  1177.1 42.1 %all-to-all-start.14 = ((bf16[4,640,320]{1,2,0:T(8,128)(2,1)}), bf16[4,640,320]{1,2,0:T(8,128)(2,1)S(1)}, u32[]{:S(2)}, u32[]{:S(2)}) async-start(bf16[4,640,320]{1,2,0:T(8,128)(2,1)} %bitcast.147), calls=%async_computation.14 | async-start | bytes 3276800 | tf_op jit(solution)/shard_map/all_to_all | solution.py:105
  1183.4 44.9 %collective-permute-start.72 = (bf16[2,128,2560]{2,1,0:T(8,128)(2,1)}, bf16[2,128,2560]{2,1,0:T(8,128)(2,1)}, u32[]{:S(2)}, u32[]{:S(2)}) collective-permute-start(bf16[2,128,2560]{2,1,0:T(8,128)(2,1)} %pad_maximum_fusion.27), channel_id=1, source_target_pairs={{0,1},{1,0},{2,3},{3,2},{4,5},{5,4},{6,7},{7,6},{8,9},{9,8},{10,11... | collective-permute-start | bytes 3932168 | tf_op jit(solution)/shard_map/ppermute | solution.py:62
  1219.2 30.3 %all-to-all-start.10 = ((bf16[4,4,96,264]{2,3,1,0:T(8,128)(2,1)}), bf16[4,4,96,264]{2,3,1,0:T(8,128)(2,1)}, u32[]{:S(2)}, u32[]{:S(2)}) async-start(bf16[4,4,96,264]{2,3,1,0:T(8,128)(2,1)} %bitcast.605), calls=%async_computation.10 | async-start | bytes 2162688 | tf_op jit(solution)/shard_map/all_to_all | solution.py:105
  (197 other events, 2103.4 us)

commit v2 on v1

v2 whole, which is shorter than its diff:
```python
import functools
import math

import jax
import jax.numpy as jnp
from jax import lax
from jax.experimental import pallas as pl
from jax.experimental.pallas import tpu as pltpu
from jax.sharding import PartitionSpec as P

NOPE = 64
ROPE = 32
VDIM = 64
KVRANK = 256
QRANK = 768
LANES = 128
HEAD = NOPE + ROPE
score_scale = 1.0 / math.sqrt(HEAD)
log2e = 1.0 / math.log(2.0)
MIB = 1024 * 1024

eps = 1e-05
res_scale = 1.4 / math.sqrt(62.0)
big_negative = -1e30
f32 = jnp.float32
bf16 = jnp.bfloat16


def rope_tables(positions):
    half = ROPE // 2
    inverse = jnp.exp(-math.log(10000.0) * jnp.arange(half, dtype=f32) * 2.0 / ROPE)
    angles = positions.astype(f32)[:, None] * inverse[None, :]
    angles = jnp.concatenate([angles, angles], axis=-1)
    return (jnp.cos(angles), jnp.sin(angles))


def rotate_half(values):
    half = values.shape[-1] // 2
    return jnp.concatenate([-values[..., half:], values[..., :half]], axis=-1)


def rotate(values, cosine, sine):
    return values * cosine + rotate_half(values) * sine


def unrotate(grads, cosine, sine):
    return grads * cosine - rotate_half(grads) * sine


def rms_inverse(values):
    return lax.rsqrt(jnp.mean(values * values, axis=-1, keepdims=True) + eps)


def norm_backward(grad_out, normed, inverse_rms, gain):
    scaled = grad_out * gain
    return inverse_rms * (scaled - normed * jnp.mean(scaled * normed, axis=-1, keepdims=True))


def dot(left, right, dims):
    return lax.dot_general(left, right, (dims, ((), ())), preferred_element_type=f32)


def round_low(values):
    return lax.reduce_precision(values, 8, 7)


def tp_xor(values, mask):
    size = lax.axis_size("tp")
    return lax.ppermute(values, "tp", [(i, i ^ mask) for i in range(size)])


def from_ctx(values, shift):
    size = lax.axis_size("ctx")
    return lax.ppermute(values, "ctx", [((i + shift) % size, i) for i in range(size)])


def exchange_ctx(parts):
    size = lax.axis_size("ctx")
    me = lax.axis_index("ctx")
    came = [lax.dynamic_index_in_dim(parts, me, 0, False)]
    for shift in range(1, size):
        send = lax.dynamic_index_in_dim(parts, lax.rem(me + shift, size), 0, False)
        came.append(lax.ppermute(send, "ctx", [(i, (i + shift) % size) for i in range(size)]))
    return came


def placed(pieces, places):
    whole = jnp.zeros((len(pieces),) + pieces[0].shape, pieces[0].dtype)
    for piece, place in zip(pieces, places):
        whole = lax.dynamic_update_index_in_dim(whole, piece, place, 0)
    return whole


def gather_ctx(values):
    size = lax.axis_size("ctx")
    me = lax.axis_index("ctx")
    pieces = [values] + [from_ctx(values, shift) for shift in range(1, size)]
    return placed(pieces, [lax.rem(me + shift, size) for shift in range(size)])


def exchange_tp(parts):
    rank = lax.axis_index("tp")
    size = lax.axis_size("tp")
    pieces = [lax.dynamic_index_in_dim(parts, rank, 0, False)]
    for mask in range(1, size):
        pieces.append(tp_xor(lax.dynamic_index_in_dim(parts, rank ^ mask, 0, False), mask))
    return placed(pieces, [rank ^ mask for mask in range(size)])


def pair_order(own, other, second, axis):
    return jnp.concatenate(
        [jnp.where(second, other, own), jnp.where(second, own, other)], axis=axis
    )


def gather_shard(values, axis):
    if lax.axis_size("shard") == 2:
        other = lax.ppermute(values, "shard", [(0, 1), (1, 0)])
        return pair_order(values, other, lax.axis_index("shard") == 1, axis)
    return lax.all_gather(values, "shard", axis=axis, tiled=True)


def scatter_shard(values, axis):
    size = lax.axis_size("shard")
    if size == 2:
        length = values.shape[axis] // 2
        low = lax.slice_in_dim(values, 0, length, axis=axis)
        high = lax.slice_in_dim(values, length, 2 * length, axis=axis)
        second = lax.axis_index("shard") == 1
        keep = jnp.where(second, high, low)
        send = jnp.where(second, low, high).astype(bf16)
        return keep + lax.ppermute(send, "shard", [(0, 1), (1, 0)]).astype(f32)
    return lax.psum_scatter(
        values.astype(bf16), "shard", scatter_dimension=axis, tiled=True
    ).astype(f32)


def scatter_ctx(values):
    me = lax.axis_index("ctx")
    own = lax.dynamic_index_in_dim(values, me, 0, False).astype(f32)
    return sum((piece.astype(f32) for piece in exchange_ctx(values.astype(bf16))[1:]), own)


def gather_tp(chunk):
    rank = lax.axis_index("tp")
    low_bit, high_bit = (rank & 1) == 1, (rank >> 1) == 1
    other = tp_xor(chunk, 2)
    pair = jnp.stack([jnp.where(high_bit, other, chunk), jnp.where(high_bit, chunk, other)])
    across = tp_xor(pair, 1)
    both = jnp.stack(
        [jnp.where(low_bit, across, pair), jnp.where(low_bit, pair, across)], axis=1
    )
    return both.reshape((4,) + chunk.shape)


def scatter_tp(partial_sum):
    rank = lax.axis_index("tp")
    low_bit, high_bit = (rank & 1) == 1, (rank >> 1) == 1
    parts = partial_sum.reshape((2, 2) + partial_sum.shape[1:])
    keep = jnp.where(low_bit, parts[:, 1], parts[:, 0])
    send = jnp.where(low_bit, parts[:, 0], parts[:, 1]).astype(bf16)
    summed = keep + tp_xor(send, 1).astype(f32)
    keep = jnp.where(high_bit, summed[1], summed[0])
    send = jnp.where(high_bit, summed[0], summed[1]).astype(bf16)
    return keep + tp_xor(send, 2).astype(f32)


def after(values, earlier):
    return lax.optimization_barrier((values, earlier))[0]


def shifts():
    size = lax.axis_size("ctx")
    return sorted(range(size), key=lambda shift: (min(shift, size - shift), shift))


def gather_tokens(chunk):
    groups, last = [], None
    for shift in shifts():
        if len(groups) == 3:
            chunk = after(chunk, last)
        here = from_ctx(chunk, shift) if shift else chunk
        if shift and last is None:
            last = here
        far = tp_xor(here, 2)
        near, near_far = tp_xor(here, 1), tp_xor(far, 1)
        groups.append(jnp.concatenate([here, far, near, near_far], axis=0))
    return groups


def scatter_tp_groups(groups):
    result = []
    for group in groups:
        half = group.shape[0] // 2
        summed = group[:half].astype(f32) + tp_xor(group[half:], 1).astype(f32)
        far = tp_xor(summed[half // 2 :].astype(bf16), 2).astype(f32)
        result.append(summed[: half // 2] + far)
    return result


def scatter_ctx_groups(groups, earlier=None):
    size = lax.axis_size("ctx")
    came = [groups[0]]
    for shift, group in list(zip(shifts(), groups))[1:]:
        came.append(
            lax.ppermute(
                group.astype(bf16), "ctx", [(i, (i + shift) % size) for i in range(size)]
            )
        )
    if earlier is not None:
        came = after(came, earlier)
    return sum((piece.astype(f32) for piece in came[1:]), came[0])


def contract(left,right,ld,rd):
    return lax.dot_general(left,right,(((ld,),(rd,)),((),())),preferred_element_type=f32)

def turned(values, keep, ahead, behind):
    return values*keep + pltpu.roll(values, LANES-ROPE//2, 1)*ahead + pltpu.roll(values, ROPE//2, 1)*behind

def padded_query(q_ref, table_ref, head):
    raw = q_ref[0, :, head*HEAD:(head+1)*HEAD]
    raw = jnp.concatenate([raw, jnp.zeros((raw.shape[0], LANES-HEAD), f32)], axis=1)
    return turned(raw, table_ref[0], table_ref[1], table_ref[2]).astype(bf16)

def forward_kernel(heads, q_ref, kv_ref, rotary_ref, table_ref, limit_ref, o_ref, lse_ref, bias_ref):
    rows, keys = bias_ref.shape
    place = lax.broadcasted_iota(jnp.int32, (rows, keys), 1)
    inside = (place >= limit_ref[0, :, 0:1]) & (place <= limit_ref[0, :, 1:2])
    bias_ref[...] = jnp.where(inside, 0.0, big_negative)
    lane = lax.broadcasted_iota(jnp.int32, (rows, LANES), 1)
    key_lane = lax.broadcasted_iota(jnp.int32, (keys, LANES), 1)
    logs = jnp.zeros((rows, LANES), f32)
    held = None
    for head in range(heads):
        query = padded_query(q_ref, table_ref, head)
        kv = kv_ref[0, :, head*LANES:(head+1)*LANES]
        key = jnp.where(key_lane < NOPE, kv, rotary_ref[0])
        scores = contract(query, key, 1, 1)*(score_scale*log2e) + bias_ref[...]
        top = jnp.max(scores, axis=1, keepdims=True)
        weights = jnp.exp2(scores - top)
        total = jnp.sum(weights, axis=1, keepdims=True)
        out = contract(weights.astype(bf16), kv, 1, 0)*(1.0/total)
        logs = jnp.where(lane == head, top + jnp.log2(total), logs)
        if head % 2 == 0:
            held = pltpu.roll(out, VDIM, 1)
        else:
            start = (head//2)*LANES
            o_ref[0, :, start:start+LANES] = jnp.where(lane < VDIM, held, out).astype(bf16)
    lse_ref[0] = logs

def attention_forward(query, kv, rotary, table, limits, heads):
    seqs, rows, _ = query.shape
    keys = kv.shape[1]
    whole = lambda *dims: pl.BlockSpec((1,)+dims, lambda s: (s,)+(0,)*len(dims))
    return pl.pallas_call(
        functools.partial(forward_kernel, heads),
        grid=(seqs,),
        in_specs=[whole(*query.shape[1:]), whole(*kv.shape[1:]), whole(*rotary.shape[1:]),
                  pl.BlockSpec(table.shape, lambda s:(0,0,0)), whole(*limits.shape[1:])],
        out_specs=[whole(rows, heads*VDIM), whole(rows, LANES)],
        out_shape=[jax.ShapeDtypeStruct((seqs,rows,heads*VDIM),bf16), jax.ShapeDtypeStruct((seqs,rows,LANES),f32)],
        scratch_shapes=[pltpu.VMEM((rows,keys),f32)],
        compiler_params=pltpu.CompilerParams(vmem_limit_bytes=50*1024*1024),
        cost_estimate=pl.CostEstimate(flops=seqs*heads*rows*keys*4*LANES, bytes_accessed=12_000_000, transcendentals=seqs*heads*rows*keys),
    )(query, kv, rotary, table, limits)

def backward_kernel(heads, q_ref, kv_ref, rotary_ref, table_ref, limit_ref, lse_ref, go_ref, gq_ref, gkv_ref, gkr_ref, bias_ref):
    keys, rows = bias_ref.shape
    place = lax.broadcasted_iota(jnp.int32, (keys, rows), 0)
    inside = (place >= limit_ref[0, 0:1, :]) & (place <= limit_ref[0, 1:2, :])
    bias_ref[...] = jnp.where(inside, 0.0, big_negative)
    lane = lax.broadcasted_iota(jnp.int32, (rows, LANES), 1)
    key_lane = lax.broadcasted_iota(jnp.int32, (keys, LANES), 1)
    logs = lse_ref[0].T
    grad_rotary = jnp.zeros((keys, LANES), f32)
    for head in range(heads):
        query = padded_query(q_ref, table_ref, head)
        kv = kv_ref[0, :, head*LANES:(head+1)*LANES]
        key = jnp.where(key_lane < NOPE, kv, rotary_ref[0])
        start = (head//2)*LANES
        go = go_ref[0, :, start:start+LANES].astype(f32)
        if head % 2 == 0:
            go = pltpu.roll(go, VDIM, 1)
        go = jnp.where(lane < VDIM, 0.0, go).astype(bf16)
        scores = contract(key, query, 1, 1)*(score_scale*log2e) + bias_ref[...]
        prob = jnp.exp2(scores - logs[head:head+1, :])
        grad_prob = contract(kv, go, 1, 1)
        grad_value = contract(prob.astype(bf16), go, 1, 0)
        mixed = jnp.sum(prob*grad_prob, axis=0, keepdims=True)
        grad_scores = (prob*(grad_prob - mixed)).astype(bf16)
        grad_key = contract(grad_scores, query, 1, 0)*score_scale
        grad_rotary = grad_rotary + grad_key
        gkv_ref[0, :, head*LANES:(head+1)*LANES] = jnp.where(key_lane < NOPE, grad_key, grad_value).astype(bf16)
        grad_query = contract(key, grad_scores, 0, 0).T*score_scale
        grad_query = turned(grad_query, table_ref[0], -table_ref[1], -table_ref[2])
        gq_ref[0, :, head*HEAD:(head+1)*HEAD] = grad_query[:, :HEAD].astype(bf16)
    gkr_ref[0] = grad_rotary

def attention_backward(query, kv, rotary, table, limits, lse, go, heads):
    seqs, rows, _ = query.shape
    keys = kv.shape[1]
    whole = lambda *dims: pl.BlockSpec((1,)+dims, lambda s: (s,)+(0,)*len(dims))
    return pl.pallas_call(
        functools.partial(backward_kernel, heads),
        grid=(seqs,),
        in_specs=[whole(*query.shape[1:]), whole(*kv.shape[1:]), whole(*rotary.shape[1:]),
                  pl.BlockSpec(table.shape, lambda s:(0,0,0)), whole(*limits.shape[1:]), whole(*lse.shape[1:]), whole(*go.shape[1:])],
        out_specs=[whole(rows, heads*HEAD), whole(keys, heads*LANES), whole(keys, LANES)],
        out_shape=[jax.ShapeDtypeStruct((seqs,rows,heads*HEAD),bf16), jax.ShapeDtypeStruct((seqs,keys,heads*LANES),bf16), jax.ShapeDtypeStruct((seqs,keys,LANES),f32)],
        scratch_shapes=[pltpu.VMEM((keys,rows),f32)],
        compiler_params=pltpu.CompilerParams(vmem_limit_bytes=58*1024*1024),
        cost_estimate=pl.CostEstimate(flops=seqs*heads*rows*keys*10*LANES, bytes_accessed=20_000_000, transcendentals=seqs*heads*rows*keys),
    )(query, kv, rotary, table, limits, lse, go)


def halves(count, length):
    if count == 1:
        return [0]
    second = lax.axis_index("shard")
    return [pl.multiple_of(second * length, LANES), pl.multiple_of((1 - second) * length, LANES)]


def weights_kernel(n_group, n_piece, *refs):
    refs = list(refs)

    def take(count):
        return [refs.pop(0) for _ in range(count)]

    tokens = [take(n_piece) for _ in range(n_group)]
    grads = [take(n_piece) for _ in range(n_group)]
    kept = [take(3) for _ in range(n_group)]
    down_out, gate_out, up_out = refs
    down = gate = up = 0.0
    for group in range(n_group):
        token = jnp.concatenate([piece[...] for piece in tokens[group]], axis=0)
        grad = jnp.concatenate([piece[...] for piece in grads[group]], axis=0)
        hidden, grad_gate, grad_up = kept[group]
        down = down + contract(hidden[...], grad, 1, 0)
        gate = gate + contract(grad_gate[...], token, 1, 0)
        up = up + contract(grad_up[...], token, 1, 0)
    down_out[...] = down.astype(bf16)
    gate_out[...] = gate.astype(bf16)
    up_out[...] = up.astype(bf16)


def ffn_weight_grads(tokens, grads, kept):
    n_group, n_piece = len(tokens), len(tokens[0])
    rows, width = tokens[0][0].shape
    units = kept[0][0].shape[0]
    step = 512

    def column(height):
        return pl.BlockSpec((height, step), lambda i: (0, i))

    whole = pl.BlockSpec(kept[0][0].shape, lambda i: (0, 0))
    flat = [piece for group in tokens for piece in group]
    flat += [piece for group in grads for piece in group]
    total = rows * n_piece * n_group
    return pl.pallas_call(
        functools.partial(weights_kernel, n_group, n_piece),
        grid=(width // step,),
        in_specs=[column(rows)] * len(flat) + [whole] * (3 * n_group),
        out_specs=[column(units)] * 3,
        out_shape=[jax.ShapeDtypeStruct((units, width), bf16)] * 3,
        compiler_params=pltpu.CompilerParams(vmem_limit_bytes=48 * MIB),
        cost_estimate=pl.CostEstimate(
            flops=6 * total * width * units, bytes_accessed=33_000_000, transcendentals=0
        ),
    )(*flat, *[array for group in kept for array in group])


def by_ctx(size, write):
    me = lax.axis_index("ctx")
    for place in range(size):

        @pl.when(me == place)
        def _(place=place):
            write(place)


def join_kernel(size, *refs):
    length = refs[0].shape[1]
    out_ref = refs[-1]

    def write(me):
        for k in range(size):
            block = (me - k) % size
            out_ref[:, block * length : (block + 1) * length] = refs[k][...]

    by_ctx(size, write)


def join_columns(pieces):
    size = len(pieces)
    height, length = pieces[0].shape
    return pl.pallas_call(
        functools.partial(join_kernel, size),
        out_shape=jax.ShapeDtypeStruct((height, size * length), pieces[0].dtype),
        compiler_params=pltpu.CompilerParams(vmem_limit_bytes=16 * MIB),
        cost_estimate=pl.CostEstimate(
            flops=0, bytes_accessed=4 * size * pieces[0].size, transcendentals=0
        ),
    )(*pieces)


def place_kernel(size, turn, *refs):
    out_ref = refs[-1]
    height = refs[0].shape[0]

    def write(me):
        for k in range(size):
            block = (me - k) % size
            piece = refs[k][...].astype(f32)
            if turn:
                out_ref[:, block * height : (block + 1) * height] = piece.T
            else:
                out_ref[block * height : (block + 1) * height, :] = piece

    by_ctx(size, write)


def place_rows(pieces, turn):
    size = len(pieces)
    height, length = pieces[0].shape
    shape = (length, size * height) if turn else (size * height, length)
    return pl.pallas_call(
        functools.partial(place_kernel, size, turn),
        out_shape=jax.ShapeDtypeStruct(shape, f32),
        compiler_params=pltpu.CompilerParams(vmem_limit_bytes=24 * MIB),
        cost_estimate=pl.CostEstimate(
            flops=0, bytes_accessed=6 * size * pieces[0].size, transcendentals=0
        ),
    )(*pieces)


def split_kernel(n_half, keep_ref, came_ref, out_ref):
    n, height, length = out_ref.shape
    keep = keep_ref[:, pl.ds(halves(n_half, n * length)[0], n * length)].astype(f32)
    total = (keep + came_ref[...].astype(f32)).astype(bf16)
    for i in range(n):
        out_ref[i] = total[:, i * length : (i + 1) * length]


def add_and_split(values, came, n):
    height, length = came.shape
    return pl.pallas_call(
        functools.partial(split_kernel, values.shape[1] // length),
        out_shape=jax.ShapeDtypeStruct((n, height, length // n), bf16),
        compiler_params=pltpu.CompilerParams(vmem_limit_bytes=24 * MIB),
        cost_estimate=pl.CostEstimate(flops=0, bytes_accessed=6 * came.size, transcendentals=0),
    )(values, came)


def on_device(
    hidden_in,
    cotangent,
    doc_lengths,
    attn_gain,
    q_gain,
    kv_gain,
    ffn_gain,
    q_down,
    kv_down,
    q_up,
    kv_up,
    out_proj,
    gate_proj,
    up_proj,
    down_proj,
):
    seqs, piece, width = hidden_in.shape
    n_shard, n_ctx, n_tp = lax.axis_size("shard"), lax.axis_size("ctx"), lax.axis_size("tp")
    rank = lax.axis_index("tp")
    low_bit = (rank & 1) == 1
    rows = seqs * piece
    chunk_rows = rows // n_tp
    seq_len = piece * n_ctx
    offset = lax.axis_index("ctx") * piece
    q_part, kv_part = QRANK // n_tp, (KVRANK + ROPE) // n_tp
    part = q_part + kv_part
    block = q_down.shape[0]
    n_gain = 2 * attn_gain.shape[0] + q_gain.shape[0] + kv_gain.shape[0]

    gain_row = jnp.concatenate([attn_gain, ffn_gain, q_gain, kv_gain])
    n_blocks = n_shard * n_ctx * n_tp
    everywhere = ("shard", "ctx", "tp")
    gains = lax.all_to_all(
        jnp.broadcast_to(gain_row[None, None], (n_blocks, 1, n_gain)), everywhere, 0, 0
    )
    gains = gains[:, 0].astype(f32)
    cut = attn_gain.shape[0]
    gain_attn = gains[:, :cut].reshape(1, -1)
    gain_ffn = gains[:, cut : 2 * cut].reshape(1, -1)
    gain_query = gains[:, 2 * cut : 2 * cut + q_gain.shape[0]].reshape(1, -1)
    gain_latent = gains[:, 2 * cut + q_gain.shape[0] :].reshape(1, -1)

    small = jnp.stack(
        [
            jnp.concatenate(
                [
                    q_down[:, i * q_part : (i + 1) * q_part],
                    kv_down[:, i * kv_part : (i + 1) * kv_part],
                ],
                axis=1,
            )
            for i in range(n_tp)
        ]
    )
    small = gather_ctx(exchange_tp(small).reshape(-1, part))
    q_up, kv_up, out_proj, gate_proj, up_proj, down_proj = lax.optimization_barrier(
        (q_up, kv_up, out_proj, gate_proj, up_proj, down_proj, small)
    )[:6]
    down_part = gather_shard(small.reshape(-1, part), 0)

    up_query = gather_ctx(q_up)
    up_latent = gather_ctx(kv_up)
    up_query = gather_shard(up_query.reshape(-1, q_up.shape[1]), 0)
    up_latent = gather_shard(up_latent.reshape(-1, kv_up.shape[1]), 0)
    out_full = lax.all_gather(out_proj, ("shard", "ctx"), axis=1, tiled=True)

    heads = up_query.shape[1] // HEAD
    positions = offset + jnp.arange(piece, dtype=jnp.int32)
    cosine_here, sine_here = rope_tables(positions)
    docs = doc_lengths.shape[1]
    ends = jnp.stack([jnp.sum(doc_lengths[:, : i + 1], axis=1) for i in range(docs)], axis=1)
    starts = jnp.max(
        jnp.where(positions[None, :, None] >= ends[:, None, :], ends[:, None, :], 0), axis=-1
    )
    limits = jnp.stack([starts, jnp.broadcast_to(positions[None], starts.shape)], axis=1)
    cosine, sine = cosine_here[:, : ROPE // 2], sine_here[:, : ROPE // 2]
    zero, fill = jnp.zeros_like(cosine), jnp.zeros((piece, LANES - HEAD), f32)
    plain = jnp.zeros((piece, NOPE), f32)
    table = jnp.stack(
        [
            jnp.concatenate([plain + 1.0, cosine, cosine, fill], axis=1),
            jnp.concatenate([plain, -sine, zero, fill], axis=1),
            jnp.concatenate([plain, zero, sine, fill], axis=1),
        ]
    )

    stream = hidden_in.astype(f32).reshape(rows, width)
    grad_out = cotangent.astype(f32).reshape(rows, width)
    chunk_start = rank * chunk_rows

    def own_chunk(values):
        return lax.dynamic_slice_in_dim(values, chunk_start, chunk_rows, 0)

    inverse_one = rms_inverse(stream)
    normed_one = stream * inverse_one
    input_low = (normed_one * gain_attn).astype(bf16)
    low_rank = gather_tp(dot(input_low, down_part, ((1,), (0,))))
    query_latent = low_rank[:, :, :q_part].transpose(1, 0, 2).reshape(rows, QRANK)
    latent_raw = low_rank[:, :, q_part:].transpose(1, 0, 2).reshape(rows, KVRANK + ROPE)
    inverse_latent = rms_inverse(latent_raw[:, :KVRANK])
    normed_latent = latent_raw[:, :KVRANK] * inverse_latent
    latent_low = (normed_latent * gain_latent).astype(bf16).reshape(seqs, piece, KVRANK)
    rotary_key = rotate(
        latent_raw[:, KVRANK:].reshape(seqs, piece, ROPE), cosine_here, sine_here
    ).astype(bf16)
    keys_here = jnp.concatenate(
        [latent_low, jnp.pad(rotary_key, ((0, 0), (0, 0), (NOPE, LANES - HEAD)))], axis=-1
    )
    half = seqs // 2
    mine = rank & 1
    keys_mine = lax.dynamic_slice_in_dim(keys_here, mine * half, half, 0)
    keys_mine = gather_ctx(keys_mine)
    keys_mine = keys_mine.transpose(1, 0, 2, 3).reshape(half, seq_len, KVRANK + LANES)
    keys_all = pair_order(keys_mine, tp_xor(keys_mine, 1), low_bit, 0)
    latent_all, rotary_all = keys_all[..., :KVRANK], keys_all[..., KVRANK:]

    grad_ffn = lax.all_gather(
        after((res_scale * own_chunk(grad_out)).astype(bf16), low_rank), ("ctx", "tp"), axis=0
    )
    grad_ffn_groups = []
    for shift in shifts():
        place = lax.rem(lax.axis_index("ctx") + shift, n_ctx) * n_tp
        grad_ffn_groups.append(
            jnp.concatenate(
                [
                    lax.dynamic_index_in_dim(grad_ffn, place + (rank ^ i), 0, False)
                    for i in (0, 2, 1, 3)
                ],
                axis=0,
            )
        )

    def hidden_rows(weight):
        return exchange_ctx(weight.reshape(n_ctx, -1, weight.shape[1]))

    gate_pieces, up_pieces = hidden_rows(gate_proj.T), hidden_rows(up_proj.T)
    down_pieces = hidden_rows(down_proj)

    down_all = gather_tp(after(down_part, keys_all))
    down_query = down_all[:, :, :q_part].transpose(1, 0, 2).reshape(width, QRANK)
    down_latent = down_all[:, :, q_part:].transpose(1, 0, 2).reshape(width, KVRANK + ROPE)

    inverse_query = rms_inverse(query_latent)
    normed_query = query_latent * inverse_query
    query_low = (normed_query * gain_query).astype(bf16)
    key_value = jnp.einsum("slr,rf->slf", latent_all, up_latent, preferred_element_type=f32)
    key_value = key_value.astype(bf16)
    query = dot(query_low, up_query, ((1,), (0,))).reshape(seqs, piece, -1)
    attended_low, log_total = attention_forward(
        query, key_value, rotary_all, table, limits.transpose(0, 2, 1), heads
    )
    attended_low = attended_low.reshape(rows, heads * VDIM)
    gate_full = gather_shard(join_columns(after(gate_pieces, attended_low)), 1)

    attn_out = scatter_tp(
        dot(attended_low, out_full, ((1,), (0,))).reshape(n_tp, chunk_rows, width)
    )
    upward_full = gather_shard(join_columns(after(up_pieces, attn_out)), 1)
    down_full = gather_shard(join_columns(after(down_pieces, attn_out)), 1)
    middle = own_chunk(stream) + res_scale * attn_out
    inverse_two = rms_inverse(middle)
    normed_two = middle * inverse_two
    ffn_groups = gather_tokens((normed_two * gain_ffn).astype(bf16))

    ffn_parts, grad_two_parts, kept = [], [], []
    for ffn_low, grad_low in zip(ffn_groups, grad_ffn_groups):
        gate_value = dot(ffn_low, gate_full, ((1,), (1,)))
        up_value = dot(ffn_low, upward_full, ((1,), (1,)))
        sigma = jax.nn.sigmoid(gate_value)
        gate_act = gate_value * sigma
        hidden_low = (gate_act * up_value).astype(bf16)
        grad_hidden = dot(grad_low, down_full, ((1,), (1,)))
        grad_gate = (grad_hidden * up_value * sigma * (1.0 + gate_value * (1.0 - sigma))).astype(
            bf16
        )
        grad_upward = (grad_hidden * gate_act).astype(bf16)
        grad_two_part = dot(grad_gate, gate_full, ((1,), (0,)))
        grad_two_part = grad_two_part + dot(grad_upward, upward_full, ((1,), (0,)))
        grad_two_parts.append(grad_two_part.astype(bf16))
        ffn_parts.append(dot(hidden_low, down_full, ((1,), (0,))).astype(bf16))
        kept.append((hidden_low.T, grad_gate.T, grad_upward.T))

    grad_two_parts = scatter_tp_groups(grad_two_parts)
    grad_down_w, grad_gate_w, grad_upward_w = ffn_weight_grads(
        [[group] for group in ffn_groups], [[group] for group in grad_ffn_groups], kept
    )
    grad_two = scatter_ctx_groups(grad_two_parts, grad_gate_w)
    ffn_parts = scatter_tp_groups(after(ffn_parts, grad_two_parts))
    grad_middle = own_chunk(grad_out) + norm_backward(grad_two, normed_two, inverse_two, gain_ffn)
    grad_gain_ffn = jnp.sum(grad_two * normed_two, axis=0)
    grad_attn = gather_tp((res_scale * grad_middle).astype(bf16)).reshape(rows, width)

    grad_out_w = lax.psum_scatter(
        dot(attended_low, grad_attn, ((0,), (0,))).astype(bf16),
        ("shard", "ctx"),
        scatter_dimension=1,
        tiled=True,
    ).astype(f32)

    grad_attended = dot(grad_attn, out_full, ((1,), (1,))).astype(bf16)
    grad_query, grad_key_value, grad_krope = attention_backward(
        query,
        key_value,
        rotary_all,
        table,
        limits,
        log_total,
        grad_attended.reshape(seqs, piece, -1),
        heads,
    )
    grad_query = grad_query.reshape(rows, heads * HEAD)
    grad_key_value = grad_key_value.reshape(seqs * seq_len, heads * (NOPE + VDIM))

    grad_keys = dot(grad_key_value, up_latent, ((1,), (1,))).astype(bf16)
    grad_keys = jnp.concatenate(
        [grad_keys.reshape(seqs, seq_len, KVRANK), grad_krope.astype(bf16)], axis=-1
    )

    def add_near(values):
        keep = lax.dynamic_slice_in_dim(values, mine * half, half, 0)
        send = lax.dynamic_slice_in_dim(values, (1 - mine) * half, half, 0)
        return keep.astype(f32) + tp_xor(send, 1).astype(f32)

    grad_keys = add_near(grad_keys).astype(bf16)
    grad_keys = scatter_ctx(
        grad_keys.reshape(half, n_ctx, piece, KVRANK + LANES).transpose(1, 0, 2, 3)
    )
    grad_pre_query = dot(grad_query, up_query, ((1,), (1,))).astype(bf16)
    grad_pre_query = add_near(grad_pre_query.reshape(seqs, piece, QRANK))
    grad_low = jnp.concatenate([grad_pre_query, grad_keys], axis=-1).astype(bf16)
    grad_low = (grad_low.astype(f32) + tp_xor(grad_low, 2).astype(f32)).astype(bf16)
    grad_low = pair_order(grad_low, tp_xor(grad_low, 1), low_bit, 0)
    grad_low = grad_low.reshape(rows, QRANK + KVRANK + LANES).astype(f32)

    grad_out_query, grad_out_latent = grad_low[:, :QRANK], grad_low[:, QRANK : QRANK + KVRANK]
    grad_query_latent = norm_backward(grad_out_query, normed_query, inverse_query, gain_query)
    grad_compressed = norm_backward(grad_out_latent, normed_latent, inverse_latent, gain_latent)
    grad_gain_query = jnp.sum(own_chunk(grad_out_query * normed_query), axis=0)
    grad_gain_latent = jnp.sum(own_chunk(grad_out_latent * normed_latent), axis=0)
    grad_rotary = grad_low[:, QRANK + KVRANK + NOPE : QRANK + KVRANK + HEAD]
    grad_rotary = grad_rotary.reshape(seqs, piece, ROPE)
    grad_rotary = unrotate(grad_rotary, cosine_here, sine_here).reshape(rows, ROPE)
    grad_query_latent = grad_query_latent.astype(bf16)
    grad_latent_raw = jnp.concatenate([grad_compressed, grad_rotary], axis=-1).astype(bf16)

    grad_pre_one = dot(own_chunk(grad_query_latent), down_query, ((1,), (1,)))
    grad_pre_one = grad_pre_one + dot(own_chunk(grad_latent_raw), down_latent, ((1,), (1,)))
    normed_own = own_chunk(normed_one)
    grad_input = grad_middle + norm_backward(
        grad_pre_one, normed_own, own_chunk(inverse_one), gain_attn
    )
    grad_gain_attn = jnp.sum(grad_pre_one * normed_own, axis=0)
    grad_input = gather_tp(round_low(grad_input).astype(bf16)).astype(f32)

    grad_part = jnp.concatenate(
        [
            lax.dynamic_slice_in_dim(grad_query_latent, rank * q_part, q_part, 1),
            lax.dynamic_slice_in_dim(grad_latent_raw, rank * kv_part, kv_part, 1),
        ],
        axis=1,
    )
    grad_small = dot(input_low, grad_part, ((0,), (0,)))
    grad_small = scatter_ctx(
        scatter_shard(grad_small, 0).reshape(n_ctx, n_tp, block, part)
    )
    grad_small = exchange_tp(grad_small.astype(bf16)).astype(f32).transpose(1, 0, 2)
    grad_down_query = grad_small[:, :, :q_part].reshape(block, QRANK)
    grad_down_latent = grad_small[:, :, q_part:].reshape(block, KVRANK + ROPE)
    grad_gains = jnp.concatenate(
        [
            grad_gain_attn.reshape(n_blocks, -1),
            grad_gain_ffn.reshape(n_blocks, -1),
            grad_gain_query.reshape(n_blocks, -1),
            grad_gain_latent.reshape(n_blocks, -1),
        ],
        axis=1,
    )
    grad_gains = lax.all_to_all(grad_gains[:, None], everywhere, 0, 0)
    grad_gains = jnp.sum(grad_gains[:, 0], axis=0)

    grad_down_w, grad_query, grad_key_value = lax.optimization_barrier(
        (grad_down_w, grad_query, grad_key_value, grad_keys)
    )[:3]
    output = round_low(middle + res_scale * scatter_ctx_groups(ffn_parts, grad_keys))
    output = gather_tp(output.astype(bf16)).astype(f32)

    def rows_grad(grad):
        mine = scatter_shard(grad, 0)
        return scatter_ctx(mine.reshape(n_ctx, -1, mine.shape[-1]))

    grad_up_query = rows_grad(dot(query_low, grad_query, ((0,), (0,))))
    grad_up_latent = rows_grad(
        dot(latent_all.reshape(-1, KVRANK), grad_key_value, ((0,), (0,)))
    )
    def hidden_grad(grad):
        length = grad.shape[1] // n_shard
        if n_shard == 2:
            other = 1 - lax.axis_index("shard")
            send = lax.dynamic_slice_in_dim(grad, other * length, length, 1)
            came = lax.ppermute(send, "shard", [(0, 1), (1, 0)])
            parts = add_and_split(grad, came, n_ctx)
        else:
            mine = scatter_shard(grad, 1).astype(bf16)
            parts = mine.reshape(mine.shape[0], n_ctx, -1).transpose(1, 0, 2)
        return parts

    grad_gate_w = exchange_ctx(hidden_grad(after(grad_gate_w, grad_attn)))
    grad_upward_w = exchange_ctx(hidden_grad(after(grad_upward_w, grad_attn)))
    grad_gate_w = place_rows(after(grad_gate_w, grad_low), True)
    grad_upward_w = place_rows(after(grad_upward_w, grad_low), True)
    grad_down_w = place_rows(exchange_ctx(hidden_grad(grad_down_w)), False)
    return (
        output.reshape(seqs, piece, width),
        grad_input.reshape(seqs, piece, width),
        grad_gains[:cut],
        grad_gains[2 * cut : 2 * cut + q_gain.shape[0]],
        grad_gains[2 * cut + q_gain.shape[0] :],
        grad_gains[cut : 2 * cut],
        grad_down_query,
        grad_down_latent,
        grad_up_query,
        grad_up_latent,
        grad_out_w,
        grad_gate_w,
        grad_upward_w,
        grad_down_w,
    )


def solution(mesh):
    all_axes = ("shard", "ctx", "tp")
    tokens, vector, square = P("shard", "ctx", None), P(all_axes), P(all_axes, None)
    inner, outer = P(("shard", "ctx"), "tp"), P("tp", ("shard", "ctx"))
    weights = (
        vector,
        vector,
        vector,
        vector,
        square,
        square,
        inner,
        inner,
        outer,
        inner,
        inner,
        outer,
    )
    return jax.shard_map(
        on_device,
        mesh=mesh,
        in_specs=(tokens, tokens, P("shard", None)) + weights,
        out_specs=(tokens, tokens) + weights,
        check_vma=False,
    )
```

time: 1280 us -> 1030 us (0.80)
  matrix products: 195 us -> 79.9 us
  waiting for transfers between devices: 474 us -> 370 us
  other arithmetic: 216 us -> 116 us
  local copies, waits for them, and re-layouts: 227 us -> 134 us
  starting transfers between devices: 149 us -> 239 us
  Pallas kernels: 0 us -> 61.9 us
  between operations: 3.8 us -> 17 us
    all_to_all x18 -> x2, waiting for transfers between devices: 187 us -> 0.01 us  [the longest x1 0.01 us: on_device(): lax.all_to_all(jnp.broadcast_to(gain_row[None, None], (n_blocks, 1, n_gai...]
    ppermute x6 -> x39, starting transfers between devices: 9.4 us -> 154 us  [the longest x30 115 us: exchange_ctx(): lax.ppermute(send, 'ctx', [(i, (i + shift) % size) for i in range(size)])]
    all_to_all x18 -> x2, starting transfers between devices: 93.2 us -> 9.55 us  [the longest x1 6.09 us: on_device(): lax.all_to_all(jnp.broadcast_to(gain_row[None, None], (n_blocks, 1, n_gai...]
    convert_element_type x48 -> x13, other arithmetic: 90.4 us -> 12.1 us  [the longest x3 2.89 us: scatter_ctx_groups(): group.astype(bf16)]
    dot_general x9 -> x0, matrix products: 72.1 us -> none  [the longest x1 15 us: masked_scores(): jnp.einsum('sqhd,skhd->shqk', query_nope, key_nope, preferred_element_typ...]
    unnamed x369 -> x281, local copies, waits for them, and re-layouts: 86.7 us -> 23 us
    pallas_call x0 -> x12, Pallas kernels: none -> 61.9 us  [the longest x1 23.1 us: attention_backward(): pl.pallas_call(functools.partial(backward_kernel, heads), grid=(seqs,), i...]
    ppermute x7 -> x6, waiting for transfers between devices: 10.5 us -> 56.5 us  [gather_shard(): other = lax.ppermute(values, 'shard', [(0, 1), (1, 0)])]
  transfers between devices with their start and end apart: 98 -> 119, of which waited for: 33 -> 40; matrix products, arithmetic and copies ran while one was open for 45% -> 26% of each run, Pallas kernels for 0% -> 6%
where the time goes in v2:
time: 1030 us; the launch traced here: 1020 us
  waiting for transfers between devices  370 us (36%)
  starting transfers between devices  239 us (23%)
  local copies, waits for them, and re-layouts  134 us (13%)
  other arithmetic  116 us (11%)
  matrix products  79.9 us (8%)
  Pallas kernels  61.9 us (6%)
  between operations  17 us (2%)
    ppermute x30, starting transfers between devices, exchange_ctx(): lax.ppermute(send, 'ctx', [(i, (i + shift) % size) for i in range(size)])  115 us
    ppermute x51, waiting for transfers between devices, tp_xor(): return lax.ppermute(values, 'tp', [(i, i ^ mask) for i in range(size)])  93.6 us
    ppermute x30, waiting for transfers between devices, exchange_ctx(): lax.ppermute(send, 'ctx', [(i, (i + shift) % size) for i in range(size)])  81.5 us
    dot_general x36, matrix products, dot(): lax.dot_general(left, right, (dims, ((), ())), preferred_element_type=f32)  76.2 us
    ppermute x15, waiting for transfers between devices, from_ctx(): lax.ppermute(values, 'ctx', [((i + shift) % size, i) for i in range(size)])  71.4 us
    ppermute x6, waiting for transfers between devices, gather_shard(): other = lax.ppermute(values, 'shard', [(0, 1), (1, 0)])  56.5 us
    ppermute x6, starting transfers between devices, scatter_ctx_groups(): lax.ppermute(group.astype(bf16), 'ctx', [(i, (i + shift) % size) for i in...  36.3 us
    ppermute x15, starting transfers between devices, from_ctx(): lax.ppermute(values, 'ctx', [((i + shift) % size, i) for i in range(size)])  34.1 us
  transfers between devices with their start and end apart: 119, of which 40 were waited for; matrix products, arithmetic and copies ran while one was open for 26% of the time, Pallas kernels for 6%

profile of v2, /device:TPU:0, one launch (start us, length us, event | category | flops | bytes accessed | tf_op | source)
XLA Modules:
  0.0 1017.9 jit_solution(7752981730759287840)
XLA Ops:
  14.1 6.1 all-to-all-start
  25.2 4.8 broadcast_multiply_fusion
  36.7 3.7 collective-permute-start.3
  43.0 4.1 dynamic_update_slice.81
  48.0 13.7 %collective-permute-done.4 = bf16[320,264]{1,0:T(8,128)(2,1)S(1)} collective-permute-done((bf16[320,264]{1,0:T(8,128)(2,1)S(1)}, bf16[320,264]{1,0:T(8,128)(2,1)S(1)}, u32[]{:S(2)}, u32[]{:S(2)}) %collective-permute-start.4) | collective-permute-done | bytes 168992 | tf_op jit(solution)/shard_map/ppermute | solution.py:74
  63.6 4.1 dynamic_update_slice.82
  67.7 4.1 dynamic_update_slice.83
  71.9 4.1 dynamic_update_slice.84
  99.4 14.0 %collective-permute-done.6 = bf16[1280,264]{0,1:T(8,128)(2,1)S(1)} collective-permute-done((bf16[1280,264]{0,1:T(8,128)(2,1)S(1)}, bf16[1280,264]{0,1:T(8,128)(2,1)S(1)}, u32[]{:S(2)}, u32[]{:S(2)}) %collective-permute-start.6) | collective-permute-done | bytes 675872 | tf_op jit(solution)/shard_map/ppermute | solution.py:118
  136.3 21.0 %collective-permute-done.12 = bf16[384,960]{0,1:T(8,128)(2,1)S(1)} collective-permute-done((bf16[384,960]{0,1:T(8,128)(2,1)}, bf16[384,960]{0,1:T(8,128)(2,1)S(1)}, u32[]{:S(2)}, u32[]{:S(2)}) %collective-permute-start.12) | collective-permute-done | bytes 737312 | tf_op jit(solution)/shard_map/ppermute | solution.py:118
  180.0 8.7 collective-permute-done.14
  200.4 3.8 convolution_convert_fusion.kv_ref
  204.1 14.4 %shard_map.254 = (bf16[2,256,640]{2,1,0:T(8,128)(2,1)S(1)}, f32[2,256,128]{2,1,0:T(8,128)S(1)}) custom-call(f32[2,256,960]{2,1,0:T(8,128)} %fusion.2.q_ref, bf16[2,1024,1280]{2,1,0:T(8,128)(2,1)} %convolution_convert_fusion.kv_ref, bf16[2,1024,128]{2,1,0:T(8,128)(2,1)S(1)} %fusion.60.rotary_ref, f32[3,256,128]{2,1,0:T(8,128)S(1)} %pad_maximum_fusion.26.table_ref, ...), custom_call_target="tpu_custom_call" | custom-call | flops 2684354560 | bytes 12000000 | tf_op jit(solution)/shard_map/pallas_call | solution.py:256
  218.6 4.7 fusion
  229.4 3.8 collective-permute-start.28
  235.6 9.6 collective-permute-done.26.refs_1_
  245.2 10.2 collective-permute-start.31
  255.3 10.7 %collective-permute-done.27.refs_2_ = bf16[400,320]{1,0:T(8,128)(2,1)S(1)} collective-permute-done((bf16[400,320]{1,0:T(8,128)(2,1)S(1)}, bf16[400,320]{1,0:T(8,128)(2,1)S(1)}, u32[]{:S(2)}, u32[]{:S(2)}) %collective-permute-start.27) | collective-permute-done | bytes 256032 | tf_op jit(solution)/shard_map/ppermute | solution.py:83
  270.7 21.5 %collective-permute-done.29 = bf16[400,1280]{1,0:T(8,128)(2,1)S(1)} collective-permute-done((bf16[400,1280]{1,0:T(8,128)(2,1)S(1)}, bf16[400,1280]{1,0:T(8,128)(2,1)S(1)}, u32[]{:S(2)}, u32[]{:S(2)}) %collective-permute-start.29) | collective-permute-done | bytes 1024032 | tf_op jit(solution)/shard_map/ppermute | solution.py:118
  292.2 27.3 %collective-permute-start.32 = (bf16[400,320]{1,0:T(8,128)(2,1)S(1)}, bf16[400,320]{1,0:T(8,128)(2,1)S(1)}, u32[]{:S(2)}, u32[]{:S(2)}) collective-permute-start(bf16[400,320]{1,0:T(8,128)(2,1)S(1)} %copy-done.99), channel_id=1, source_target_pairs={{0,12},{4,0},{8,4},{12,8},{1,13},{5,1},{9,5},{13,9},{2,14},{6,2},{... | collective-permute-start | bytes 768008 | tf_op jit(solution)/shard_map/ppermute | solution.py:83
  326.6 6.5 collective-permute-done.32.refs_3_
  335.1 8.3 collective-permute-start.42
  350.2 10.9 %collective-permute-done.38 = bf16[128,2560]{1,0:T(8,128)(2,1)S(1)} collective-permute-done((bf16[128,2560]{1,0:T(8,128)(2,1)S(1)}, bf16[128,2560]{1,0:T(8,128)(2,1)S(1)}, u32[]{:S(2)}, u32[]{:S(2)}) %collective-permute-start.38) | collective-permute-done | bytes 655392 | tf_op jit(solution)/shard_map/ppermute | solution.py:74
  362.4 12.3 %collective-permute-done.42 = bf16[128,2560]{1,0:T(8,128)(2,1)S(1)} collective-permute-done((bf16[128,2560]{1,0:T(8,128)(2,1)S(1)}, bf16[128,2560]{1,0:T(8,128)(2,1)S(1)}, u32[]{:S(2)}, u32[]{:S(2)}) %collective-permute-start.42) | collective-permute-done | bytes 655392 | tf_op jit(solution)/shard_map/ppermute | solution.py:74
  374.7 9.0 collective-permute-start.46
  386.9 25.8 %collective-permute-done.46 = bf16[128,2560]{1,0:T(8,128)(2,1)S(1)} collective-permute-done((bf16[128,2560]{1,0:T(8,128)(2,1)S(1)}, bf16[128,2560]{1,0:T(8,128)(2,1)S(1)}, u32[]{:S(2)}, u32[]{:S(2)}) %collective-permute-start.46) | collective-permute-done | bytes 655392 | tf_op jit(solution)/shard_map/ppermute | solution.py:74
  421.2 8.6 collective-permute-done.47
  445.9 5.9 dynamic-slice_bitcast_fusion.3
  489.1 16.9 %shard_map.258 = (bf16[400,2560]{1,0:T(8,128)(2,1)}, bf16[400,2560]{1,0:T(8,128)(2,1)}, bf16[400,2560]{1,0:T(8,128)(2,1)}) custom-call(bf16[512,2560]{1,0:T(8,128)(2,1)} %copy-done.58, bf16[512,2560]{1,0:T(8,128)(2,1)} %copy-done.103, bf16[512,2560]{1,0:T(8,128)(2,1)} %copy-done.104, bf16[512,2560]{1,0:T(8,128)(2,1)} %copy-done.105, ...), custom_call_target="tpu_custom_call" | custom-call | flops 12582912000 | bytes 33000000 | tf_op jit(solution)/shard_map/pallas_call | solution.py:360
  516.4 9.2 collective-permute-done.57
  525.7 5.7 collective-permute-start.71
  531.4 8.2 collective-permute-done.55
  540.8 12.9 %collective-permute-done.53 = bf16[128,2560]{1,0:T(8,128)(2,1)S(1)} collective-permute-done((bf16[128,2560]{1,0:T(8,128)(2,1)S(1)}, bf16[128,2560]{1,0:T(8,128)(2,1)S(1)}, u32[]{:S(2)}, u32[]{:S(2)}) %collective-permute-start.53) | collective-permute-done | bytes 655392 | tf_op jit(solution)/shard_map/ppermute | solution.py:69
  553.8 6.7 collective-permute-start.69
  560.5 6.7 collective-permute-done.51
  567.4 18.1 %collective-permute-done.70 = bf16[128,2560]{1,0:T(8,128)(2,1)S(1)} collective-permute-done((bf16[128,2560]{1,0:T(8,128)(2,1)S(1)}, bf16[128,2560]{1,0:T(8,128)(2,1)S(1)}, u32[]{:S(2)}, u32[]{:S(2)}) %collective-permute-start.70) | collective-permute-done | bytes 655392 | tf_op jit(solution)/shard_map/ppermute | solution.py:206
  617.3 7.9 collective-permute-done.67
  626.2 5.5 collective-permute-start.68
  631.7 7.5 collective-permute-done.64
  640.2 6.7 collective-permute-start.65
  646.9 6.4 collective-permute-done.61
  654.3 12.5 %collective-permute-done.59 = bf16[128,2560]{1,0:T(8,128)(2,1)S(1)} collective-permute-done((bf16[128,2560]{1,0:T(8,128)(2,1)S(1)}, bf16[128,2560]{1,0:T(8,128)(2,1)S(1)}, u32[]{:S(2)}, u32[]{:S(2)}) %collective-permute-start.59) | collective-permute-done | bytes 655392 | tf_op jit(solution)/shard_map/ppermute | solution.py:69
  673.4 23.1 %shard_map.259 = (bf16[2,256,960]{2,1,0:T(8,128)(2,1)}, bf16[2,1024,1280]{2,1,0:T(8,128)(2,1)}, f32[2,1024,128]{2,1,0:T(8,128)}) custom-call(f32[2,256,960]{2,1,0:T(8,128)} %fusion.2.q_ref, bf16[2,1024,1280]{2,1,0:T(8,128)(2,1)} %convolution_convert_fusion.kv_ref, bf16[2,1024,128]{2,1,0:T(8,128)(2,1)} %copy-done.4, f32[3,256,128]{2,1,0:T(8,128)} %copy-done.5, ...), custom_call_target="tpu_custom_call" | custom-call | flops 6710886400 | bytes 20000000 | tf_op jit(solution)/shard_map/pallas_call | solution.py:304
  696.6 4.1 convolution_convert_fusion.6
  705.9 4.0 convolution_convert_fusion.1
  712.7 3.7 collective-permute-start.75
  725.2 10.5 %collective-permute-start.62 = (bf16[128,2560]{1,0:T(8,128)(2,1)S(1)}, bf16[128,2560]{1,0:T(8,128)(2,1)S(1)}, u32[]{:S(2)}, u32[]{:S(2)}) collective-permute-start(bf16[128,2560]{1,0:T(8,128)(2,1)S(1)} %copy-done.97), channel_id=1, source_target_pairs={{0,4},{4,8},{8,12},{12,0},{1,5},{5,9},{9,13},{13,1},{2,6},{6,10},{... | collective-permute-start | bytes 1966088 | tf_op jit(solution)/shard_map/ppermute | solution.py:206
  735.6 10.5 %collective-permute-done.76 = bf16[1,256,384]{2,1,0:T(8,128)(2,1)S(1)} collective-permute-done((bf16[1,256,384]{2,1,0:T(8,128)(2,1)S(1)}, bf16[1,256,384]{2,1,0:T(8,128)(2,1)S(1)}, u32[]{:S(2)}, u32[]{:S(2)}) %collective-permute-start.76) | collective-permute-done | bytes 196640 | tf_op jit(solution)/shard_map/ppermute | solution.py:83
  748.3 4.2 fusion.148
  755.0 10.9 %collective-permute-done.62 = bf16[128,2560]{1,0:T(8,128)(2,1)S(1)} collective-permute-done((bf16[128,2560]{1,0:T(8,128)(2,1)S(1)}, bf16[128,2560]{1,0:T(8,128)(2,1)S(1)}, u32[]{:S(2)}, u32[]{:S(2)}) %collective-permute-start.62) | collective-permute-done | bytes 655392 | tf_op jit(solution)/shard_map/ppermute | solution.py:206
  767.2 8.9 collective-permute-done.106.came_ref
  777.5 6.1 collective-permute-start.107
  783.6 23.2 %collective-permute-done.102.came_ref = bf16[400,1280]{1,0:T(8,128)(2,1)S(1)} collective-permute-done((bf16[400,1280]{1,0:T(8,128)(2,1)S(1)}, bf16[400,1280]{1,0:T(8,128)(2,1)S(1)}, u32[]{:S(2)}, u32[]{:S(2)}) %collective-permute-start.102) | collective-permute-done | bytes 1024032 | tf_op jit(solution)/shard_map/ppermute | solution.py:755
  808.2 5.7 collective-permute-done.98
  818.1 9.7 collective-permute-done.100
  827.9 19.4 %collective-permute-start.103 = (bf16[400,320]{1,0:T(8,128)(2,1)}, bf16[400,320]{1,0:T(8,128)(2,1)S(1)}, u32[]{:S(2)}, u32[]{:S(2)}) collective-permute-start(bf16[400,320]{1,0:T(8,128)(2,1)} %get-tuple-element.283), channel_id=1, source_target_pairs={{0,4},{4,8},{8,12},{12,0},{1,5},{5,9},{9,13},{13,1},{2,6},{6,10},{... | collective-permute-start | bytes 768008 | tf_op jit(solution)/shard_map/ppermute | solution.py:83
  856.8 3.8 multiply_reduce_fusion.1
  873.8 3.9 reduce-precision_convert_fusion
  910.1 10.9 %collective-permute-done.112.refs_2_ = bf16[400,320]{1,0:T(8,128)(2,1)S(1)} collective-permute-done((bf16[400,320]{1,0:T(8,128)(2,1)}, bf16[400,320]{1,0:T(8,128)(2,1)S(1)}, u32[]{:S(2)}, u32[]{:S(2)}) %collective-permute-start.112) | collective-permute-done | bytes 256032 | tf_op jit(solution)/shard_map/ppermute | solution.py:83
  930.2 7.7 collective-permute-done.78
  949.7 5.3 collective-permute-start.88
  967.4 7.8 collective-permute-done.89
  978.7 5.6 collective-permute-start.95
  991.3 6.5 collective-permute-done.96
  (785 shorter events, 392.5 us)
Async XLA Ops:
  20.2 198.4 %all-gather.4.cloned.1.call-start = ((), (), s32[]{:S(2)}) async-start(), calls=%async_computation.3 | async-start | bytes 3686400 | tf_op jit(solution)/shard_map/all_gather | solution.py:520
  80.5 38.1 %collective-permute-start.9 = (bf16[96,960]{1,0:T(8,128)(2,1)}, bf16[96,960]{1,0:T(8,128)(2,1)}, u32[]{:S(2)}, u32[]{:S(2)}) collective-permute-start(bf16[96,960]{1,0:T(8,128)(2,1)} %param.24), channel_id=1, source_target_pairs={{4,0},{8,4},{12,8},{0,12},{5,1},{9,5},{13,9},{1,13},{6,2},{10,6},{... | collective-permute-start | bytes 552968 | tf_op jit(solution)/shard_map/ppermute | solution.py:74
  82.4 39.3 %collective-permute-start.10 = (bf16[96,960]{1,0:T(8,128)(2,1)}, bf16[96,960]{1,0:T(8,128)(2,1)}, u32[]{:S(2)}, u32[]{:S(2)}) collective-permute-start(bf16[96,960]{1,0:T(8,128)(2,1)} %param.24), channel_id=1, source_target_pairs={{8,0},{12,4},{0,8},{4,12},{9,1},{13,5},{1,9},{5,13},{10,2},{14,6},... | collective-permute-start | bytes 552968 | tf_op jit(solution)/shard_map/ppermute | solution.py:74
  86.4 359.6 %all-gather.6.cloned.1.call-start = ((), (), s32[]{:S(2)}) async-start(), calls=%async_computation.5 | async-start | bytes 11141120 | tf_op jit(solution)/shard_map/all_gather | solution.py:572
  92.4 31.0 %collective-permute-start.11 = (bf16[96,960]{1,0:T(8,128)(2,1)}, bf16[96,960]{1,0:T(8,128)(2,1)S(1)}, u32[]{:S(2)}, u32[]{:S(2)}) collective-permute-start(bf16[96,960]{1,0:T(8,128)(2,1)} %param.24), channel_id=1, source_target_pairs={{12,0},{0,4},{4,8},{8,12},{13,1},{1,5},{5,9},{9,13},{14,2},{2,6},{... | collective-permute-start | bytes 552968 | tf_op jit(solution)/shard_map/ppermute | solution.py:74
  96.4 226.1 %collective-permute-start.30 = (bf16[400,320]{1,0:T(8,128)(2,1)}, bf16[400,320]{1,0:T(8,128)(2,1)S(1)}, u32[]{:S(2)}, u32[]{:S(2)}) collective-permute-start(bf16[400,320]{1,0:T(8,128)(2,1)} %get-tuple-element.295), channel_id=1, source_target_pairs={{0,4},{4,8},{8,12},{12,0},{1,5},{5,9},{9,13},{13,1},{2,6},{6,10},{... | collective-permute-start | bytes 768008 | tf_op jit(solution)/shard_map/ppermute | solution.py:83
  126.3 31.0 %collective-permute-start.12 = (bf16[384,960]{0,1:T(8,128)(2,1)}, bf16[384,960]{0,1:T(8,128)(2,1)S(1)}, u32[]{:S(2)}, u32[]{:S(2)}) collective-permute-start(bf16[384,960]{0,1:T(8,128)(2,1)} %copy.243), channel_id=1, source_target_pairs={{0,16},{16,0},{1,17},{17,1},{2,18},{18,2},{3,19},{19,3},{4,20},{20... | collective-permute-start | bytes 2211848 | tf_op jit(solution)/shard_map/ppermute | solution.py:118
  131.6 26.9 %collective-permute-start.8 = (f32[2,512,264]{1,2,0:T(8,128)S(1)}, f32[2,512,264]{1,2,0:T(8,128)S(1)}, u32[]{:S(2)}, u32[]{:S(2)}) collective-permute-start(f32[2,512,264]{1,2,0:T(8,128)S(1)} %pad_maximum_fusion.19), channel_id=1, source_target_pairs={{0,1},{1,0},{2,3},{3,2},{4,5},{5,4},{6,7},{7,6},{8,9},{9,8},{10,11... | collective-permute-start | bytes 3244040 | tf_op jit(solution)/shard_map/ppermute | solution.py:69
  134.9 94.4 %collective-permute-start.83 = (bf16[2560,264]{0,1:T(8,128)(2,1)}, bf16[2560,264]{0,1:T(8,128)(2,1)}, u32[]{:S(2)}, u32[]{:S(2)}) collective-permute-start(bf16[2560,264]{0,1:T(8,128)(2,1)} %pad_maximum_fusion.14), channel_id=1, source_target_pairs={{0,2},{1,3},{2,0},{3,1},{4,6},{5,7},{6,4},{7,5},{8,10},{9,11},{10,... | collective-permute-start | bytes 4055048 | tf_op jit(solution)/shard_map/ppermute | solution.py:69
  178.0 831.1 %reduce-scatter.2.cloned.1.call-start = ((), (), s32[]{:S(2)}) async-start(), calls=%async_computation.4 | async-start | bytes 3686400 | tf_op jit(solution)/shard_map/reduce_scatter | solution.py:648
  224.7 42.9 %collective-permute-start.21 = (bf16[2,128,2560]{2,1,0:T(8,128)(2,1)}, bf16[2,128,2560]{2,1,0:T(8,128)(2,1)}, u32[]{:S(2)}, u32[]{:S(2)}) collective-permute-start(bf16[2,128,2560]{2,1,0:T(8,128)(2,1)} %fusion.5), channel_id=1, source_target_pairs={{0,1},{1,0},{2,3},{3,2},{4,5},{5,4},{6,7},{7,6},{8,9},{9,8},{10,11... | collective-permute-start | bytes 3932168 | tf_op jit(solution)/shard_map/ppermute | solution.py:69
  226.4 39.6 %collective-permute-start.27 = (bf16[400,320]{1,0:T(8,128)(2,1)S(1)}, bf16[400,320]{1,0:T(8,128)(2,1)S(1)}, u32[]{:S(2)}, u32[]{:S(2)}) collective-permute-start(bf16[400,320]{1,0:T(8,128)(2,1)S(1)} %get-tuple-element.290), channel_id=1, source_target_pairs={{0,8},{4,12},{8,0},{12,4},{1,9},{5,13},{9,1},{13,5},{2,10},{6,14},... | collective-permute-start | bytes 768008 | tf_op jit(solution)/shard_map/ppermute | solution.py:83
  229.4 37.8 %collective-permute-start.28 = (bf16[400,320]{1,0:T(8,128)(2,1)S(1)}, bf16[400,320]{1,0:T(8,128)(2,1)S(1)}, u32[]{:S(2)}, u32[]{:S(2)}) collective-permute-start(bf16[400,320]{1,0:T(8,128)(2,1)S(1)} %get-tuple-element.289), channel_id=1, source_target_pairs={{0,12},{4,0},{8,4},{12,8},{1,13},{5,1},{9,5},{13,9},{2,14},{6,2},{... | collective-permute-start | bytes 768008 | tf_op jit(solution)/shard_map/ppermute | solution.py:83
  245.2 79.1 %collective-permute-start.31 = (bf16[400,320]{1,0:T(8,128)(2,1)S(1)}, bf16[400,320]{1,0:T(8,128)(2,1)S(1)}, u32[]{:S(2)}, u32[]{:S(2)}) collective-permute-start(bf16[400,320]{1,0:T(8,128)(2,1)S(1)} %copy-done.100), channel_id=1, source_target_pairs={{0,8},{4,12},{8,0},{12,4},{1,9},{5,13},{9,1},{13,5},{2,10},{6,14},... | collective-permute-start | bytes 768008 | tf_op jit(solution)/shard_map/ppermute | solution.py:83
  266.1 77.3 %collective-permute-start.84 = (bf16[2,2560,264]{1,2,0:T(8,128)(2,1)S(1)}, bf16[2,2560,264]{1,2,0:T(8,128)(2,1)S(1)}, u32[]{:S(2)}, u32[]{:S(2)}) collective-permute-start(bf16[2,2560,264]{1,2,0:T(8,128)(2,1)S(1)} %pad_maximum_fusion.1), channel_id=1, source_target_pairs={{0,1},{1,0},{2,3},{3,2},{4,5},{5,4},{6,7},{7,6},{8,9},{9,8},{10,11... | collective-permute-start | bytes 8110088 | tf_op jit(solution)/shard_map/ppermute | solution.py:69
  269.8 49.9 %collective-permute-start.22 = (bf16[128,2560]{1,0:T(8,128)(2,1)S(1)}, bf16[128,2560]{1,0:T(8,128)(2,1)S(1)}, u32[]{:S(2)}, u32[]{:S(2)}) collective-permute-start(bf16[128,2560]{1,0:T(8,128)(2,1)S(1)} %fusion.57), channel_id=1, source_target_pairs={{0,2},{1,3},{2,0},{3,1},{4,6},{5,7},{6,4},{7,5},{8,10},{9,11},{10,... | collective-permute-start | bytes 1966088 | tf_op jit(solution)/shard_map/ppermute | solution.py:69
  292.2 40.8 %collective-permute-start.32 = (bf16[400,320]{1,0:T(8,128)(2,1)S(1)}, bf16[400,320]{1,0:T(8,128)(2,1)S(1)}, u32[]{:S(2)}, u32[]{:S(2)}) collective-permute-start(bf16[400,320]{1,0:T(8,128)(2,1)S(1)} %copy-done.99), channel_id=1, source_target_pairs={{0,12},{4,0},{8,4},{12,8},{1,13},{5,1},{9,5},{13,9},{2,14},{6,2},{... | collective-permute-start | bytes 768008 | tf_op jit(solution)/shard_map/ppermute | solution.py:83
  322.5 26.6 %collective-permute-start.35 = (bf16[400,320]{1,0:T(8,128)(2,1)S(1)}, bf16[400,320]{1,0:T(8,128)(2,1)S(1)}, u32[]{:S(2)}, u32[]{:S(2)}) collective-permute-start(bf16[400,320]{1,0:T(8,128)(2,1)S(1)} %get-tuple-element.286), channel_id=1, source_target_pairs={{0,8},{4,12},{8,0},{12,4},{1,9},{5,13},{9,1},{13,5},{2,10},{6,14},... | collective-permute-start | bytes 768008 | tf_op jit(solution)/shard_map/ppermute | solution.py:83
  333.0 28.1 %collective-permute-start.38 = (bf16[128,2560]{1,0:T(8,128)(2,1)S(1)}, bf16[128,2560]{1,0:T(8,128)(2,1)S(1)}, u32[]{:S(2)}, u32[]{:S(2)}) collective-permute-start(bf16[128,2560]{1,0:T(8,128)(2,1)S(1)} %multiply_convert_fusion.5), channel_id=1, source_target_pairs={{4,0},{8,4},{12,8},{0,12},{5,1},{9,5},{13,9},{1,13},{6,2},{10,6},{... | collective-permute-start | bytes 1966088 | tf_op jit(solution)/shard_map/ppermute | solution.py:74
  335.1 39.6 %collective-permute-start.42 = (bf16[128,2560]{1,0:T(8,128)(2,1)S(1)}, bf16[128,2560]{1,0:T(8,128)(2,1)S(1)}, u32[]{:S(2)}, u32[]{:S(2)}) collective-permute-start(bf16[128,2560]{1,0:T(8,128)(2,1)S(1)} %multiply_convert_fusion.5), channel_id=1, source_target_pairs={{12,0},{0,4},{4,8},{8,12},{13,1},{1,5},{5,9},{9,13},{14,2},{2,6},{... | collective-permute-start | bytes 1966088 | tf_op jit(solution)/shard_map/ppermute | solution.py:74
  343.4 41.5 %collective-permute-start.33 = (bf16[400,1280]{1,0:T(8,128)(2,1)S(1)}, bf16[400,1280]{1,0:T(8,128)(2,1)S(1)}, u32[]{:S(2)}, u32[]{:S(2)}) collective-permute-start(bf16[400,1280]{1,0:T(8,128)(2,1)S(1)} %shard_map.256), channel_id=1, source_target_pairs={{0,16},{16,0},{1,17},{17,1},{2,18},{18,2},{3,19},{19,3},{4,20},{20... | collective-permute-start | bytes 3072008 | tf_op jit(solution)/shard_map/ppermute | solution.py:118
  349.1 34.7 %collective-permute-start.23 = (bf16[128,2560]{1,0:T(8,128)(2,1)S(1)}, bf16[128,2560]{1,0:T(8,128)(2,1)S(1)}, u32[]{:S(2)}, u32[]{:S(2)}) collective-permute-start(bf16[128,2560]{1,0:T(8,128)(2,1)S(1)} %multiply_convert_fusion.5), channel_id=1, source_target_pairs={{0,2},{1,3},{2,0},{3,1},{4,6},{5,7},{6,4},{7,5},{8,10},{9,11},{10,... | collective-permute-start | bytes 1966088 | tf_op jit(solution)/shard_map/ppermute | solution.py:69
  349.9 35.9 %collective-permute-start.24 = (bf16[128,2560]{1,0:T(8,128)(2,1)S(1)}, bf16[128,2560]{1,0:T(8,128)(2,1)S(1)}, u32[]{:S(2)}, u32[]{:S(2)}) collective-permute-start(bf16[128,2560]{1,0:T(8,128)(2,1)S(1)} %multiply_convert_fusion.5), channel_id=1, source_target_pairs={{0,1},{1,0},{2,3},{3,2},{4,5},{5,4},{6,7},{7,6},{8,9},{9,8},{10,11... | collective-permute-start | bytes 1966088 | tf_op jit(solution)/shard_map/ppermute | solution.py:69
  374.7 37.9 %collective-permute-start.46 = (bf16[128,2560]{1,0:T(8,128)(2,1)S(1)}, bf16[128,2560]{1,0:T(8,128)(2,1)S(1)}, u32[]{:S(2)}, u32[]{:S(2)}) collective-permute-start(bf16[128,2560]{1,0:T(8,128)(2,1)S(1)} %multiply_convert_fusion.5), channel_id=1, source_target_pairs={{8,0},{12,4},{0,8},{4,12},{9,1},{13,5},{1,9},{5,13},{10,2},{14,6},... | collective-permute-start | bytes 1966088 | tf_op jit(solution)/shard_map/ppermute | solution.py:74
  383.8 36.2 %collective-permute-start.43 = (bf16[128,2560]{1,0:T(8,128)(2,1)S(1)}, bf16[128,2560]{1,0:T(8,128)(2,1)S(1)}, u32[]{:S(2)}, u32[]{:S(2)}) collective-permute-start(bf16[128,2560]{1,0:T(8,128)(2,1)S(1)} %collective-permute-done.42), channel_id=1, source_target_pairs={{0,2},{1,3},{2,0},{3,1},{4,6},{5,7},{6,4},{7,5},{8,10},{9,11},{10,... | collective-permute-start | bytes 1966088 | tf_op jit(solution)/shard_map/ppermute | solution.py:69
  384.9 27.7 %collective-permute-start.25 = (bf16[128,2560]{1,0:T(8,128)(2,1)S(1)}, bf16[128,2560]{1,0:T(8,128)(2,1)S(1)}, u32[]{:S(2)}, u32[]{:S(2)}) collective-permute-start(bf16[128,2560]{1,0:T(8,128)(2,1)S(1)} %collective-permute-done.23), channel_id=1, source_target_pairs={{0,1},{1,0},{2,3},{3,2},{4,5},{5,4},{6,7},{7,6},{8,9},{9,8},{10,11... | collective-permute-start | bytes 1966088 | tf_op jit(solution)/shard_map/ppermute | solution.py:69
  385.1 35.7 %collective-permute-start.44 = (bf16[128,2560]{1,0:T(8,128)(2,1)S(1)}, bf16[128,2560]{1,0:T(8,128)(2,1)S(1)}, u32[]{:S(2)}, u32[]{:S(2)}) collective-permute-start(bf16[128,2560]{1,0:T(8,128)(2,1)S(1)} %collective-permute-done.42), channel_id=1, source_target_pairs={{0,1},{1,0},{2,3},{3,2},{4,5},{5,4},{6,7},{7,6},{8,9},{9,8},{10,11... | collective-permute-start | bytes 1966088 | tf_op jit(solution)/shard_map/ppermute | solution.py:69
  385.8 34.6 %collective-permute-start.39 = (bf16[128,2560]{1,0:T(8,128)(2,1)S(1)}, bf16[128,2560]{1,0:T(8,128)(2,1)S(1)}, u32[]{:S(2)}, u32[]{:S(2)}) collective-permute-start(bf16[128,2560]{1,0:T(8,128)(2,1)S(1)} %collective-permute-done.38), channel_id=1, source_target_pairs={{0,2},{1,3},{2,0},{3,1},{4,6},{5,7},{6,4},{7,5},{8,10},{9,11},{10,... | collective-permute-start | bytes 1966088 | tf_op jit(solution)/shard_map/ppermute | solution.py:69
  472.5 33.4 %collective-permute-start.56 = (bf16[256,2560]{1,0:T(8,128)(2,1)}, bf16[256,2560]{1,0:T(8,128)(2,1)}, u32[]{:S(2)}, u32[]{:S(2)}) collective-permute-start(bf16[256,2560]{1,0:T(8,128)(2,1)} %slice.366), channel_id=1, source_target_pairs={{0,1},{1,0},{2,3},{3,2},{4,5},{5,4},{6,7},{7,6},{8,9},{9,8},{10,11... | collective-permute-start | bytes 3932168 | tf_op jit(solution)/shard_map/ppermute | solution.py:69
  478.0 31.1 %collective-permute-start.54 = (bf16[256,2560]{1,0:T(8,128)(2,1)}, bf16[256,2560]{1,0:T(8,128)(2,1)}, u32[]{:S(2)}, u32[]{:S(2)}) collective-permute-start(bf16[256,2560]{1,0:T(8,128)(2,1)} %slice.362), channel_id=1, source_target_pairs={{0,1},{1,0},{2,3},{3,2},{4,5},{5,4},{6,7},{7,6},{8,9},{9,8},{10,11... | collective-permute-start | bytes 3932168 | tf_op jit(solution)/shard_map/ppermute | solution.py:69
  483.3 28.6 %collective-permute-start.52 = (bf16[256,2560]{1,0:T(8,128)(2,1)}, bf16[256,2560]{1,0:T(8,128)(2,1)}, u32[]{:S(2)}, u32[]{:S(2)}) collective-permute-start(bf16[256,2560]{1,0:T(8,128)(2,1)} %slice.358), channel_id=1, source_target_pairs={{0,1},{1,0},{2,3},{3,2},{4,5},{5,4},{6,7},{7,6},{8,9},{9,8},{10,11... | collective-permute-start | bytes 3932168 | tf_op jit(solution)/shard_map/ppermute | solution.py:69
  510.9 28.7 %collective-permute-start.55 = (bf16[128,2560]{1,0:T(8,128)(2,1)S(1)}, bf16[128,2560]{1,0:T(8,128)(2,1)S(1)}, u32[]{:S(2)}, u32[]{:S(2)}) collective-permute-start(bf16[128,2560]{1,0:T(8,128)(2,1)S(1)} %slice.480), channel_id=1, source_target_pairs={{0,2},{1,3},{2,0},{3,1},{4,6},{5,7},{6,4},{7,5},{8,10},{9,11},{10,... | collective-permute-start | bytes 1966088 | tf_op jit(solution)/shard_map/ppermute | solution.py:69
  513.7 39.9 %collective-permute-start.53 = (bf16[128,2560]{1,0:T(8,128)(2,1)S(1)}, bf16[128,2560]{1,0:T(8,128)(2,1)S(1)}, u32[]{:S(2)}, u32[]{:S(2)}) collective-permute-start(bf16[128,2560]{1,0:T(8,128)(2,1)S(1)} %slice.481), channel_id=1, source_target_pairs={{0,2},{1,3},{2,0},{3,1},{4,6},{5,7},{6,4},{7,5},{8,10},{9,11},{10,... | collective-permute-start | bytes 1966088 | tf_op jit(solution)/shard_map/ppermute | solution.py:69
  515.4 51.9 %collective-permute-start.51 = (bf16[128,2560]{1,0:T(8,128)(2,1)S(1)}, bf16[128,2560]{1,0:T(8,128)(2,1)S(1)}, u32[]{:S(2)}, u32[]{:S(2)}) collective-permute-start(bf16[128,2560]{1,0:T(8,128)(2,1)S(1)} %slice.482), channel_id=1, source_target_pairs={{0,2},{1,3},{2,0},{3,1},{4,6},{5,7},{6,4},{7,5},{8,10},{9,11},{10,... | collective-permute-start | bytes 1966088 | tf_op jit(solution)/shard_map/ppermute | solution.py:69
  525.7 41.7 %collective-permute-start.71 = (bf16[128,2560]{1,0:T(8,128)(2,1)S(1)}, bf16[128,2560]{1,0:T(8,128)(2,1)S(1)}, u32[]{:S(2)}, u32[]{:S(2)}) collective-permute-start(bf16[128,2560]{1,0:T(8,128)(2,1)S(1)} %slice_add_fusion.4), channel_id=1, source_target_pairs={{0,8},{4,12},{8,0},{12,4},{1,9},{5,13},{9,1},{13,5},{2,10},{6,14},... | collective-permute-start | bytes 1966088 | tf_op jit(solution)/shard_map/ppermute | solution.py:206
  539.7 45.8 %collective-permute-start.70 = (bf16[128,2560]{1,0:T(8,128)(2,1)S(1)}, bf16[128,2560]{1,0:T(8,128)(2,1)S(1)}, u32[]{:S(2)}, u32[]{:S(2)}) collective-permute-start(bf16[128,2560]{1,0:T(8,128)(2,1)S(1)} %slice_add_fusion.5), channel_id=1, source_target_pairs={{0,12},{4,0},{8,4},{12,8},{1,13},{5,1},{9,5},{13,9},{2,14},{6,2},{... | collective-permute-start | bytes 1966088 | tf_op jit(solution)/shard_map/ppermute | solution.py:206
  553.8 31.7 %collective-permute-start.69 = (bf16[128,2560]{1,0:T(8,128)(2,1)S(1)}, bf16[128,2560]{1,0:T(8,128)(2,1)S(1)}, u32[]{:S(2)}, u32[]{:S(2)}) collective-permute-start(bf16[128,2560]{1,0:T(8,128)(2,1)S(1)} %slice_add_fusion.6), channel_id=1, source_target_pairs={{0,4},{4,8},{8,12},{12,0},{1,5},{5,9},{9,13},{13,1},{2,6},{6,10},{... | collective-permute-start | bytes 1966088 | tf_op jit(solution)/shard_map/ppermute | solution.py:206
  605.5 62.5 %collective-permute-start.73 = (bf16[2,128,2560]{2,1,0:T(8,128)(2,1)S(1)}, bf16[2,128,2560]{2,1,0:T(8,128)(2,1)S(1)}, u32[]{:S(2)}, u32[]{:S(2)}) collective-permute-start(bf16[2,128,2560]{2,1,0:T(8,128)(2,1)S(1)} %pad_maximum_fusion.15), channel_id=1, source_target_pairs={{0,1},{1,0},{2,3},{3,2},{4,5},{5,4},{6,7},{7,6},{8,9},{9,8},{10,11... | collective-permute-start | bytes 3932168 | tf_op jit(solution)/shard_map/ppermute | solution.py:69
  610.7 28.6 %collective-permute-start.64 = (bf16[128,2560]{1,0:T(8,128)(2,1)S(1)}, bf16[128,2560]{1,0:T(8,128)(2,1)S(1)}, u32[]{:S(2)}, u32[]{:S(2)}) collective-permute-start(bf16[128,2560]{1,0:T(8,128)(2,1)S(1)} %slice.476), channel_id=1, source_target_pairs={{0,2},{1,3},{2,0},{3,1},{4,6},{5,7},{6,4},{7,5},{8,10},{9,11},{10,... | collective-permute-start | bytes 1966088 | tf_op jit(solution)/shard_map/ppermute | solution.py:69
  613.4 39.9 %collective-permute-start.61 = (bf16[128,2560]{1,0:T(8,128)(2,1)S(1)}, bf16[128,2560]{1,0:T(8,128)(2,1)S(1)}, u32[]{:S(2)}, u32[]{:S(2)}) collective-permute-start(bf16[128,2560]{1,0:T(8,128)(2,1)S(1)} %slice.477), channel_id=1, source_target_pairs={{0,2},{1,3},{2,0},{3,1},{4,6},{5,7},{6,4},{7,5},{8,10},{9,11},{10,... | collective-permute-start | bytes 1966088 | tf_op jit(solution)/shard_map/ppermute | solution.py:69
  616.4 50.3 %collective-permute-start.59 = (bf16[128,2560]{1,0:T(8,128)(2,1)S(1)}, bf16[128,2560]{1,0:T(8,128)(2,1)S(1)}, u32[]{:S(2)}, u32[]{:S(2)}) collective-permute-start(bf16[128,2560]{1,0:T(8,128)(2,1)S(1)} %slice.478), channel_id=1, source_target_pairs={{0,2},{1,3},{2,0},{3,1},{4,6},{5,7},{6,4},{7,5},{8,10},{9,11},{10,... | collective-permute-start | bytes 1966088 | tf_op jit(solution)/shard_map/ppermute | solution.py:69
  626.2 126.5 %collective-permute-start.68 = (bf16[128,2560]{1,0:T(8,128)(2,1)}, bf16[128,2560]{1,0:T(8,128)(2,1)}, u32[]{:S(2)}, u32[]{:S(2)}) collective-permute-start(bf16[128,2560]{1,0:T(8,128)(2,1)} %fusion.6), channel_id=1, source_target_pairs={{0,8},{4,12},{8,0},{12,4},{1,9},{5,13},{9,1},{13,5},{2,10},{6,14},... | collective-permute-start | bytes 1966088 | tf_op jit(solution)/shard_map/ppermute | solution.py:206
  640.2 113.8 %collective-permute-start.65 = (bf16[128,2560]{1,0:T(8,128)(2,1)}, bf16[128,2560]{1,0:T(8,128)(2,1)}, u32[]{:S(2)}, u32[]{:S(2)}) collective-permute-start(bf16[128,2560]{1,0:T(8,128)(2,1)} %fusion.7), channel_id=1, source_target_pairs={{0,12},{4,0},{8,4},{12,8},{1,13},{5,1},{9,5},{13,9},{2,14},{6,2},{... | collective-permute-start | bytes 1966088 | tf_op jit(solution)/shard_map/ppermute | solution.py:206
  716.4 29.7 %collective-permute-start.76 = (bf16[1,256,384]{2,1,0:T(8,128)(2,1)S(1)}, bf16[1,256,384]{2,1,0:T(8,128)(2,1)S(1)}, u32[]{:S(2)}, u32[]{:S(2)}) collective-permute-start(bf16[1,256,384]{2,1,0:T(8,128)(2,1)S(1)} %get-tuple-element.308), channel_id=1, source_target_pairs={{0,8},{4,12},{8,0},{12,4},{1,9},{5,13},{9,1},{13,5},{2,10},{6,14},... | collective-permute-start | bytes 589832 | tf_op jit(solution)/shard_map/ppermute | solution.py:83
  719.9 27.4 %collective-permute-start.77 = (bf16[1,256,384]{2,1,0:T(8,128)(2,1)S(1)}, bf16[1,256,384]{2,1,0:T(8,128)(2,1)S(1)}, u32[]{:S(2)}, u32[]{:S(2)}) collective-permute-start(bf16[1,256,384]{2,1,0:T(8,128)(2,1)S(1)} %get-tuple-element.309), channel_id=1, source_target_pairs={{0,12},{4,0},{8,4},{12,8},{1,13},{5,1},{9,5},{13,9},{2,14},{6,2},{... | collective-permute-start | bytes 589832 | tf_op jit(solution)/shard_map/ppermute | solution.py:83
  725.2 40.7 %collective-permute-start.62 = (bf16[128,2560]{1,0:T(8,128)(2,1)S(1)}, bf16[128,2560]{1,0:T(8,128)(2,1)S(1)}, u32[]{:S(2)}, u32[]{:S(2)}) collective-permute-start(bf16[128,2560]{1,0:T(8,128)(2,1)S(1)} %copy-done.97), channel_id=1, source_target_pairs={{0,4},{4,8},{8,12},{12,0},{1,5},{5,9},{9,13},{13,1},{2,6},{6,10},{... | collective-permute-start | bytes 1966088 | tf_op jit(solution)/shard_map/ppermute | solution.py:206
  746.2 30.0 %collective-permute-start.106 = (bf16[400,1280]{1,0:T(8,128)(2,1)S(1)}, bf16[400,1280]{1,0:T(8,128)(2,1)S(1)}, u32[]{:S(2)}, u32[]{:S(2)}) collective-permute-start(bf16[400,1280]{1,0:T(8,128)(2,1)S(1)} %copy-done.68), channel_id=1, source_target_pairs={{0,16},{16,0},{1,17},{17,1},{2,18},{18,2},{3,19},{19,3},{4,20},{20... | collective-permute-start | bytes 3072008 | tf_op jit(solution)/shard_map/ppermute | solution.py:755
  747.3 59.5 %collective-permute-start.102 = (bf16[400,1280]{1,0:T(8,128)(2,1)S(1)}, bf16[400,1280]{1,0:T(8,128)(2,1)S(1)}, u32[]{:S(2)}, u32[]{:S(2)}) collective-permute-start(bf16[400,1280]{1,0:T(8,128)(2,1)S(1)} %copy-done.67), channel_id=1, source_target_pairs={{0,16},{16,0},{1,17},{17,1},{2,18},{18,2},{3,19},{19,3},{4,20},{20... | collective-permute-start | bytes 3072008 | tf_op jit(solution)/shard_map/ppermute | solution.py:755
  752.7 61.1 %collective-permute-start.98 = (bf16[128,1280]{1,0:T(8,128)(2,1)S(1)}, bf16[128,1280]{1,0:T(8,128)(2,1)S(1)}, u32[]{:S(2)}, u32[]{:S(2)}) collective-permute-start(bf16[128,1280]{1,0:T(8,128)(2,1)S(1)} %select_convert_fusion.4), channel_id=1, source_target_pairs={{0,16},{16,0},{1,17},{17,1},{2,18},{18,2},{3,19},{19,3},{4,20},{20... | collective-permute-start | bytes 983048 | tf_op jit(solution)/shard_map/ppermute | solution.py:132
  754.0 93.9 %collective-permute-start.110 = (bf16[400,1280]{1,0:T(8,128)(2,1)S(1)}, bf16[400,1280]{1,0:T(8,128)(2,1)S(1)}, u32[]{:S(2)}, u32[]{:S(2)}) collective-permute-start(bf16[400,1280]{1,0:T(8,128)(2,1)S(1)} %constant_dynamic-slice_fusion), channel_id=1, source_target_pairs={{0,16},{16,0},{1,17},{17,1},{2,18},{18,2},{3,19},{19,3},{4,20},{20... | collective-permute-start | bytes 3072008 | tf_op jit(solution)/shard_map/ppermute | solution.py:755
  765.9 51.6 %collective-permute-start.81 = (bf16[1,256,1152]{2,1,0:T(8,128)(2,1)S(1)}, bf16[1,256,1152]{2,1,0:T(8,128)(2,1)S(1)}, u32[]{:S(2)}, u32[]{:S(2)}) collective-permute-start(bf16[1,256,1152]{2,1,0:T(8,128)(2,1)S(1)} %pad_maximum_fusion.23), channel_id=1, source_target_pairs={{0,2},{1,3},{2,0},{3,1},{4,6},{5,7},{6,4},{7,5},{8,10},{9,11},{10,... | collective-permute-start | bytes 1769480 | tf_op jit(solution)/shard_map/ppermute | solution.py:69
  777.5 101.2 %collective-permute-start.107 = (bf16[400,320]{1,0:T(8,128)(2,1)}, bf16[400,320]{1,0:T(8,128)(2,1)S(1)}, u32[]{:S(2)}, u32[]{:S(2)}) collective-permute-start(bf16[400,320]{1,0:T(8,128)(2,1)} %get-tuple-element.279), channel_id=1, source_target_pairs={{0,4},{4,8},{8,12},{12,0},{1,5},{5,9},{9,13},{13,1},{2,6},{6,10},{... | collective-permute-start | bytes 768008 | tf_op jit(solution)/shard_map/ppermute | solution.py:83
  817.4 29.8 %collective-permute-start.99 = (bf16[32,1280]{1,0:T(8,128)(2,1)S(1)}, bf16[32,1280]{1,0:T(8,128)(2,1)S(1)}, u32[]{:S(2)}, u32[]{:S(2)}) collective-permute-start(bf16[32,1280]{1,0:T(8,128)(2,1)S(1)} %get-tuple-element.312), channel_id=1, source_target_pairs={{0,4},{4,8},{8,12},{12,0},{1,5},{5,9},{9,13},{13,1},{2,6},{6,10},{... | collective-permute-start | bytes 245768 | tf_op jit(solution)/shard_map/ppermute | solution.py:83
  827.8 61.6 %collective-permute-start.108 = (bf16[400,320]{1,0:T(8,128)(2,1)S(1)}, bf16[400,320]{1,0:T(8,128)(2,1)S(1)}, u32[]{:S(2)}, u32[]{:S(2)}) collective-permute-start(bf16[400,320]{1,0:T(8,128)(2,1)S(1)} %get-tuple-element.278), channel_id=1, source_target_pairs={{0,8},{4,12},{8,0},{12,4},{1,9},{5,13},{9,1},{13,5},{2,10},{6,14},... | collective-permute-start | bytes 768008 | tf_op jit(solution)/shard_map/ppermute | solution.py:83
  827.9 65.3 %collective-permute-start.103 = (bf16[400,320]{1,0:T(8,128)(2,1)}, bf16[400,320]{1,0:T(8,128)(2,1)S(1)}, u32[]{:S(2)}, u32[]{:S(2)}) collective-permute-start(bf16[400,320]{1,0:T(8,128)(2,1)} %get-tuple-element.283), channel_id=1, source_target_pairs={{0,4},{4,8},{8,12},{12,0},{1,5},{5,9},{9,13},{13,1},{2,6},{6,10},{... | collective-permute-start | bytes 768008 | tf_op jit(solution)/shard_map/ppermute | solution.py:83
  847.9 45.2 %collective-permute-start.104 = (bf16[400,320]{1,0:T(8,128)(2,1)}, bf16[400,320]{1,0:T(8,128)(2,1)S(1)}, u32[]{:S(2)}, u32[]{:S(2)}) collective-permute-start(bf16[400,320]{1,0:T(8,128)(2,1)} %get-tuple-element.282), channel_id=1, source_target_pairs={{0,8},{4,12},{8,0},{12,4},{1,9},{5,13},{9,1},{13,5},{2,10},{6,14},... | collective-permute-start | bytes 768008 | tf_op jit(solution)/shard_map/ppermute | solution.py:83
  849.3 44.9 %collective-permute-start.105 = (bf16[400,320]{1,0:T(8,128)(2,1)}, bf16[400,320]{1,0:T(8,128)(2,1)S(1)}, u32[]{:S(2)}, u32[]{:S(2)}) collective-permute-start(bf16[400,320]{1,0:T(8,128)(2,1)} %get-tuple-element.281), channel_id=1, source_target_pairs={{0,12},{4,0},{8,4},{12,8},{1,13},{5,1},{9,5},{13,9},{2,14},{6,2},{... | collective-permute-start | bytes 768008 | tf_op jit(solution)/shard_map/ppermute | solution.py:83
  878.7 48.6 %collective-permute-start.85 = (bf16[128,2560]{1,0:T(8,128)(2,1)}, bf16[128,2560]{1,0:T(8,128)(2,1)}, u32[]{:S(2)}, u32[]{:S(2)}) collective-permute-start(bf16[128,2560]{1,0:T(8,128)(2,1)} %get-tuple-element.267), channel_id=1, source_target_pairs={{0,2},{1,3},{2,0},{3,1},{4,6},{5,7},{6,4},{7,5},{8,10},{9,11},{10,... | collective-permute-start | bytes 1966088 | tf_op jit(solution)/shard_map/ppermute | solution.py:69
  893.1 27.8 %collective-permute-start.112 = (bf16[400,320]{1,0:T(8,128)(2,1)}, bf16[400,320]{1,0:T(8,128)(2,1)S(1)}, u32[]{:S(2)}, u32[]{:S(2)}) collective-permute-start(bf16[400,320]{1,0:T(8,128)(2,1)} %get-tuple-element.274), channel_id=1, source_target_pairs={{0,8},{4,12},{8,0},{12,4},{1,9},{5,13},{9,1},{13,5},{2,10},{6,14},... | collective-permute-start | bytes 768008 | tf_op jit(solution)/shard_map/ppermute | solution.py:83
  894.2 28.9 %collective-permute-start.113 = (bf16[400,320]{1,0:T(8,128)(2,1)}, bf16[400,320]{1,0:T(8,128)(2,1)}, u32[]{:S(2)}, u32[]{:S(2)}) collective-permute-start(bf16[400,320]{1,0:T(8,128)(2,1)} %get-tuple-element.273), channel_id=1, source_target_pairs={{0,12},{4,0},{8,4},{12,8},{1,13},{5,1},{9,5},{13,9},{2,14},{6,2},{... | collective-permute-start | bytes 768008 | tf_op jit(solution)/shard_map/ppermute | solution.py:83
  901.1 61.1 %collective-permute-start.94 = (bf16[384,960]{0,1:T(8,128)(2,1)}, bf16[384,960]{0,1:T(8,128)(2,1)}, u32[]{:S(2)}, u32[]{:S(2)}) collective-permute-start(bf16[384,960]{0,1:T(8,128)(2,1)} %select_convert_fusion.1), channel_id=1, source_target_pairs={{0,16},{16,0},{1,17},{17,1},{2,18},{18,2},{3,19},{19,3},{4,20},{20... | collective-permute-start | bytes 2211848 | tf_op jit(solution)/shard_map/ppermute | solution.py:132
  908.8 32.3 %collective-permute-start.87 = (bf16[1280,264]{0,1:T(8,128)(2,1)}, bf16[1280,264]{0,1:T(8,128)(2,1)}, u32[]{:S(2)}, u32[]{:S(2)}) collective-permute-start(bf16[1280,264]{0,1:T(8,128)(2,1)} %select_convert_fusion.2), channel_id=1, source_target_pairs={{0,16},{16,0},{1,17},{17,1},{2,18},{18,2},{3,19},{19,3},{4,20},{20... | collective-permute-start | bytes 2027528 | tf_op jit(solution)/shard_map/ppermute | solution.py:132
  930.0 69.8 %collective-permute-start.86 = (bf16[2,128,2560]{2,1,0:T(8,128)(2,1)}, bf16[2,128,2560]{2,1,0:T(8,128)(2,1)}, u32[]{:S(2)}, u32[]{:S(2)}) collective-permute-start(bf16[2,128,2560]{2,1,0:T(8,128)(2,1)} %pad_maximum_fusion.17), channel_id=1, source_target_pairs={{0,1},{1,0},{2,3},{3,2},{4,5},{5,4},{6,7},{7,6},{8,9},{9,8},{10,11... | collective-permute-start | bytes 3932168 | tf_op jit(solution)/shard_map/ppermute | solution.py:69
  941.1 63.3 %collective-permute-start.79 = (bf16[2,128,2560]{2,1,0:T(8,128)(2,1)}, bf16[2,128,2560]{2,1,0:T(8,128)(2,1)}, u32[]{:S(2)}, u32[]{:S(2)}) collective-permute-start(bf16[2,128,2560]{2,1,0:T(8,128)(2,1)} %pad_maximum_fusion.16), channel_id=1, source_target_pairs={{0,1},{1,0},{2,3},{3,2},{4,5},{5,4},{6,7},{7,6},{8,9},{9,8},{10,11... | collective-permute-start | bytes 3932168 | tf_op jit(solution)/shard_map/ppermute | solution.py:69
  (186 other events, 2792.0 us)
Sparse Core Ops, SparseCore 0:
  86.5 92.0 all-gather.3
  180.9 124.1 all-gather.5
  711.1 140.7 reduce-scatter.1

commit v3 on v2

--- a/solution.py
+++ b/solution.py
@@ -153,7 +153,7 @@
     return both.reshape((4,) + chunk.shape)
 
 
-def scatter_tp(partial_sum):
+def scatter_tp(partial_sum, *earlier):
     rank = lax.axis_index("tp")
     low_bit, high_bit = (rank & 1) == 1, (rank >> 1) == 1
     parts = partial_sum.reshape((2, 2) + partial_sum.shape[1:])
@@ -162,54 +162,88 @@
     summed = keep + tp_xor(send, 1).astype(f32)
     keep = jnp.where(high_bit, summed[1], summed[0])
     send = jnp.where(high_bit, summed[0], summed[1]).astype(bf16)
+    if earlier:
+        send = after(send, *earlier)
     return keep + tp_xor(send, 2).astype(f32)
 
 
-def after(values, earlier):
-    return lax.optimization_barrier((values, earlier))[0]
-
-
-def shifts():
-    size = lax.axis_size("ctx")
-    return sorted(range(size), key=lambda shift: (min(shift, size - shift), shift))
-
-
-def gather_tokens(chunk):
-    groups, last = [], None
-    for shift in shifts():
-        if len(groups) == 3:
-            chunk = after(chunk, last)
-        here = from_ctx(chunk, shift) if shift else chunk
-        if shift and last is None:
-            last = here
-        far = tp_xor(here, 2)
-        near, near_far = tp_xor(here, 1), tp_xor(far, 1)
-        groups.append(jnp.concatenate([here, far, near, near_far], axis=0))
-    return groups
-
-
-def scatter_tp_groups(groups):
+def after_kernel(*refs):
+    pass
+
+
+def after(values, *earlier):
+    anywhere = pl.BlockSpec(memory_space=pl.ANY)
+    return pl.pallas_call(
+        after_kernel,
+        in_specs=[anywhere] * (1 + len(earlier)),
+        out_specs=anywhere,
+        out_shape=jax.ShapeDtypeStruct(values.shape, values.dtype),
+        input_output_aliases={0: 0},
+        cost_estimate=pl.CostEstimate(flops=0, bytes_accessed=0, transcendentals=0),
+    )(values, *earlier)
+
+
+def swap(values, axis, mask):
+    size = lax.axis_size(axis)
+    return lax.ppermute(values, axis, [(i, i ^ mask) for i in range(size)])
+
+
+WAYS = {"x": ("tp", 2, 0), "y": ("shard", 1, 1), "z": ("ctx", 1, 2)}
+ORDERS = (("x", "y", "z"), ("y", "z", "x"), ("z", "x", "y"))
+
+
+def column_cuts(width):
+    tiles = width // LANES
+    cuts = [0, (tiles + 2) // 3, (tiles + 2) // 3 + (tiles + 1) // 3, tiles]
+    return [cut * LANES for cut in cuts]
+
+
+def gather_tokens(chunk, *earlier):
+    cuts = column_cuts(chunk.shape[1])
+    parts = [
+        chunk[None, None, None, :, cuts[i] : cuts[i + 1]] for i in range(len(ORDERS))
+    ]
+    for step in range(3):
+        if step == 1 and earlier:
+            parts[0] = after(parts[0], *earlier)
+        for i, order in enumerate(ORDERS):
+            axis, mask, dim = WAYS[order[step]]
+            parts[i] = jnp.concatenate([parts[i], swap(parts[i], axis, mask)], axis=dim)
+    whole = jnp.concatenate(parts, axis=-1)
+    return whole.reshape(-1, chunk.shape[1])
+
+
+def scatter_near(own, other):
+    return (own.astype(f32) + swap(other, "tp", 1).astype(f32)).astype(bf16)
+
+
+def scatter_step(parts, step):
     result = []
-    for group in groups:
-        half = group.shape[0] // 2
-        summed = group[:half].astype(f32) + tp_xor(group[half:], 1).astype(f32)
-        far = tp_xor(summed[half // 2 :].astype(bf16), 2).astype(f32)
-        result.append(summed[: half // 2] + far)
+    for part, order in zip(parts, ORDERS):
+        axis, mask, dim = WAYS[order[step]]
+        keep = lax.slice_in_dim(part, 0, 1, axis=dim)
+        send = lax.slice_in_dim(part, 1, 2, axis=dim)
+        summed = keep.astype(f32) + swap(send, axis, mask).astype(f32)
+        result.append(summed.astype(bf16) if step else summed)
     return result
 
 
-def scatter_ctx_groups(groups, earlier=None):
-    size = lax.axis_size("ctx")
-    came = [groups[0]]
-    for shift, group in list(zip(shifts(), groups))[1:]:
-        came.append(
-            lax.ppermute(
-                group.astype(bf16), "ctx", [(i, (i + shift) % size) for i in range(size)]
-            )
-        )
-    if earlier is not None:
-        came = after(came, earlier)
-    return sum((piece.astype(f32) for piece in came[1:]), came[0])
+def scatter_begin(total):
+    cuts = column_cuts(total.shape[1])
+    total = total.reshape(2, 2, 2, -1, total.shape[1])
+    return [total[..., cuts[i] : cuts[i + 1]] for i in range(len(ORDERS))]
+
+
+def scatter_end(parts):
+    whole = jnp.concatenate(parts, axis=-1)
+    return whole.reshape(-1, whole.shape[-1])
+
+
+def scatter_tokens(total):
+    parts = scatter_begin(total)
+    for step in reversed(range(3)):
+        parts = scatter_step(parts, step)
+    return scatter_end(parts)
 
 
 def contract(left,right,ld,rd):
@@ -314,13 +348,6 @@
     )(query, kv, rotary, table, limits, lse, go)
 
 
-def halves(count, length):
-    if count == 1:
-        return [0]
-    second = lax.axis_index("shard")
-    return [pl.multiple_of(second * length, LANES), pl.multiple_of((1 - second) * length, LANES)]
-
-
 def weights_kernel(n_group, n_piece, *refs):
     refs = list(refs)
 
@@ -330,7 +357,7 @@
     tokens = [take(n_piece) for _ in range(n_group)]
     grads = [take(n_piece) for _ in range(n_group)]
     kept = [take(3) for _ in range(n_group)]
-    down_out, gate_out, up_out = refs
+    (out,) = refs
     down = gate = up = 0.0
     for group in range(n_group):
         token = jnp.concatenate([piece[...] for piece in tokens[group]], axis=0)
@@ -339,16 +366,17 @@
         down = down + contract(hidden[...], grad, 1, 0)
         gate = gate + contract(grad_gate[...], token, 1, 0)
         up = up + contract(grad_up[...], token, 1, 0)
-    down_out[...] = down.astype(bf16)
-    gate_out[...] = gate.astype(bf16)
-    up_out[...] = up.astype(bf16)
+    units = gate.shape[0]
+    out[0, :units] = gate.astype(bf16)
+    out[0, units : 2 * units] = up.astype(bf16)
+    out[0, 2 * units :] = down.astype(bf16)
 
 
 def ffn_weight_grads(tokens, grads, kept):
     n_group, n_piece = len(tokens), len(tokens[0])
     rows, width = tokens[0][0].shape
     units = kept[0][0].shape[0]
-    step = 512
+    step = width // 4
 
     def column(height):
         return pl.BlockSpec((height, step), lambda i: (0, i))
@@ -361,8 +389,8 @@
         functools.partial(weights_kernel, n_group, n_piece),
         grid=(width // step,),
         in_specs=[column(rows)] * len(flat) + [whole] * (3 * n_group),
-        out_specs=[column(units)] * 3,
-        out_shape=[jax.ShapeDtypeStruct((units, width), bf16)] * 3,
+        out_specs=pl.BlockSpec((1, 3 * units, step), lambda i: (i % 2, 0, i // 2)),
+        out_shape=jax.ShapeDtypeStruct((2, 3 * units, width // 2), bf16),
         compiler_params=pltpu.CompilerParams(vmem_limit_bytes=48 * MIB),
         cost_estimate=pl.CostEstimate(
             flops=6 * total * width * units, bytes_accessed=33_000_000, transcendentals=0
@@ -370,86 +398,144 @@
     )(*flat, *[array for group in kept for array in group])
 
 
-def by_ctx(size, write):
-    me = lax.axis_index("ctx")
-    for place in range(size):
+def group_place():
+    return (lax.axis_index("shard") & 1) * 2 + (lax.axis_index("ctx") & 1)
+
+
+def by_place(write):
+    me = group_place()
+    for place in range(4):
 
         @pl.when(me == place)
         def _(place=place):
             write(place)
 
 
-def join_kernel(size, *refs):
+def join_kernel(*refs):
     length = refs[0].shape[1]
     out_ref = refs[-1]
 
     def write(me):
-        for k in range(size):
-            block = (me - k) % size
+        for k in range(4):
+            block = me ^ k
             out_ref[:, block * length : (block + 1) * length] = refs[k][...]
 
-    by_ctx(size, write)
+    by_place(write)
 
 
 def join_columns(pieces):
-    size = len(pieces)
     height, length = pieces[0].shape
     return pl.pallas_call(
-        functools.partial(join_kernel, size),
-        out_shape=jax.ShapeDtypeStruct((height, size * length), pieces[0].dtype),
+        join_kernel,
+        out_shape=jax.ShapeDtypeStruct((height, 4 * length), pieces[0].dtype),
         compiler_params=pltpu.CompilerParams(vmem_limit_bytes=16 * MIB),
         cost_estimate=pl.CostEstimate(
-            flops=0, bytes_accessed=4 * size * pieces[0].size, transcendentals=0
+            flops=0, bytes_accessed=16 * pieces[0].size, transcendentals=0
         ),
     )(*pieces)
 
 
-def place_kernel(size, turn, *refs):
-    out_ref = refs[-1]
-    height = refs[0].shape[0]
+def place_kernel(*refs):
+    pieces, (gate_ref, up_ref, down_ref) = refs[:4], refs[4:]
+    height = pieces[0].shape[0] // 3
 
     def write(me):
-        for k in range(size):
-            block = (me - k) % size
-            piece = refs[k][...].astype(f32)
-            if turn:
-                out_ref[:, block * height : (block + 1) * height] = piece.T
-            else:
-                out_ref[block * height : (block + 1) * height, :] = piece
-
-    by_ctx(size, write)
-
-
-def place_rows(pieces, turn):
-    size = len(pieces)
+        for k in range(4):
+            rows = slice((me ^ k) * height, ((me ^ k) + 1) * height)
+            gate_ref[:, rows] = pieces[k][:height].astype(f32).T
+            up_ref[:, rows] = pieces[k][height : 2 * height].astype(f32).T
+            down_ref[rows, :] = pieces[k][2 * height :].astype(f32)
+
+    by_place(write)
+
+
+def place_rows(pieces):
     height, length = pieces[0].shape
-    shape = (length, size * height) if turn else (size * height, length)
+    total = 4 * height // 3
+    inner = jax.ShapeDtypeStruct((length, total), f32)
     return pl.pallas_call(
-        functools.partial(place_kernel, size, turn),
-        out_shape=jax.ShapeDtypeStruct(shape, f32),
-        compiler_params=pltpu.CompilerParams(vmem_limit_bytes=24 * MIB),
+        place_kernel,
+        out_shape=[inner, inner, jax.ShapeDtypeStruct((total, length), f32)],
+        compiler_params=pltpu.CompilerParams(vmem_limit_bytes=40 * MIB),
         cost_estimate=pl.CostEstimate(
-            flops=0, bytes_accessed=6 * size * pieces[0].size, transcendentals=0
+            flops=0, bytes_accessed=24 * pieces[0].size, transcendentals=0
         ),
     )(*pieces)
 
 
-def split_kernel(n_half, keep_ref, came_ref, out_ref):
-    n, height, length = out_ref.shape
-    keep = keep_ref[:, pl.ds(halves(n_half, n * length)[0], n * length)].astype(f32)
-    total = (keep + came_ref[...].astype(f32)).astype(bf16)
-    for i in range(n):
-        out_ref[i] = total[:, i * length : (i + 1) * length]
-
-
-def add_and_split(values, came, n):
-    height, length = came.shape
+def split_kernel(in_ref, out_ref):
+    length = out_ref.shape[2]
+    for i in range(4):
+        out_ref[i] = in_ref[:, i * length : (i + 1) * length]
+
+
+def split_columns(values):
+    height, length = values.shape
     return pl.pallas_call(
-        functools.partial(split_kernel, values.shape[1] // length),
-        out_shape=jax.ShapeDtypeStruct((n, height, length // n), bf16),
+        split_kernel,
+        out_shape=jax.ShapeDtypeStruct((4, height, length // 4), bf16),
         compiler_params=pltpu.CompilerParams(vmem_limit_bytes=24 * MIB),
-        cost_estimate=pl.CostEstimate(flops=0, bytes_accessed=6 * came.size, transcendentals=0),
-    )(values, came)
+        cost_estimate=pl.CostEstimate(flops=0, bytes_accessed=4 * values.size, transcendentals=0),
+    )(values)
+
+
+def exchange_group(parts):
+    me = group_place()
+    pieces = [lax.dynamic_index_in_dim(parts, me, 0, False)]
+    size = lax.axis_size("ctx")
+    for k in range(1, 4):
+        send = lax.dynamic_index_in_dim(parts, me ^ k, 0, False)
+        pairs = [
+            (i * size + j, (i ^ (k >> 1)) * size + (j ^ (k & 1)))
+            for i in range(lax.axis_size("shard"))
+            for j in range(size)
+        ]
+        pieces.append(lax.ppermute(send, ("shard", "ctx"), pairs))
+    return pieces
+
+
+def block_sized():
+    return lax.axis_size("shard") == 2 and lax.axis_size("ctx") == 4
+
+
+def hidden_pieces(weights):
+    parts = [weight.reshape(4, -1, weight.shape[1]) for weight in weights]
+    return exchange_group(jnp.concatenate(parts, axis=1))
+
+
+def far_groups():
+    size = lax.axis_size("ctx")
+    return [list(range(first, size, 2)) for first in range(2)]
+
+
+def hidden_gather(joined):
+    return lax.all_gather(joined, "ctx", axis_index_groups=far_groups(), axis=0)
+
+
+def hidden_rows(whole):
+    length, height = whole.shape[2] // 2, whole.shape[1] // 3
+    weights = []
+    for w in range(3):
+        rows = whole[:, w * height : (w + 1) * height]
+        blocks = [rows[far, :, i * length : (i + 1) * length] for i in range(2) for far in range(2)]
+        weights.append(jnp.concatenate(blocks, axis=1))
+    return weights
+
+
+def hidden_rows_plain(weight):
+    whole = lax.all_gather(weight, ("shard", "ctx"), axis=1, tiled=True)
+    height = whole.shape[0] // 4
+    return lax.dynamic_slice_in_dim(whole, group_place() * height, height, 0)
+
+
+def hidden_grad_plain(grad):
+    length = grad.shape[2] // 2
+    blocks = [grad[far, :, i * length : (i + 1) * length] for i in range(2) for far in range(2)]
+    grad = jnp.concatenate(blocks, axis=1)
+    whole = jnp.zeros((4 * grad.shape[0], grad.shape[1]), bf16)
+    whole = lax.dynamic_update_slice_in_dim(whole, grad, group_place() * grad.shape[0], 0)
+    whole = lax.psum_scatter(whole, ("shard", "ctx"), scatter_dimension=1, tiled=True)
+    return whole.astype(f32)
 
 
 def on_device(
@@ -485,16 +571,6 @@
     gain_row = jnp.concatenate([attn_gain, ffn_gain, q_gain, kv_gain])
     n_blocks = n_shard * n_ctx * n_tp
     everywhere = ("shard", "ctx", "tp")
-    gains = lax.all_to_all(
-        jnp.broadcast_to(gain_row[None, None], (n_blocks, 1, n_gain)), everywhere, 0, 0
-    )
-    gains = gains[:, 0].astype(f32)
-    cut = attn_gain.shape[0]
-    gain_attn = gains[:, :cut].reshape(1, -1)
-    gain_ffn = gains[:, cut : 2 * cut].reshape(1, -1)
-    gain_query = gains[:, 2 * cut : 2 * cut + q_gain.shape[0]].reshape(1, -1)
-    gain_latent = gains[:, 2 * cut + q_gain.shape[0] :].reshape(1, -1)
-
     small = jnp.stack(
         [
             jnp.concatenate(
@@ -507,19 +583,33 @@
             for i in range(n_tp)
         ]
     )
-    small = gather_ctx(exchange_tp(small).reshape(-1, part))
-    q_up, kv_up, out_proj, gate_proj, up_proj, down_proj = lax.optimization_barrier(
-        (q_up, kv_up, out_proj, gate_proj, up_proj, down_proj, small)
-    )[:6]
+    small = jnp.broadcast_to(small[None], (n_ctx,) + small.shape)
+    small = lax.all_to_all(small.reshape(n_ctx * n_tp, block, part), ("ctx", "tp"), 0, 0)
+    gains = lax.all_to_all(
+        after(jnp.broadcast_to(gain_row[None, None], (n_blocks, 1, n_gain)), small), everywhere, 0, 0
+    )
+    gains = gains[:, 0].astype(f32)
+    cut = attn_gain.shape[0]
+    gain_attn = gains[:, :cut].reshape(1, -1)
+    gain_ffn = gains[:, cut : 2 * cut].reshape(1, -1)
+    gain_query = gains[:, 2 * cut : 2 * cut + q_gain.shape[0]].reshape(1, -1)
+    gain_latent = gains[:, 2 * cut + q_gain.shape[0] :].reshape(1, -1)
+
     down_part = gather_shard(small.reshape(-1, part), 0)
-
-    up_query = gather_ctx(q_up)
-    up_latent = gather_ctx(kv_up)
-    up_query = gather_shard(up_query.reshape(-1, q_up.shape[1]), 0)
-    up_latent = gather_shard(up_latent.reshape(-1, kv_up.shape[1]), 0)
-    out_full = lax.all_gather(out_proj, ("shard", "ctx"), axis=1, tiled=True)
-
-    heads = up_query.shape[1] // HEAD
+    out_full = lax.all_gather(after(out_proj, small), ("shard", "ctx"), axis=1, tiled=True)
+    hidden_weights = (gate_proj.T, up_proj.T, down_proj)
+    if block_sized():
+        pieces = hidden_pieces((after(gate_proj.T, small),) + hidden_weights[1:])
+        hidden_joined = join_columns(pieces)
+    else:
+        gate_full, upward_full, down_full = map(hidden_rows_plain, hidden_weights)
+        hidden_joined = gate_full
+
+    up_query = gather_ctx(after(q_up, down_part))
+    up_latent = gather_ctx(after(kv_up, down_part))
+
+
+    heads = q_up.shape[1] // HEAD
     positions = offset + jnp.arange(piece, dtype=jnp.int32)
     cosine_here, sine_here = rope_tables(positions)
     docs = doc_lengths.shape[1]
@@ -550,6 +640,8 @@
     normed_one = stream * inverse_one
     input_low = (normed_one * gain_attn).astype(bf16)
     low_rank = gather_tp(dot(input_low, down_part, ((1,), (0,))))
+    up_query = gather_shard(after(up_query.reshape(-1, q_up.shape[1]), low_rank), 0)
+    up_latent = gather_shard(after(up_latent.reshape(-1, kv_up.shape[1]), low_rank), 0)
     query_latent = low_rank[:, :, :q_part].transpose(1, 0, 2).reshape(rows, QRANK)
     latent_raw = low_rank[:, :, q_part:].transpose(1, 0, 2).reshape(rows, KVRANK + ROPE)
     inverse_latent = rms_inverse(latent_raw[:, :KVRANK])
@@ -564,36 +656,15 @@
     half = seqs // 2
     mine = rank & 1
     keys_mine = lax.dynamic_slice_in_dim(keys_here, mine * half, half, 0)
-    keys_mine = gather_ctx(keys_mine)
+    keys_mine = gather_ctx(after(keys_mine, hidden_joined))
+    if block_sized():
+        hidden_gathered = hidden_gather(after(hidden_joined, keys_mine))
+        gate_full, upward_full, down_full = hidden_rows(hidden_gathered)
     keys_mine = keys_mine.transpose(1, 0, 2, 3).reshape(half, seq_len, KVRANK + LANES)
     keys_all = pair_order(keys_mine, tp_xor(keys_mine, 1), low_bit, 0)
     latent_all, rotary_all = keys_all[..., :KVRANK], keys_all[..., KVRANK:]
 
-    grad_ffn = lax.all_gather(
-        after((res_scale * own_chunk(grad_out)).astype(bf16), low_rank), ("ctx", "tp"), axis=0
-    )
-    grad_ffn_groups = []
-    for shift in shifts():
-        place = lax.rem(lax.axis_index("ctx") + shift, n_ctx) * n_tp
-        grad_ffn_groups.append(
-            jnp.concatenate(
-                [
-                    lax.dynamic_index_in_dim(grad_ffn, place + (rank ^ i), 0, False)
-                    for i in (0, 2, 1, 3)
-                ],
-                axis=0,
-            )
-        )
-
-    def hidden_rows(weight):
-        return exchange_ctx(weight.reshape(n_ctx, -1, weight.shape[1]))
-
-    gate_pieces, up_pieces = hidden_rows(gate_proj.T), hidden_rows(up_proj.T)
-    down_pieces = hidden_rows(down_proj)
-
-    down_all = gather_tp(after(down_part, keys_all))
-    down_query = down_all[:, :, :q_part].transpose(1, 0, 2).reshape(width, QRANK)
-    down_latent = down_all[:, :, q_part:].transpose(1, 0, 2).reshape(width, KVRANK + ROPE)
+    grad_ffn = gather_tokens((res_scale * own_chunk(grad_out)).astype(bf16))
 
     inverse_query = rms_inverse(query_latent)
     normed_query = query_latent * inverse_query
@@ -605,18 +676,18 @@
         query, key_value, rotary_all, table, limits.transpose(0, 2, 1), heads
     )
     attended_low = attended_low.reshape(rows, heads * VDIM)
-    gate_full = gather_shard(join_columns(after(gate_pieces, attended_low)), 1)
 
     attn_out = scatter_tp(
         dot(attended_low, out_full, ((1,), (0,))).reshape(n_tp, chunk_rows, width)
     )
-    upward_full = gather_shard(join_columns(after(up_pieces, attn_out)), 1)
-    down_full = gather_shard(join_columns(after(down_pieces, attn_out)), 1)
     middle = own_chunk(stream) + res_scale * attn_out
     inverse_two = rms_inverse(middle)
     normed_two = middle * inverse_two
-    ffn_groups = gather_tokens((normed_two * gain_ffn).astype(bf16))
-
+    ffn_own = gather_tokens(
+        (normed_two * gain_ffn).astype(bf16), *([hidden_gathered] if block_sized() else [])
+    )
+    ffn_groups = [ffn_own, swap(ffn_own, "tp", 1)]
+    grad_ffn_groups = [grad_ffn, swap(grad_ffn, "tp", 1)]
     ffn_parts, grad_two_parts, kept = [], [], []
     for ffn_low, grad_low in zip(ffn_groups, grad_ffn_groups):
         gate_value = dot(ffn_low, gate_full, ((1,), (1,)))
@@ -635,15 +706,23 @@
         ffn_parts.append(dot(hidden_low, down_full, ((1,), (0,))).astype(bf16))
         kept.append((hidden_low.T, grad_gate.T, grad_upward.T))
 
-    grad_two_parts = scatter_tp_groups(grad_two_parts)
-    grad_down_w, grad_gate_w, grad_upward_w = ffn_weight_grads(
+    grad_two = scatter_tokens(scatter_near(*grad_two_parts))
+    hidden_grads = ffn_weight_grads(
         [[group] for group in ffn_groups], [[group] for group in grad_ffn_groups], kept
     )
-    grad_two = scatter_ctx_groups(grad_two_parts, grad_gate_w)
-    ffn_parts = scatter_tp_groups(after(ffn_parts, grad_two_parts))
+    if block_sized():
+        hidden_sums = lax.psum_scatter(
+            hidden_grads,
+            "ctx",
+            scatter_dimension=0,
+            axis_index_groups=far_groups(),
+        )
+    ffn_sum = scatter_near(ffn_parts[0], after(ffn_parts[1], grad_two))
+    down_all = gather_tp(after(down_part.T, grad_two)).reshape(-1, width)
     grad_middle = own_chunk(grad_out) + norm_backward(grad_two, normed_two, inverse_two, gain_ffn)
     grad_gain_ffn = jnp.sum(grad_two * normed_two, axis=0)
-    grad_attn = gather_tp((res_scale * grad_middle).astype(bf16)).reshape(rows, width)
+    grad_attn = after((res_scale * grad_middle).astype(bf16), hidden_grads)
+    grad_attn = gather_tp(grad_attn).reshape(rows, width)
 
     grad_out_w = lax.psum_scatter(
         dot(attended_low, grad_attn, ((0,), (0,))).astype(bf16),
@@ -682,10 +761,19 @@
     )
     grad_pre_query = dot(grad_query, up_query, ((1,), (1,))).astype(bf16)
     grad_pre_query = add_near(grad_pre_query.reshape(seqs, piece, QRANK))
+    ffn_sum = scatter_step(scatter_begin(ffn_sum), 2)
     grad_low = jnp.concatenate([grad_pre_query, grad_keys], axis=-1).astype(bf16)
+    grad_low = after(grad_low, *ffn_sum)
     grad_low = (grad_low.astype(f32) + tp_xor(grad_low, 2).astype(f32)).astype(bf16)
     grad_low = pair_order(grad_low, tp_xor(grad_low, 1), low_bit, 0)
-    grad_low = grad_low.reshape(rows, QRANK + KVRANK + LANES).astype(f32)
+    ffn_sum = scatter_step(ffn_sum, 1)
+    grad_low = after(grad_low.reshape(rows, QRANK + KVRANK + LANES), *ffn_sum)
+    ffn_sum = scatter_end(scatter_step(ffn_sum, 0))
+    hidden_back = []
+    if block_sized():
+        hidden_back = exchange_group(split_columns(hidden_sums))
+        down_all = after(down_all, *hidden_back)
+    grad_low = grad_low.astype(f32)
 
     grad_out_query, grad_out_latent = grad_low[:, :QRANK], grad_low[:, QRANK : QRANK + KVRANK]
     grad_query_latent = norm_backward(grad_out_query, normed_query, inverse_query, gain_query)
@@ -698,14 +786,20 @@
     grad_query_latent = grad_query_latent.astype(bf16)
     grad_latent_raw = jnp.concatenate([grad_compressed, grad_rotary], axis=-1).astype(bf16)
 
-    grad_pre_one = dot(own_chunk(grad_query_latent), down_query, ((1,), (1,)))
-    grad_pre_one = grad_pre_one + dot(own_chunk(grad_latent_raw), down_latent, ((1,), (1,)))
+    own_query, own_latent = own_chunk(grad_query_latent), own_chunk(grad_latent_raw)
+    grad_parts = [
+        part_of[:, i * length : (i + 1) * length]
+        for i in range(n_tp)
+        for part_of, length in ((own_query, q_part), (own_latent, kv_part))
+    ]
+    grad_pre_one = dot(jnp.concatenate(grad_parts, axis=1), down_all, ((1,), (0,)))
     normed_own = own_chunk(normed_one)
     grad_input = grad_middle + norm_backward(
         grad_pre_one, normed_own, own_chunk(inverse_one), gain_attn
     )
     grad_gain_attn = jnp.sum(grad_pre_one * normed_own, axis=0)
-    grad_input = gather_tp(round_low(grad_input).astype(bf16)).astype(f32)
+    grad_input = round_low(grad_input).astype(bf16)
+    grad_input = gather_tp(grad_input).astype(f32)
 
     grad_part = jnp.concatenate(
         [
@@ -715,9 +809,8 @@
         axis=1,
     )
     grad_small = dot(input_low, grad_part, ((0,), (0,)))
-    grad_small = scatter_ctx(
-        scatter_shard(grad_small, 0).reshape(n_ctx, n_tp, block, part)
-    )
+    grad_half = scatter_shard(grad_small, 0)
+    grad_small = scatter_ctx(grad_half.reshape(n_ctx, n_tp, block, part))
     grad_small = exchange_tp(grad_small.astype(bf16)).astype(f32).transpose(1, 0, 2)
     grad_down_query = grad_small[:, :, :q_part].reshape(block, QRANK)
     grad_down_latent = grad_small[:, :, q_part:].reshape(block, KVRANK + ROPE)
@@ -733,10 +826,7 @@
     grad_gains = lax.all_to_all(grad_gains[:, None], everywhere, 0, 0)
     grad_gains = jnp.sum(grad_gains[:, 0], axis=0)
 
-    grad_down_w, grad_query, grad_key_value = lax.optimization_barrier(
-        (grad_down_w, grad_query, grad_key_value, grad_keys)
-    )[:3]
-    output = round_low(middle + res_scale * scatter_ctx_groups(ffn_parts, grad_keys))
+    output = round_low(middle + res_scale * ffn_sum)
     output = gather_tp(output.astype(bf16)).astype(f32)
 
     def rows_grad(grad):
@@ -747,23 +837,13 @@
     grad_up_latent = rows_grad(
         dot(latent_all.reshape(-1, KVRANK), grad_key_value, ((0,), (0,)))
     )
-    def hidden_grad(grad):
-        length = grad.shape[1] // n_shard
-        if n_shard == 2:
-            other = 1 - lax.axis_index("shard")
-            send = lax.dynamic_slice_in_dim(grad, other * length, length, 1)
-            came = lax.ppermute(send, "shard", [(0, 1), (1, 0)])
-            parts = add_and_split(grad, came, n_ctx)
-        else:
-            mine = scatter_shard(grad, 1).astype(bf16)
-            parts = mine.reshape(mine.shape[0], n_ctx, -1).transpose(1, 0, 2)
-        return parts
-
-    grad_gate_w = exchange_ctx(hidden_grad(after(grad_gate_w, grad_attn)))
-    grad_upward_w = exchange_ctx(hidden_grad(after(grad_upward_w, grad_attn)))
-    grad_gate_w = place_rows(after(grad_gate_w, grad_low), True)
-    grad_upward_w = place_rows(after(grad_upward_w, grad_low), True)
-    grad_down_w = place_rows(exchange_ctx(hidden_grad(grad_down_w)), False)
+    if block_sized():
+        grad_gate_w, grad_upward_w, grad_down_w = place_rows(hidden_back)
+    else:
+        units = hidden_grads.shape[1] // 3
+        split = [hidden_grads[:, i * units : (i + 1) * units] for i in range(3)]
+        grad_gate_w, grad_upward_w, grad_down_w = map(hidden_grad_plain, split)
+        grad_gate_w, grad_upward_w = grad_gate_w.T, grad_upward_w.T
     return (
         output.reshape(seqs, piece, width),
         grad_input.reshape(seqs, piece, width),

time: 1030 us -> 964 us (0.936)
  starting transfers between devices: 239 us -> 115 us
  matrix products: 79.9 us -> 102 us
  local copies, waits for them, and re-layouts: 134 us -> 154 us
    ppermute x30 -> x12, starting transfers between devices: 115 us -> 20 us  [exchange_ctx(): lax.ppermute(send, 'ctx', [(i, (i + shift) % size) for i in range(size)])]
    all_gather x2, waiting for transfers between devices: 0.02 us -> 66.9 us  [the longest x1 66.9 us: hidden_gather(): return lax.all_gather(joined, 'ctx', axis_index_groups=far_groups(), axis=0)]
    ppermute x9 -> x46, waiting for transfers between devices: 61.1 us -> 115 us  [the longest x40 92.1 us: swap(): return lax.ppermute(values, axis, [(i, i ^ mask) for i in range(size)])]
    ppermute x6 -> x3, waiting for transfers between devices: 56.5 us -> 12.2 us  [gather_shard(): other = lax.ppermute(values, 'shard', [(0, 1), (1, 0)])]
    ppermute x15 -> x9, waiting for transfers between devices: 71.4 us -> 43.1 us  [from_ctx(): lax.ppermute(values, 'ctx', [((i + shift) % size, i) for i in range(size)])]
    ppermute x15 -> x9, starting transfers between devices: 34.1 us -> 11.7 us  [from_ctx(): lax.ppermute(values, 'ctx', [((i + shift) % size, i) for i in range(size)])]
    dot_general x36 -> x23, matrix products: 76.2 us -> 98 us  [dot(): lax.dot_general(left, right, (dims, ((), ())), preferred_element_type=f32)]
    dynamic_update_slice x24 -> x16, local copies, waits for them, and re-layouts: 30 us -> 8.83 us  [placed(): whole = lax.dynamic_update_index_in_dim(whole, piece, place, 0)]
  transfers between devices with their start and end apart: 119 -> 100, of which waited for: 40 -> 43; matrix products, arithmetic and copies ran while one was open for 26% -> 33% of each run, Pallas kernels for 6% -> 7%
where the time goes in v3:
time: 964 us; the launch traced here: 950 us
  waiting for transfers between devices  378 us (39%)
  local copies, waits for them, and re-layouts  154 us (16%)
  other arithmetic  121 us (13%)
  starting transfers between devices  115 us (12%)
  matrix products  102 us (11%)
  Pallas kernels  63.9 us (7%)
  between operations  17.1 us (2%)
    dot_general x23, matrix products, dot(): lax.dot_general(left, right, (dims, ((), ())), preferred_element_type=f32)  98 us
    ppermute x40, waiting for transfers between devices, swap(): return lax.ppermute(values, axis, [(i, i ^ mask) for i in range(size)])  92.1 us
    ppermute x20, waiting for transfers between devices, tp_xor(): return lax.ppermute(values, 'tp', [(i, i ^ mask) for i in range(size)])  78 us
    all_gather x1, waiting for transfers between devices, hidden_gather(): return lax.all_gather(joined, 'ctx', axis_index_groups=far_groups(), axis=0)  66.9 us
    ppermute x12, waiting for transfers between devices, exchange_ctx(): lax.ppermute(send, 'ctx', [(i, (i + shift) % size) for i in range(size)])  61.6 us
    ppermute x9, waiting for transfers between devices, from_ctx(): lax.ppermute(values, 'ctx', [((i + shift) % size, i) for i in range(size)])  43.1 us
    unnamed x324, local copies, waits for them, and re-layouts  39.1 us
    ppermute x40, starting transfers between devices, swap(): return lax.ppermute(values, axis, [(i, i ^ mask) for i in range(size)])  38.1 us
  transfers between devices with their start and end apart: 100, of which 43 were waited for; matrix products, arithmetic and copies ran while one was open for 33% of the time, Pallas kernels for 7%

profile of v3, /device:TPU:0, one launch (start us, length us, event | category | flops | bytes accessed | tf_op | source)
XLA Modules:
  0.0 950.4 jit_solution(1059605446645425927)
XLA Ops:
  13.5 7.4 all-to-all-start
  34.3 6.6 broadcast_multiply_fusion
  46.4 6.6 all-to-all-start.1
  70.5 6.8 collective-permute-done
  80.3 3.7 copy.387.refs_1_
  88.0 3.4 fusion.34
  94.1 36.2 %collective-permute-done.14 = bf16[32,1280]{1,0:T(8,128)(2,1)S(1)} collective-permute-done((bf16[32,1280]{1,0:T(8,128)(2,1)}, bf16[32,1280]{1,0:T(8,128)(2,1)S(1)}, u32[]{:S(2)}, u32[]{:S(2)}) %collective-permute-start.14) | collective-permute-done | bytes 81952 | tf_op jit(solution)/shard_map/ppermute | solution.py:74
  131.8 12.3 %collective-permute-done.1 = f32[512,264]{0,1:T(8,128)S(1)} collective-permute-done((f32[512,264]{0,1:T(8,128)S(1)}, f32[512,264]{0,1:T(8,128)S(1)}, u32[]{:S(2)}, u32[]{:S(2)}) %collective-permute-start.1) | collective-permute-done | bytes 540704 | tf_op jit(solution)/shard_map/ppermute | solution.py:69
  144.2 3.0 collective-permute-start.3
  160.1 6.9 collective-permute-done.4
  189.4 3.0 slice_bitcast_fusion
  196.5 4.1 multiply_convert_fusion.9
  204.8 5.4 collective-permute-done.6
  217.0 3.8 convolution_convert_fusion.2.kv_ref
  220.8 14.4 %shard_map.262 = (bf16[2,256,640]{2,1,0:T(8,128)(2,1)S(1)}, f32[2,256,128]{2,1,0:T(8,128)S(1)}) custom-call(f32[2,256,960]{2,1,0:T(8,128)} %fusion.22.q_ref, bf16[2,1024,1280]{2,1,0:T(8,128)(2,1)} %convolution_convert_fusion.2.kv_ref, bf16[2,1024,128]{2,1,0:T(8,128)(2,1)S(1)} %pad_maximum_fusion.25.rotary_ref, ...), custom_call_target="tpu_custom_call" | custom-call | flops 2684354560 | bytes 12000000 | tf_op jit(solution)/shard_map/pallas_call | solution.py:290
  235.3 4.5 fusion
  240.1 3.0 collective-permute-done.18
  248.0 14.2 %collective-permute-done.19 = bf16[128,2560]{1,0:T(8,128)(2,1)S(1)} collective-permute-done((bf16[128,2560]{1,0:T(8,128)(2,1)S(1)}, bf16[128,2560]{1,0:T(8,128)(2,1)S(1)}, u32[]{:S(2)}, u32[]{:S(2)}) %collective-permute-start.19) | collective-permute-done | bytes 655392 | tf_op jit(solution)/shard_map/ppermute | solution.py:69
  269.1 7.7 collective-permute-done.26
  281.3 66.9 %all-gather.6.cloned.1.call-done = bf16[2400,1280]{1,0:T(8,128)(2,1)} async-done(((bf16[1200,1280]{1,0:T(8,128)(2,1)}), bf16[2400,1280]{1,0:T(8,128)(2,1)}) %all-gather.6.cloned.1.call-update) | async-done | bytes 6144016 | tf_op jit(solution)/shard_map/all_gather | solution.py:512
  352.6 9.2 collective-permute-done.21
  369.0 23.2 %collective-permute-done.31 = bf16[2,1,1,128,896]{4,3,2,1,0:T(8,128)(2,1)S(1)} collective-permute-done((bf16[2,1,1,128,896]{4,3,2,1,0:T(8,128)(2,1)S(1)}, bf16[2,1,1,128,896]{4,3,2,1,0:T(8,128)(2,1)S(1)}, u32[]{:S(2)}, u32[]{:S(2)}) %collective-permute-start.31) | collective-permute-done | bytes 458784 | tf_op jit(solution)/shard_map/ppermute | solution.py:188
  399.4 9.6 %collective-permute-done.38 = bf16[2,1,2,128,768]{4,3,2,1,0:T(8,128)(2,1)S(1)} collective-permute-done((bf16[2,1,2,128,768]{4,3,2,1,0:T(8,128)(2,1)S(1)}, bf16[2,1,2,128,768]{4,3,2,1,0:T(8,128)(2,1)S(1)}, u32[]{:S(2)}, u32[]{:S(2)}) %collective-permute-start.38) | collective-permute-done | bytes 786464 | tf_op jit(solution)/shard_map/ppermute | solution.py:188
  409.0 4.1 collective-permute-done.32
  423.4 5.3 fusion.5
  428.8 7.4 fusion.36
  436.2 8.9 add_convert_fusion.2
  450.1 2.9 fusion.14
  453.0 7.4 fusion.35
  460.4 8.6 add_convert_fusion.1
  475.6 19.9 %shard_map.267.refs_1_ = bf16[2,1200,1280]{2,1,0:T(8,128)(2,1)} custom-call(bf16[1024,2560]{1,0:T(8,128)(2,1)} %bitcast.437, bf16[1024,2560]{1,0:T(8,128)(2,1)} %copy-done.139, bf16[1024,2560]{1,0:T(8,128)(2,1)} %bitcast.439, bf16[1024,2560]{1,0:T(8,128)(2,1)} %collective-permute-done.39.refs_3_, bf16[400,1024]{1,0:T(8,128)(2,1)S(1)} %get-tuple-element.167.refs_4_, ...), custom_call_target="tpu_custom_call" | custom-call | flops 12582912000 | bytes 33000000 | tf_op jit(solution)/shard_map/pallas_call | solution.py:388
  504.6 4.6 collective-permute-done.48
  514.3 12.8 %collective-permute-done.45 = bf16[1,2,1,128,896]{4,3,2,1,0:T(8,128)(2,1)S(1)} collective-permute-done((bf16[1,2,1,128,896]{4,3,2,1,0:T(8,128)(2,1)S(1)}, bf16[1,2,1,128,896]{4,3,2,1,0:T(8,128)(2,1)S(1)}, u32[]{:S(2)}, u32[]{:S(2)}) %collective-permute-start.45) | collective-permute-done | bytes 458784 | tf_op jit(solution)/shard_map/ppermute | solution.py:188
  528.2 4.9 collective-permute-done.49
  548.3 7.0 collective-permute-done.62
  557.7 7.1 convolution_convert_fusion.refs_0_
  566.0 15.6 %collective-permute-done.71 = bf16[264,2560]{1,0:T(8,128)(2,1)} collective-permute-done((bf16[264,2560]{1,0:T(8,128)(2,1)}, bf16[264,2560]{1,0:T(8,128)(2,1)}, u32[]{:S(2)}, u32[]{:S(2)}) %collective-permute-start.71) | collective-permute-done | bytes 1351712 | tf_op jit(solution)/shard_map/ppermute | solution.py:69
  590.1 3.0 convolution_convert_fusion.6
  593.1 23.8 %shard_map.269 = (bf16[2,256,960]{2,1,0:T(8,128)(2,1)}, bf16[2,1024,1280]{2,1,0:T(8,128)(2,1)}, f32[2,1024,128]{2,1,0:T(8,128)}) custom-call(f32[2,256,960]{2,1,0:T(8,128)} %fusion.22.q_ref, bf16[2,1024,1280]{2,1,0:T(8,128)(2,1)} %convolution_convert_fusion.2.kv_ref, bf16[2,1024,128]{2,1,0:T(8,128)(2,1)} %copy-done.8, f32[3,256,128]{2,1,0:T(8,128)} %copy-done.9, ...), custom_call_target="tpu_custom_call" | custom-call | flops 6710886400 | bytes 20000000 | tf_op jit(solution)/shard_map/pallas_call | solution.py:338
  617.0 4.2 convolution_bitcast_fusion
  631.1 5.7 convolution_convert_fusion.3
  637.8 4.0 convolution_convert_fusion.4
  653.1 7.6 collective-permute-done.91
  665.6 3.8 collective-permute-start.88
  670.8 8.4 collective-permute-done.86
  679.3 3.8 collective-permute-start.66
  684.0 3.3 collective-permute-start.68
  687.2 15.8 %collective-permute-done.87 = bf16[96,960]{1,0:T(8,128)(2,1)S(1)} collective-permute-done((bf16[96,960]{1,0:T(8,128)(2,1)S(1)}, bf16[96,960]{1,0:T(8,128)(2,1)S(1)}, u32[]{:S(2)}, u32[]{:S(2)}) %collective-permute-start.87) | collective-permute-done | bytes 184352 | tf_op jit(solution)/shard_map/ppermute | solution.py:83
  703.9 11.0 %collective-permute-done.67 = bf16[1,256,384]{2,1,0:T(8,128)(2,1)S(1)} collective-permute-done((bf16[1,256,384]{2,1,0:T(8,128)(2,1)S(1)}, bf16[1,256,384]{2,1,0:T(8,128)(2,1)S(1)}, u32[]{:S(2)}, u32[]{:S(2)}) %collective-permute-start.67) | collective-permute-done | bytes 196640 | tf_op jit(solution)/shard_map/ppermute | solution.py:83
  719.3 5.9 add_convert_fusion
  728.4 2.8 copy.425
  749.9 6.8 collective-permute-done.51
  765.0 9.3 collective-permute-done.73
  779.7 13.1 %collective-permute-done.75 = bf16[1200,320]{0,1:T(8,128)(2,1)} collective-permute-done((bf16[1200,320]{0,1:T(8,128)(2,1)}, bf16[1200,320]{0,1:T(8,128)(2,1)}, u32[]{:S(2)}, u32[]{:S(2)}) %collective-permute-start.75) | collective-permute-done | bytes 768032 | tf_op jit(solution)/shard_map/ppermute | solution.py:493
  796.2 3.8 shard_map.275
  801.4 3.1 copy.452
  840.4 5.2 multiply_reduce_fusion.4
  846.4 3.3 all-to-all-start.2
  849.8 4.3 reduce-precision_convert_fusion
  863.2 22.3 %collective-permute-done.60 = bf16[128,2560]{1,0:T(8,128)(2,1)} collective-permute-done((bf16[128,2560]{1,0:T(8,128)(2,1)}, bf16[128,2560]{1,0:T(8,128)(2,1)}, u32[]{:S(2)}, u32[]{:S(2)}) %collective-permute-start.60) | collective-permute-done | bytes 655392 | tf_op jit(solution)/shard_map/ppermute | solution.py:69
  892.8 3.7 reshape.432
  908.8 8.0 collective-permute-done.80
  916.8 6.1 collective-permute-done.79
  935.9 2.8 copy.416
  (798 shorter events, 359.8 us)
Async XLA Ops:
  13.5 29.2 %all-to-all-start = ((bf16[16,80,264]{2,1,0:T(8,128)(2,1)}), bf16[16,80,264]{2,1,0:T(8,128)(2,1)S(1)}, u32[]{:S(2)}, u32[]{:S(2)}) async-start(bf16[16,80,264]{2,1,0:T(8,128)(2,1)} %bitcast.5), calls=%async_computation | async-start | bytes 1966080 | tf_op jit(solution)/shard_map/all_to_all | solution.py:587
  20.9 214.3 %all-gather.4.cloned.1.call-start = ((), (), s32[]{:S(2)}) async-start(), calls=%async_computation.5 | async-start | bytes 3686400 | tf_op jit(solution)/shard_map/all_gather | solution.py:599
  46.4 21.6 %all-to-all-start.1 = ((bf16[32,1,192]{2,1,0:T(2,128)(2,1)}), bf16[32,1,192]{2,1,0:T(2,128)(2,1)}, u32[]{:S(2)}, u32[]{:S(2)}) async-start(bf16[32,1,192]{2,1,0:T(2,128)(2,1)} %shard_map.254), calls=%async_computation.1 | async-start | bytes 65536 | tf_op jit(solution)/shard_map/all_to_all | solution.py:588
  53.0 295.1 %all-gather.6.cloned.1.call-start = ((), (), s32[]{:S(2)}) async-start(), calls=%async_computation.8 | async-start | bytes 9216000 | tf_op jit(solution)/shard_map/all_gather | solution.py:512
  54.4 22.9 %collective-permute-start = (bf16[1280,264]{0,1:T(8,128)(2,1)}, bf16[1280,264]{0,1:T(8,128)(2,1)}, u32[]{:S(2)}, u32[]{:S(2)}) collective-permute-start(bf16[1280,264]{0,1:T(8,128)(2,1)} %copy.459), channel_id=1, source_target_pairs={{0,16},{16,0},{1,17},{17,1},{2,18},{18,2},{3,19},{19,3},{4,20},{20... | collective-permute-start | bytes 2027528 | tf_op jit(solution)/shard_map/ppermute | solution.py:118
  64.6 83.9 %collective-permute-start.7 = (bf16[1200,320]{0,1:T(8,128)(2,1)}, bf16[1200,320]{0,1:T(8,128)(2,1)}, u32[]{:S(2)}, u32[]{:S(2)}) collective-permute-start(bf16[1200,320]{0,1:T(8,128)(2,1)} %bitcast.29), channel_id=1, source_target_pairs={{0,4},{4,0},{8,12},{12,8},{16,20},{20,16},{24,28},{28,24},{1,5},{5... | collective-permute-start | bytes 2304008 | tf_op jit(solution)/shard_map/ppermute | solution.py:493
  66.1 84.8 %collective-permute-start.8 = (bf16[1200,320]{0,1:T(8,128)(2,1)}, bf16[1200,320]{0,1:T(8,128)(2,1)}, u32[]{:S(2)}, u32[]{:S(2)}) collective-permute-start(bf16[1200,320]{0,1:T(8,128)(2,1)} %bitcast.484), channel_id=1, source_target_pairs={{0,16},{4,20},{8,24},{12,28},{16,0},{20,4},{24,8},{28,12},{1,17},{... | collective-permute-start | bytes 2304008 | tf_op jit(solution)/shard_map/ppermute | solution.py:493
  66.7 87.0 %collective-permute-start.9 = (bf16[1200,320]{0,1:T(8,128)(2,1)}, bf16[1200,320]{0,1:T(8,128)(2,1)}, u32[]{:S(2)}, u32[]{:S(2)}) collective-permute-start(bf16[1200,320]{0,1:T(8,128)(2,1)} %bitcast.483), channel_id=1, source_target_pairs={{0,20},{4,16},{8,28},{12,24},{16,4},{20,0},{24,12},{28,8},{1,21},{... | collective-permute-start | bytes 2304008 | tf_op jit(solution)/shard_map/ppermute | solution.py:493
  84.0 47.7 %collective-permute-start.15 = (bf16[32,1280]{1,0:T(8,128)(2,1)}, bf16[32,1280]{1,0:T(8,128)(2,1)S(1)}, u32[]{:S(2)}, u32[]{:S(2)}) collective-permute-start(bf16[32,1280]{1,0:T(8,128)(2,1)} %shard_map.260), channel_id=1, source_target_pairs={{8,0},{12,4},{0,8},{4,12},{9,1},{13,5},{1,9},{5,13},{10,2},{14,6},... | collective-permute-start | bytes 245768 | tf_op jit(solution)/shard_map/ppermute | solution.py:74
  86.5 43.8 %collective-permute-start.14 = (bf16[32,1280]{1,0:T(8,128)(2,1)}, bf16[32,1280]{1,0:T(8,128)(2,1)S(1)}, u32[]{:S(2)}, u32[]{:S(2)}) collective-permute-start(bf16[32,1280]{1,0:T(8,128)(2,1)} %shard_map.260), channel_id=1, source_target_pairs={{4,0},{8,4},{12,8},{0,12},{5,1},{9,5},{13,9},{1,13},{6,2},{10,6},{... | collective-permute-start | bytes 245768 | tf_op jit(solution)/shard_map/ppermute | solution.py:74
  148.4 21.8 %collective-permute-start.2 = (f32[2,512,264]{1,2,0:T(8,128)}, f32[2,512,264]{1,2,0:T(8,128)}, u32[]{:S(2)}, u32[]{:S(2)}) collective-permute-start(f32[2,512,264]{1,2,0:T(8,128)} %pad_maximum_fusion.14), channel_id=1, source_target_pairs={{0,1},{1,0},{2,3},{3,2},{4,5},{5,4},{6,7},{7,6},{8,9},{9,8},{10,11... | collective-permute-start | bytes 3244040 | tf_op jit(solution)/shard_map/ppermute | solution.py:69
  149.2 19.5 %collective-permute-start.5 = (bf16[96,960]{1,0:T(8,128)(2,1)}, bf16[96,960]{1,0:T(8,128)(2,1)}, u32[]{:S(2)}, u32[]{:S(2)}) collective-permute-start(bf16[96,960]{1,0:T(8,128)(2,1)} %shard_map.255), channel_id=1, source_target_pairs={{12,0},{0,4},{4,8},{8,12},{13,1},{1,5},{5,9},{9,13},{14,2},{2,6},{... | collective-permute-start | bytes 552968 | tf_op jit(solution)/shard_map/ppermute | solution.py:74
  179.3 23.4 %collective-permute-start.12 = (bf16[1,256,384]{2,1,0:T(8,128)(2,1)}, bf16[1,256,384]{2,1,0:T(8,128)(2,1)S(1)}, u32[]{:S(2)}, u32[]{:S(2)}) collective-permute-start(bf16[1,256,384]{2,1,0:T(8,128)(2,1)} %shard_map.259), channel_id=1, source_target_pairs={{12,0},{0,4},{4,8},{8,12},{13,1},{1,5},{5,9},{9,13},{14,2},{2,6},{... | collective-permute-start | bytes 589832 | tf_op jit(solution)/shard_map/ppermute | solution.py:74
  179.3 22.4 %collective-permute-start.11 = (bf16[1,256,384]{2,1,0:T(8,128)(2,1)}, bf16[1,256,384]{2,1,0:T(8,128)(2,1)}, u32[]{:S(2)}, u32[]{:S(2)}) collective-permute-start(bf16[1,256,384]{2,1,0:T(8,128)(2,1)} %shard_map.259), channel_id=1, source_target_pairs={{8,0},{12,4},{0,8},{4,12},{9,1},{13,5},{1,9},{5,13},{10,2},{14,6},... | collective-permute-start | bytes 589832 | tf_op jit(solution)/shard_map/ppermute | solution.py:74
  180.5 20.3 %collective-permute-start.10 = (bf16[1,256,384]{2,1,0:T(8,128)(2,1)}, bf16[1,256,384]{2,1,0:T(8,128)(2,1)}, u32[]{:S(2)}, u32[]{:S(2)}) collective-permute-start(bf16[1,256,384]{2,1,0:T(8,128)(2,1)} %shard_map.259), channel_id=1, source_target_pairs={{4,0},{8,4},{12,8},{0,12},{5,1},{9,5},{13,9},{1,13},{6,2},{10,6},{... | collective-permute-start | bytes 589832 | tf_op jit(solution)/shard_map/ppermute | solution.py:74
  185.1 18.7 %collective-permute-start.17 = (bf16[128,1280]{1,0:T(8,128)(2,1)S(1)}, bf16[128,1280]{1,0:T(8,128)(2,1)}, u32[]{:S(2)}, u32[]{:S(2)}) collective-permute-start(bf16[128,1280]{1,0:T(8,128)(2,1)S(1)} %copy-done.74), channel_id=1, source_target_pairs={{0,16},{16,0},{1,17},{17,1},{2,18},{18,2},{3,19},{19,3},{4,20},{20... | collective-permute-start | bytes 983048 | tf_op jit(solution)/shard_map/ppermute | solution.py:118
  187.6 22.5 %collective-permute-start.6 = (bf16[384,960]{0,1:T(8,128)(2,1)}, bf16[384,960]{0,1:T(8,128)(2,1)}, u32[]{:S(2)}, u32[]{:S(2)}) collective-permute-start(bf16[384,960]{0,1:T(8,128)(2,1)} %copy.388), channel_id=1, source_target_pairs={{0,16},{16,0},{1,17},{17,1},{2,18},{18,2},{3,19},{19,3},{4,20},{20... | collective-permute-start | bytes 2211848 | tf_op jit(solution)/shard_map/ppermute | solution.py:118
  203.7 530.7 %reduce-scatter.3.cloned.1.call-start = ((), (), s32[]{:S(2)}) async-start(), calls=%async_computation.6 | async-start | bytes 9216000 | tf_op jit(solution)/shard_map/reduce_scatter | solution.py:714
  265.9 85.3 %collective-permute-start.36 = (bf16[1,1,1,128,768]{4,3,2,1,0:T(8,128)(2,1)S(1)}, bf16[1,1,1,128,768]{4,3,2,1,0:T(8,128)(2,1)S(1)}, u32[]{:S(2)}, u32[]{:S(2)}) collective-permute-start(bf16[1,1,1,128,768]{4,3,2,1,0:T(8,128)(2,1)S(1)} %slice_bitcast_fusion.18), channel_id=1, source_target_pairs={{0,4},{4,0},{8,12},{12,8},{1,5},{5,1},{9,13},{13,9},{2,6},{6,2},{1... | collective-permute-start | bytes 589832 | tf_op jit(solution)/shard_map/ppermute | solution.py:188
  277.6 85.8 %collective-permute-start.27 = (bf16[1,1,2,128,768]{4,3,2,1,0:T(8,128)(2,1)}, bf16[1,1,2,128,768]{4,3,2,1,0:T(8,128)(2,1)}, u32[]{:S(2)}, u32[]{:S(2)}) collective-permute-start(bf16[1,1,2,128,768]{4,3,2,1,0:T(8,128)(2,1)} %pad_maximum_fusion.33), channel_id=1, source_target_pairs={{0,2},{1,3},{2,0},{3,1},{4,6},{5,7},{6,4},{7,5},{8,10},{9,11},{10,... | collective-permute-start | bytes 1179656 | tf_op jit(solution)/shard_map/ppermute | solution.py:188
  279.7 72.1 %collective-permute-start.24 = (bf16[1,2,1,128,896]{4,3,2,1,0:T(8,128)(2,1)}, bf16[1,2,1,128,896]{4,3,2,1,0:T(8,128)(2,1)S(1)}, u32[]{:S(2)}, u32[]{:S(2)}) collective-permute-start(bf16[1,2,1,128,896]{4,3,2,1,0:T(8,128)(2,1)} %pad_maximum_fusion.27), channel_id=1, source_target_pairs={{0,4},{4,0},{8,12},{12,8},{1,5},{5,1},{9,13},{13,9},{2,6},{6,2},{1... | collective-permute-start | bytes 1376264 | tf_op jit(solution)/shard_map/ppermute | solution.py:188
  361.8 34.8 %collective-permute-start.25 = (bf16[1,2,2,128,896]{4,3,2,1,0:T(8,128)(2,1)S(1)}, bf16[1,2,2,128,896]{4,3,2,1,0:T(8,128)(2,1)S(1)}, u32[]{:S(2)}, u32[]{:S(2)}) collective-permute-start(bf16[1,2,2,128,896]{4,3,2,1,0:T(8,128)(2,1)S(1)} %pad_maximum_fusion.18), channel_id=1, source_target_pairs={{0,2},{1,3},{2,0},{3,1},{4,6},{5,7},{6,4},{7,5},{8,10},{9,11},{10,... | collective-permute-start | bytes 2752520 | tf_op jit(solution)/shard_map/ppermute | solution.py:188
  363.4 33.2 %collective-permute-start.22 = (bf16[2,2,1,128,896]{4,3,2,1,0:T(8,128)(2,1)S(1)}, bf16[2,2,1,128,896]{4,3,2,1,0:T(8,128)(2,1)S(1)}, u32[]{:S(2)}, u32[]{:S(2)}) collective-permute-start(bf16[2,2,1,128,896]{4,3,2,1,0:T(8,128)(2,1)S(1)} %pad_maximum_fusion.17), channel_id=1, source_target_pairs={{0,4},{4,0},{8,12},{12,8},{1,5},{5,1},{9,13},{13,9},{2,6},{6,2},{1... | collective-permute-start | bytes 2752520 | tf_op jit(solution)/shard_map/ppermute | solution.py:188
  364.6 31.4 %collective-permute-start.28 = (bf16[2,1,2,128,768]{4,3,2,1,0:T(8,128)(2,1)S(1)}, bf16[2,1,2,128,768]{4,3,2,1,0:T(8,128)(2,1)S(1)}, u32[]{:S(2)}, u32[]{:S(2)}) collective-permute-start(bf16[2,1,2,128,768]{4,3,2,1,0:T(8,128)(2,1)S(1)} %pad_maximum_fusion.21), channel_id=1, source_target_pairs={{0,16},{16,0},{1,17},{17,1},{2,18},{18,2},{3,19},{19,3},{4,20},{20... | collective-permute-start | bytes 2359304 | tf_op jit(solution)/shard_map/ppermute | solution.py:188
  366.3 25.9 %collective-permute-start.31 = (bf16[2,1,1,128,896]{4,3,2,1,0:T(8,128)(2,1)S(1)}, bf16[2,1,1,128,896]{4,3,2,1,0:T(8,128)(2,1)S(1)}, u32[]{:S(2)}, u32[]{:S(2)}) collective-permute-start(bf16[2,1,1,128,896]{4,3,2,1,0:T(8,128)(2,1)S(1)} %pad_maximum_fusion.28), channel_id=1, source_target_pairs={{0,16},{16,0},{1,17},{17,1},{2,18},{18,2},{3,19},{19,3},{4,20},{20... | collective-permute-start | bytes 1376264 | tf_op jit(solution)/shard_map/ppermute | solution.py:188
  367.9 25.9 %collective-permute-start.34 = (bf16[1,2,1,128,896]{4,3,2,1,0:T(8,128)(2,1)S(1)}, bf16[1,2,1,128,896]{4,3,2,1,0:T(8,128)(2,1)S(1)}, u32[]{:S(2)}, u32[]{:S(2)}) collective-permute-start(bf16[1,2,1,128,896]{4,3,2,1,0:T(8,128)(2,1)S(1)} %pad_maximum_fusion.29), channel_id=1, source_target_pairs={{0,4},{4,0},{8,12},{12,8},{1,5},{5,1},{9,13},{13,9},{2,6},{6,2},{1... | collective-permute-start | bytes 1376264 | tf_op jit(solution)/shard_map/ppermute | solution.py:188
  393.8 19.4 %collective-permute-start.32 = (bf16[2,2,1,128,896]{4,3,2,1,0:T(8,128)(2,1)S(1)}, bf16[2,2,1,128,896]{4,3,2,1,0:T(8,128)(2,1)S(1)}, u32[]{:S(2)}, u32[]{:S(2)}) collective-permute-start(bf16[2,2,1,128,896]{4,3,2,1,0:T(8,128)(2,1)S(1)} %pad_maximum_fusion.19), channel_id=1, source_target_pairs={{0,4},{4,0},{8,12},{12,8},{1,5},{5,1},{9,13},{13,9},{2,6},{6,2},{1... | collective-permute-start | bytes 2752520 | tf_op jit(solution)/shard_map/ppermute | solution.py:188
  396.0 18.1 %collective-permute-start.35 = (bf16[1,2,2,128,896]{4,3,2,1,0:T(8,128)(2,1)S(1)}, bf16[1,2,2,128,896]{4,3,2,1,0:T(8,128)(2,1)S(1)}, u32[]{:S(2)}, u32[]{:S(2)}) collective-permute-start(bf16[1,2,2,128,896]{4,3,2,1,0:T(8,128)(2,1)S(1)} %pad_maximum_fusion.20), channel_id=1, source_target_pairs={{0,2},{1,3},{2,0},{3,1},{4,6},{5,7},{6,4},{7,5},{8,10},{9,11},{10,... | collective-permute-start | bytes 2752520 | tf_op jit(solution)/shard_map/ppermute | solution.py:188
  399.4 17.6 %collective-permute-start.29 = (bf16[1024,2560]{1,0:T(8,128)(2,1)S(1)}, bf16[1024,2560]{1,0:T(8,128)(2,1)S(1)}, u32[]{:S(2)}, u32[]{:S(2)}) collective-permute-start(bf16[1024,2560]{1,0:T(8,128)(2,1)S(1)} %bitcast.434), channel_id=1, source_target_pairs={{0,1},{1,0},{2,3},{3,2},{4,5},{5,4},{6,7},{7,6},{8,9},{9,8},{10,11... | collective-permute-start | bytes 15728648 | tf_op jit(solution)/shard_map/ppermute | solution.py:188
  471.6 25.4 %collective-permute-start.47 = (bf16[2,1,2,128,768]{4,3,2,1,0:T(8,128)(2,1)}, bf16[2,1,2,128,768]{4,3,2,1,0:T(8,128)(2,1)}, u32[]{:S(2)}, u32[]{:S(2)}) collective-permute-start(bf16[2,1,2,128,768]{4,3,2,1,0:T(8,128)(2,1)} %slice.519), channel_id=1, source_target_pairs={{0,16},{16,0},{1,17},{17,1},{2,18},{18,2},{3,19},{19,3},{4,20},{20... | collective-permute-start | bytes 2359304 | tf_op jit(solution)/shard_map/ppermute | solution.py:188
  472.1 26.8 %collective-permute-start.41 = (bf16[2,2,1,128,896]{4,3,2,1,0:T(8,128)(2,1)S(1)}, bf16[2,2,1,128,896]{4,3,2,1,0:T(8,128)(2,1)}, u32[]{:S(2)}, u32[]{:S(2)}) collective-permute-start(bf16[2,2,1,128,896]{4,3,2,1,0:T(8,128)(2,1)S(1)} %slice.507), channel_id=1, source_target_pairs={{0,4},{4,0},{8,12},{12,8},{1,5},{5,1},{9,13},{13,9},{2,6},{6,2},{1... | collective-permute-start | bytes 2752520 | tf_op jit(solution)/shard_map/ppermute | solution.py:188
  473.9 28.3 %collective-permute-start.44 = (bf16[1,2,2,128,896]{4,3,2,1,0:T(8,128)(2,1)S(1)}, bf16[1,2,2,128,896]{4,3,2,1,0:T(8,128)(2,1)}, u32[]{:S(2)}, u32[]{:S(2)}) collective-permute-start(bf16[1,2,2,128,896]{4,3,2,1,0:T(8,128)(2,1)S(1)} %slice.513), channel_id=1, source_target_pairs={{0,2},{1,3},{2,0},{3,1},{4,6},{5,7},{6,4},{7,5},{8,10},{9,11},{10,... | collective-permute-start | bytes 2752520 | tf_op jit(solution)/shard_map/ppermute | solution.py:188
  495.6 436.6 %reduce-scatter.5.cloned.1.call-start = ((), (), s32[]{:S(2)}) async-start(), calls=%async_computation.7 | async-start | bytes 3686400 | tf_op jit(solution)/shard_map/reduce_scatter | solution.py:727
  503.9 23.2 %collective-permute-start.45 = (bf16[1,2,1,128,896]{4,3,2,1,0:T(8,128)(2,1)S(1)}, bf16[1,2,1,128,896]{4,3,2,1,0:T(8,128)(2,1)S(1)}, u32[]{:S(2)}, u32[]{:S(2)}) collective-permute-start(bf16[1,2,1,128,896]{4,3,2,1,0:T(8,128)(2,1)S(1)} %slice.515), channel_id=1, source_target_pairs={{0,4},{4,0},{8,12},{12,8},{1,5},{5,1},{9,13},{13,9},{2,6},{6,2},{1... | collective-permute-start | bytes 1376264 | tf_op jit(solution)/shard_map/ppermute | solution.py:188
  509.3 23.8 %collective-permute-start.49 = (bf16[1,1,1,128,768]{4,3,2,1,0:T(8,128)(2,1)S(1)}, bf16[1,1,1,128,768]{4,3,2,1,0:T(8,128)(2,1)S(1)}, u32[]{:S(2)}, u32[]{:S(2)}) collective-permute-start(bf16[1,1,1,128,768]{4,3,2,1,0:T(8,128)(2,1)S(1)} %slice.523), channel_id=1, source_target_pairs={{0,4},{4,0},{8,12},{12,8},{1,5},{5,1},{9,13},{13,9},{2,6},{6,2},{1... | collective-permute-start | bytes 589832 | tf_op jit(solution)/shard_map/ppermute | solution.py:188
  512.5 20.6 %collective-permute-start.43 = (bf16[1,1,1,128,896]{4,3,2,1,0:T(8,128)(2,1)S(1)}, bf16[1,1,1,128,896]{4,3,2,1,0:T(8,128)(2,1)S(1)}, u32[]{:S(2)}, u32[]{:S(2)}) collective-permute-start(bf16[1,1,1,128,896]{4,3,2,1,0:T(8,128)(2,1)S(1)} %slice.511), channel_id=1, source_target_pairs={{0,2},{1,3},{2,0},{3,1},{4,6},{5,7},{6,4},{7,5},{8,10},{9,11},{10,... | collective-permute-start | bytes 688136 | tf_op jit(solution)/shard_map/ppermute | solution.py:188
  537.3 18.0 %collective-permute-start.62 = (bf16[128,2560]{1,0:T(8,128)(2,1)}, bf16[128,2560]{1,0:T(8,128)(2,1)}, u32[]{:S(2)}, u32[]{:S(2)}) collective-permute-start(bf16[128,2560]{1,0:T(8,128)(2,1)} %shard_map.268), channel_id=1, source_target_pairs={{0,2},{1,3},{2,0},{3,1},{4,6},{5,7},{6,4},{7,5},{8,10},{9,11},{10,... | collective-permute-start | bytes 1966088 | tf_op jit(solution)/shard_map/ppermute | solution.py:69
  546.4 35.1 %collective-permute-start.71 = (bf16[264,2560]{1,0:T(8,128)(2,1)}, bf16[264,2560]{1,0:T(8,128)(2,1)}, u32[]{:S(2)}, u32[]{:S(2)}) collective-permute-start(bf16[264,2560]{1,0:T(8,128)(2,1)} %shard_map.272), channel_id=1, source_target_pairs={{0,2},{1,3},{2,0},{3,1},{4,6},{5,7},{6,4},{7,5},{8,10},{9,11},{10,... | collective-permute-start | bytes 4055048 | tf_op jit(solution)/shard_map/ppermute | solution.py:69
  557.7 27.8 %collective-permute-start.63 = (bf16[2,128,2560]{2,1,0:T(8,128)(2,1)}, bf16[2,128,2560]{2,1,0:T(8,128)(2,1)}, u32[]{:S(2)}, u32[]{:S(2)}) collective-permute-start(bf16[2,128,2560]{2,1,0:T(8,128)(2,1)} %pad_maximum_fusion.11), channel_id=1, source_target_pairs={{0,1},{1,0},{2,3},{3,2},{4,5},{5,4},{6,7},{7,6},{8,9},{9,8},{10,11... | collective-permute-start | bytes 3932168 | tf_op jit(solution)/shard_map/ppermute | solution.py:69
  565.5 152.8 %collective-permute-start.50 = (bf16[1024,2560]{1,0:T(8,128)(2,1)}, bf16[1024,2560]{1,0:T(8,128)(2,1)}, u32[]{:S(2)}, u32[]{:S(2)}) collective-permute-start(bf16[1024,2560]{1,0:T(8,128)(2,1)} %shard_map.266), channel_id=1, source_target_pairs={{0,1},{1,0},{2,3},{3,2},{4,5},{5,4},{6,7},{7,6},{8,9},{9,8},{10,11... | collective-permute-start | bytes 15728648 | tf_op jit(solution)/shard_map/ppermute | solution.py:188
  585.4 130.5 %collective-permute-start.72 = (bf16[2,264,2560]{2,1,0:T(8,128)(2,1)}, bf16[2,264,2560]{2,1,0:T(8,128)(2,1)}, u32[]{:S(2)}, u32[]{:S(2)}) collective-permute-start(bf16[2,264,2560]{2,1,0:T(8,128)(2,1)} %pad_maximum_fusion.2), channel_id=1, source_target_pairs={{0,1},{1,0},{2,3},{3,2},{4,5},{5,4},{6,7},{7,6},{8,9},{9,8},{10,11... | collective-permute-start | bytes 8110088 | tf_op jit(solution)/shard_map/ppermute | solution.py:69
  621.9 20.0 %collective-permute-start.89 = (bf16[128,1280]{1,0:T(8,128)(2,1)}, bf16[128,1280]{1,0:T(8,128)(2,1)S(1)}, u32[]{:S(2)}, u32[]{:S(2)}) collective-permute-start(bf16[128,1280]{1,0:T(8,128)(2,1)} %select_convert_fusion.4), channel_id=1, source_target_pairs={{0,16},{16,0},{1,17},{17,1},{2,18},{18,2},{3,19},{19,3},{4,20},{20... | collective-permute-start | bytes 983048 | tf_op jit(solution)/shard_map/ppermute | solution.py:132
  624.1 21.2 %collective-permute-start.64 = (bf16[1,256,768]{2,1,0:T(8,128)(2,1)}, bf16[1,256,768]{2,1,0:T(8,128)(2,1)}, u32[]{:S(2)}, u32[]{:S(2)}) collective-permute-start(bf16[1,256,768]{2,1,0:T(8,128)(2,1)} %constant_dynamic-slice_fusion.10), channel_id=1, source_target_pairs={{0,1},{1,0},{2,3},{3,2},{4,5},{5,4},{6,7},{7,6},{8,9},{9,8},{10,11... | collective-permute-start | bytes 1179656 | tf_op jit(solution)/shard_map/ppermute | solution.py:69
  629.4 32.1 %collective-permute-start.85 = (bf16[384,960]{0,1:T(8,128)(2,1)}, bf16[384,960]{0,1:T(8,128)(2,1)}, u32[]{:S(2)}, u32[]{:S(2)}) collective-permute-start(bf16[384,960]{0,1:T(8,128)(2,1)} %copy.445), channel_id=1, source_target_pairs={{0,16},{16,0},{1,17},{17,1},{2,18},{18,2},{3,19},{19,3},{4,20},{20... | collective-permute-start | bytes 2211848 | tf_op jit(solution)/shard_map/ppermute | solution.py:132
  665.6 18.4 %collective-permute-start.88 = (bf16[96,960]{1,0:T(8,128)(2,1)S(1)}, bf16[96,960]{1,0:T(8,128)(2,1)S(1)}, u32[]{:S(2)}, u32[]{:S(2)}) collective-permute-start(bf16[96,960]{1,0:T(8,128)(2,1)S(1)} %get-tuple-element.202), channel_id=1, source_target_pairs={{0,12},{4,0},{8,4},{12,8},{1,13},{5,1},{9,5},{13,9},{2,14},{6,2},{... | collective-permute-start | bytes 552968 | tf_op jit(solution)/shard_map/ppermute | solution.py:83
  669.4 33.7 %collective-permute-start.87 = (bf16[96,960]{1,0:T(8,128)(2,1)S(1)}, bf16[96,960]{1,0:T(8,128)(2,1)S(1)}, u32[]{:S(2)}, u32[]{:S(2)}) collective-permute-start(bf16[96,960]{1,0:T(8,128)(2,1)S(1)} %get-tuple-element.203), channel_id=1, source_target_pairs={{0,8},{4,12},{8,0},{12,4},{1,9},{5,13},{9,1},{13,5},{2,10},{6,14},... | collective-permute-start | bytes 552968 | tf_op jit(solution)/shard_map/ppermute | solution.py:83
  679.3 24.6 %collective-permute-start.66 = (bf16[1,256,384]{2,1,0:T(8,128)(2,1)S(1)}, bf16[1,256,384]{2,1,0:T(8,128)(2,1)S(1)}, u32[]{:S(2)}, u32[]{:S(2)}) collective-permute-start(bf16[1,256,384]{2,1,0:T(8,128)(2,1)S(1)} %get-tuple-element.208), channel_id=1, source_target_pairs={{0,4},{4,8},{8,12},{12,0},{1,5},{5,9},{9,13},{13,1},{2,6},{6,10},{... | collective-permute-start | bytes 589832 | tf_op jit(solution)/shard_map/ppermute | solution.py:83
  684.0 19.9 %collective-permute-start.68 = (bf16[1,256,384]{2,1,0:T(8,128)(2,1)S(1)}, bf16[1,256,384]{2,1,0:T(8,128)(2,1)S(1)}, u32[]{:S(2)}, u32[]{:S(2)}) collective-permute-start(bf16[1,256,384]{2,1,0:T(8,128)(2,1)S(1)} %get-tuple-element.209), channel_id=1, source_target_pairs={{0,12},{4,0},{8,4},{12,8},{1,13},{5,1},{9,5},{13,9},{2,14},{6,2},{... | collective-permute-start | bytes 589832 | tf_op jit(solution)/shard_map/ppermute | solution.py:83
  727.8 19.7 %collective-permute-start.57 = (bf16[2,1,2,128,768]{4,3,2,1,0:T(8,128)(2,1)}, bf16[2,1,2,128,768]{4,3,2,1,0:T(8,128)(2,1)}, u32[]{:S(2)}, u32[]{:S(2)}) collective-permute-start(bf16[2,1,2,128,768]{4,3,2,1,0:T(8,128)(2,1)} %slice.537), channel_id=1, source_target_pairs={{0,16},{16,0},{1,17},{17,1},{2,18},{18,2},{3,19},{19,3},{4,20},{20... | collective-permute-start | bytes 2359304 | tf_op jit(solution)/shard_map/ppermute | solution.py:188
  727.9 28.9 %collective-permute-start.51 = (bf16[2,2,1,128,896]{4,3,2,1,0:T(8,128)(2,1)}, bf16[2,2,1,128,896]{4,3,2,1,0:T(8,128)(2,1)}, u32[]{:S(2)}, u32[]{:S(2)}) collective-permute-start(bf16[2,2,1,128,896]{4,3,2,1,0:T(8,128)(2,1)} %slice.525), channel_id=1, source_target_pairs={{0,4},{4,0},{8,12},{12,8},{1,5},{5,1},{9,13},{13,9},{2,6},{6,2},{1... | collective-permute-start | bytes 2752520 | tf_op jit(solution)/shard_map/ppermute | solution.py:188
  732.2 28.7 %collective-permute-start.54 = (bf16[1,2,2,128,896]{4,3,2,1,0:T(8,128)(2,1)}, bf16[1,2,2,128,896]{4,3,2,1,0:T(8,128)(2,1)}, u32[]{:S(2)}, u32[]{:S(2)}) collective-permute-start(bf16[1,2,2,128,896]{4,3,2,1,0:T(8,128)(2,1)} %slice.531), channel_id=1, source_target_pairs={{0,2},{1,3},{2,0},{3,1},{4,6},{5,7},{6,4},{7,5},{8,10},{9,11},{10,... | collective-permute-start | bytes 2752520 | tf_op jit(solution)/shard_map/ppermute | solution.py:188
  744.0 30.4 %collective-permute-start.73 = (bf16[1200,320]{0,1:T(8,128)(2,1)}, bf16[1200,320]{0,1:T(8,128)(2,1)}, u32[]{:S(2)}, u32[]{:S(2)}) collective-permute-start(bf16[1200,320]{0,1:T(8,128)(2,1)} %bitcast.123), channel_id=1, source_target_pairs={{0,4},{4,0},{8,12},{12,8},{16,20},{20,16},{24,28},{28,24},{1,5},{5... | collective-permute-start | bytes 2304008 | tf_op jit(solution)/shard_map/ppermute | solution.py:493
  746.0 30.1 %collective-permute-start.74 = (bf16[1200,320]{0,1:T(8,128)(2,1)}, bf16[1200,320]{0,1:T(8,128)(2,1)}, u32[]{:S(2)}, u32[]{:S(2)}) collective-permute-start(bf16[1200,320]{0,1:T(8,128)(2,1)} %bitcast.486), channel_id=1, source_target_pairs={{0,16},{4,20},{8,24},{12,28},{16,0},{20,4},{24,8},{28,12},{1,17},{... | collective-permute-start | bytes 2304008 | tf_op jit(solution)/shard_map/ppermute | solution.py:493
  747.5 45.3 %collective-permute-start.75 = (bf16[1200,320]{0,1:T(8,128)(2,1)}, bf16[1200,320]{0,1:T(8,128)(2,1)}, u32[]{:S(2)}, u32[]{:S(2)}) collective-permute-start(bf16[1200,320]{0,1:T(8,128)(2,1)} %bitcast.485), channel_id=1, source_target_pairs={{0,20},{4,16},{8,28},{12,24},{16,4},{20,0},{24,12},{28,8},{1,21},{... | collective-permute-start | bytes 2304008 | tf_op jit(solution)/shard_map/ppermute | solution.py:493
  756.8 47.8 %collective-permute-start.58 = (bf16[1,1,2,128,768]{4,3,2,1,0:T(8,128)(2,1)}, bf16[1,1,2,128,768]{4,3,2,1,0:T(8,128)(2,1)}, u32[]{:S(2)}, u32[]{:S(2)}) collective-permute-start(bf16[1,1,2,128,768]{4,3,2,1,0:T(8,128)(2,1)} %slice.539), channel_id=1, source_target_pairs={{0,2},{1,3},{2,0},{3,1},{4,6},{5,7},{6,4},{7,5},{8,10},{9,11},{10,... | collective-permute-start | bytes 1179656 | tf_op jit(solution)/shard_map/ppermute | solution.py:188
  761.0 46.2 %collective-permute-start.52 = (bf16[2,1,1,128,896]{4,3,2,1,0:T(8,128)(2,1)}, bf16[2,1,1,128,896]{4,3,2,1,0:T(8,128)(2,1)}, u32[]{:S(2)}, u32[]{:S(2)}) collective-permute-start(bf16[2,1,1,128,896]{4,3,2,1,0:T(8,128)(2,1)} %slice.527), channel_id=1, source_target_pairs={{0,16},{16,0},{1,17},{17,1},{2,18},{18,2},{3,19},{19,3},{4,20},{20... | collective-permute-start | bytes 1376264 | tf_op jit(solution)/shard_map/ppermute | solution.py:188
  774.3 35.5 %collective-permute-start.55 = (bf16[1,2,1,128,896]{4,3,2,1,0:T(8,128)(2,1)}, bf16[1,2,1,128,896]{4,3,2,1,0:T(8,128)(2,1)}, u32[]{:S(2)}, u32[]{:S(2)}) collective-permute-start(bf16[1,2,1,128,896]{4,3,2,1,0:T(8,128)(2,1)} %slice.533), channel_id=1, source_target_pairs={{0,4},{4,0},{8,12},{12,8},{1,5},{5,1},{9,13},{13,9},{2,6},{6,2},{1... | collective-permute-start | bytes 1376264 | tf_op jit(solution)/shard_map/ppermute | solution.py:188
  776.2 35.5 %collective-permute-start.69 = (bf16[1,256,1152]{2,1,0:T(8,128)(2,1)}, bf16[1,256,1152]{2,1,0:T(8,128)(2,1)}, u32[]{:S(2)}, u32[]{:S(2)}) collective-permute-start(bf16[1,256,1152]{2,1,0:T(8,128)(2,1)} %shard_map.270), channel_id=1, source_target_pairs={{0,2},{1,3},{2,0},{3,1},{4,6},{5,7},{6,4},{7,5},{8,10},{9,11},{10,... | collective-permute-start | bytes 1769480 | tf_op jit(solution)/shard_map/ppermute | solution.py:69
  854.1 34.0 %collective-permute-start.76 = (bf16[128,2560]{1,0:T(8,128)(2,1)}, bf16[128,2560]{1,0:T(8,128)(2,1)}, u32[]{:S(2)}, u32[]{:S(2)}) collective-permute-start(bf16[128,2560]{1,0:T(8,128)(2,1)} %get-tuple-element.188), channel_id=1, source_target_pairs={{0,2},{1,3},{2,0},{3,1},{4,6},{5,7},{6,4},{7,5},{8,10},{9,11},{10,... | collective-permute-start | bytes 1966088 | tf_op jit(solution)/shard_map/ppermute | solution.py:69
  856.0 29.5 %collective-permute-start.60 = (bf16[128,2560]{1,0:T(8,128)(2,1)}, bf16[128,2560]{1,0:T(8,128)(2,1)}, u32[]{:S(2)}, u32[]{:S(2)}) collective-permute-start(bf16[128,2560]{1,0:T(8,128)(2,1)} %get-tuple-element.189), channel_id=1, source_target_pairs={{0,2},{1,3},{2,0},{3,1},{4,6},{5,7},{6,4},{7,5},{8,10},{9,11},{10,... | collective-permute-start | bytes 1966088 | tf_op jit(solution)/shard_map/ppermute | solution.py:69
  859.5 30.9 %collective-permute-start.78 = (bf16[1280,264]{0,1:T(8,128)(2,1)}, bf16[1280,264]{0,1:T(8,128)(2,1)}, u32[]{:S(2)}, u32[]{:S(2)}) collective-permute-start(bf16[1280,264]{0,1:T(8,128)(2,1)} %select_convert_fusion.2), channel_id=1, source_target_pairs={{0,16},{16,0},{1,17},{17,1},{2,18},{18,2},{3,19},{19,3},{4,20},{20... | collective-permute-start | bytes 2027528 | tf_op jit(solution)/shard_map/ppermute | solution.py:132
  888.2 45.9 %collective-permute-start.61 = (bf16[2,128,2560]{2,1,0:T(8,128)(2,1)}, bf16[2,128,2560]{2,1,0:T(8,128)(2,1)}, u32[]{:S(2)}, u32[]{:S(2)}) collective-permute-start(bf16[2,128,2560]{2,1,0:T(8,128)(2,1)} %pad_maximum_fusion.10), channel_id=1, source_target_pairs={{0,1},{1,0},{2,3},{3,2},{4,5},{5,4},{6,7},{7,6},{8,9},{9,8},{10,11... | collective-permute-start | bytes 3932168 | tf_op jit(solution)/shard_map/ppermute | solution.py:69
  905.6 17.3 %collective-permute-start.79 = (bf16[4,80,264]{2,1,0:T(8,128)(2,1)}, bf16[4,80,264]{2,1,0:T(8,128)(2,1)}, u32[]{:S(2)}, u32[]{:S(2)}) collective-permute-start(bf16[4,80,264]{2,1,0:T(8,128)(2,1)} %bitcast.493), channel_id=1, source_target_pairs={{0,4},{4,8},{8,12},{12,0},{1,5},{5,9},{9,13},{13,1},{2,6},{6,10},{... | collective-permute-start | bytes 506888 | tf_op jit(solution)/shard_map/ppermute | solution.py:83
  908.4 30.3 %collective-permute-start.77 = (bf16[2,128,2560]{2,1,0:T(8,128)(2,1)}, bf16[2,128,2560]{2,1,0:T(8,128)(2,1)}, u32[]{:S(2)}, u32[]{:S(2)}) collective-permute-start(bf16[2,128,2560]{2,1,0:T(8,128)(2,1)} %pad_maximum_fusion.12), channel_id=1, source_target_pairs={{0,1},{1,0},{2,3},{3,2},{4,5},{5,4},{6,7},{7,6},{8,9},{9,8},{10,11... | collective-permute-start | bytes 3932168 | tf_op jit(solution)/shard_map/ppermute | solution.py:69
  (191 other events, 2614.2 us)
Sparse Core Ops, SparseCore 0:
  45.9 97.9 all-gather.3
  203.8 144.3 all-gather.5
  495.7 140.7 reduce-scatter.2
  640.4 101.5 reduce-scatter.4

commit v4 on v3

--- a/solution.py
+++ b/solution.py
@@ -596,7 +596,7 @@
     gain_latent = gains[:, 2 * cut + q_gain.shape[0] :].reshape(1, -1)
 
     down_part = gather_shard(small.reshape(-1, part), 0)
-    out_full = lax.all_gather(after(out_proj, small), ("shard", "ctx"), axis=1, tiled=True)
+    out_full = lax.all_gather(out_proj, ("shard", "ctx"), axis=1, tiled=True)
     hidden_weights = (gate_proj.T, up_proj.T, down_proj)
     if block_sized():
         pieces = hidden_pieces((after(gate_proj.T, small),) + hidden_weights[1:])

time: 964 us -> 962 us (level)
    ppermute x9, waiting for transfers between devices: 43.1 us -> 23.1 us  [from_ctx(): lax.ppermute(values, 'ctx', [((i + shift) % size, i) for i in range(size)])]
    all_to_all x1, waiting for transfers between devices: 1.82 us -> 16.1 us  [on_device(): lax.all_to_all(small.reshape(n_ctx * n_tp, block, part), ('ctx', 'tp'), 0...]
    unnamed x324 -> x319, local copies, waits for them, and re-layouts: 39.1 us -> 37.4 us
where the time goes in v4:
time: 962 us; the launch traced here: 947 us
  waiting for transfers between devices  378 us (39%)
  local copies, waits for them, and re-layouts  151 us (16%)
  other arithmetic  120 us (12%)
  starting transfers between devices  116 us (12%)
  matrix products  101 us (10%)
  Pallas kernels  63.9 us (7%)
  between operations  17.1 us (2%)
    dot_general x23, matrix products, dot(): lax.dot_general(left, right, (dims, ((), ())), preferred_element_type=f32)  97.7 us
    ppermute x40, waiting for transfers between devices, swap(): return lax.ppermute(values, axis, [(i, i ^ mask) for i in range(size)])  91.9 us
    ppermute x20, waiting for transfers between devices, tp_xor(): return lax.ppermute(values, 'tp', [(i, i ^ mask) for i in range(size)])  77.2 us
    all_gather x1, waiting for transfers between devices, hidden_gather(): return lax.all_gather(joined, 'ctx', axis_index_groups=far_groups(), axis=0)  67 us
    ppermute x12, waiting for transfers between devices, exchange_ctx(): lax.ppermute(send, 'ctx', [(i, (i + shift) % size) for i in range(size)])  61.5 us
    ppermute x40, starting transfers between devices, swap(): return lax.ppermute(values, axis, [(i, i ^ mask) for i in range(size)])  38.3 us
    unnamed x319, local copies, waits for them, and re-layouts  37.4 us
    pallas_call x1, Pallas kernels, attention_backward(): pl.pallas_call(functools.partial(backward_kernel, heads), grid=(seqs,), i...  23.8 us
  transfers between devices with their start and end apart: 100, of which 43 were waited for; matrix products, arithmetic and copies ran while one was open for 33% of the time, Pallas kernels for 7%

profile of v4, /device:TPU:0, one launch (start us, length us, event | category | flops | bytes accessed | tf_op | source)
XLA Modules:
  0.0 947.4 jit_solution(18431284296453256086)
XLA Ops:
  13.6 7.4 all-to-all-start
  33.3 6.6 broadcast_multiply_fusion
  39.9 16.1 %all-to-all-done.refs_1_ = bf16[16,80,264]{2,1,0:T(8,128)(2,1)S(1)} async-done(((bf16[16,80,264]{2,1,0:T(8,128)(2,1)}), bf16[16,80,264]{2,1,0:T(8,128)(2,1)S(1)}, u32[]{:S(2)}, u32[]{:S(2)}) %all-to-all-start) | async-done | bytes 675872 | tf_op jit(solution)/shard_map/all_to_all | solution.py:587
  56.9 6.9 all-to-all-start.1
  82.1 13.0 %collective-permute-done = bf16[1280,264]{0,1:T(8,128)(2,1)} collective-permute-done((bf16[1280,264]{0,1:T(8,128)(2,1)}, bf16[1280,264]{0,1:T(8,128)(2,1)}, u32[]{:S(2)}, u32[]{:S(2)}) %collective-permute-start) | collective-permute-done | bytes 675872 | tf_op jit(solution)/shard_map/ppermute | solution.py:118
  98.1 3.7 copy.374.refs_1_
  105.7 3.4 fusion.34
  111.8 16.8 %collective-permute-done.14 = bf16[32,1280]{1,0:T(8,128)(2,1)S(1)} collective-permute-done((bf16[32,1280]{1,0:T(8,128)(2,1)}, bf16[32,1280]{1,0:T(8,128)(2,1)S(1)}, u32[]{:S(2)}, u32[]{:S(2)}) %collective-permute-start.14) | collective-permute-done | bytes 81952 | tf_op jit(solution)/shard_map/ppermute | solution.py:74
  130.2 11.8 %collective-permute-done.1 = f32[512,264]{0,1:T(8,128)S(1)} collective-permute-done((f32[512,264]{0,1:T(8,128)S(1)}, f32[512,264]{0,1:T(8,128)S(1)}, u32[]{:S(2)}, u32[]{:S(2)}) %collective-permute-start.1) | collective-permute-done | bytes 540704 | tf_op jit(solution)/shard_map/ppermute | solution.py:69
  158.2 6.3 collective-permute-done.4
  186.9 3.0 slice_bitcast_fusion
  194.0 4.1 multiply_convert_fusion.9
  202.3 5.4 collective-permute-done.6
  214.4 3.8 convolution_convert_fusion.2.kv_ref
  218.2 14.4 %shard_map.262 = (bf16[2,256,640]{2,1,0:T(8,128)(2,1)S(1)}, f32[2,256,128]{2,1,0:T(8,128)S(1)}) custom-call(f32[2,256,960]{2,1,0:T(8,128)} %fusion.22.q_ref, bf16[2,1024,1280]{2,1,0:T(8,128)(2,1)} %convolution_convert_fusion.2.kv_ref, bf16[2,1024,128]{2,1,0:T(8,128)(2,1)S(1)} %pad_maximum_fusion.25.rotary_ref, ...), custom_call_target="tpu_custom_call" | custom-call | flops 2684354560 | bytes 12000000 | tf_op jit(solution)/shard_map/pallas_call | solution.py:290
  232.7 4.5 fusion
  237.5 3.0 collective-permute-done.18
  245.5 14.1 %collective-permute-done.19 = bf16[128,2560]{1,0:T(8,128)(2,1)S(1)} collective-permute-done((bf16[128,2560]{1,0:T(8,128)(2,1)S(1)}, bf16[128,2560]{1,0:T(8,128)(2,1)S(1)}, u32[]{:S(2)}, u32[]{:S(2)}) %collective-permute-start.19) | collective-permute-done | bytes 655392 | tf_op jit(solution)/shard_map/ppermute | solution.py:69
  266.7 7.6 collective-permute-done.26
  278.8 67.0 %all-gather.6.cloned.1.call-done = bf16[2400,1280]{1,0:T(8,128)(2,1)} async-done(((bf16[1200,1280]{1,0:T(8,128)(2,1)}), bf16[2400,1280]{1,0:T(8,128)(2,1)}) %all-gather.6.cloned.1.call-update) | async-done | bytes 6144016 | tf_op jit(solution)/shard_map/all_gather | solution.py:512
  350.2 9.2 collective-permute-done.21
  366.6 23.2 %collective-permute-done.31 = bf16[2,1,1,128,896]{4,3,2,1,0:T(8,128)(2,1)S(1)} collective-permute-done((bf16[2,1,1,128,896]{4,3,2,1,0:T(8,128)(2,1)S(1)}, bf16[2,1,1,128,896]{4,3,2,1,0:T(8,128)(2,1)S(1)}, u32[]{:S(2)}, u32[]{:S(2)}) %collective-permute-start.31) | collective-permute-done | bytes 458784 | tf_op jit(solution)/shard_map/ppermute | solution.py:188
  397.0 9.6 %collective-permute-done.38 = bf16[2,1,2,128,768]{4,3,2,1,0:T(8,128)(2,1)S(1)} collective-permute-done((bf16[2,1,2,128,768]{4,3,2,1,0:T(8,128)(2,1)S(1)}, bf16[2,1,2,128,768]{4,3,2,1,0:T(8,128)(2,1)S(1)}, u32[]{:S(2)}, u32[]{:S(2)}) %collective-permute-start.38) | collective-permute-done | bytes 786464 | tf_op jit(solution)/shard_map/ppermute | solution.py:188
  406.6 4.2 collective-permute-done.32
  421.0 5.3 fusion.5
  426.4 7.2 fusion.36
  433.5 8.9 add_convert_fusion.2
  447.4 2.9 fusion.14
  450.3 7.2 fusion.35
  457.5 8.6 add_convert_fusion.1
  472.7 19.9 %shard_map.266.refs_1_ = bf16[2,1200,1280]{2,1,0:T(8,128)(2,1)} custom-call(bf16[1024,2560]{1,0:T(8,128)(2,1)} %bitcast.437, bf16[1024,2560]{1,0:T(8,128)(2,1)} %copy-done.137, bf16[1024,2560]{1,0:T(8,128)(2,1)} %bitcast.439, bf16[1024,2560]{1,0:T(8,128)(2,1)} %collective-permute-done.39.refs_3_, bf16[400,1024]{1,0:T(8,128)(2,1)S(1)} %get-tuple-element.167.refs_4_, ...), custom_call_target="tpu_custom_call" | custom-call | flops 12582912000 | bytes 33000000 | tf_op jit(solution)/shard_map/pallas_call | solution.py:388
  501.6 4.6 collective-permute-done.48
  511.4 12.8 %collective-permute-done.45 = bf16[1,2,1,128,896]{4,3,2,1,0:T(8,128)(2,1)S(1)} collective-permute-done((bf16[1,2,1,128,896]{4,3,2,1,0:T(8,128)(2,1)S(1)}, bf16[1,2,1,128,896]{4,3,2,1,0:T(8,128)(2,1)S(1)}, u32[]{:S(2)}, u32[]{:S(2)}) %collective-permute-start.45) | collective-permute-done | bytes 458784 | tf_op jit(solution)/shard_map/ppermute | solution.py:188
  525.3 4.9 collective-permute-done.49
  545.4 6.9 collective-permute-done.62
  554.8 7.2 convolution_convert_fusion.refs_0_
  563.1 15.5 %collective-permute-done.71 = bf16[264,2560]{1,0:T(8,128)(2,1)} collective-permute-done((bf16[264,2560]{1,0:T(8,128)(2,1)}, bf16[264,2560]{1,0:T(8,128)(2,1)}, u32[]{:S(2)}, u32[]{:S(2)}) %collective-permute-start.71) | collective-permute-done | bytes 1351712 | tf_op jit(solution)/shard_map/ppermute | solution.py:69
  587.1 3.0 convolution_convert_fusion.6
  590.1 23.8 %shard_map.268 = (bf16[2,256,960]{2,1,0:T(8,128)(2,1)}, bf16[2,1024,1280]{2,1,0:T(8,128)(2,1)}, f32[2,1024,128]{2,1,0:T(8,128)}) custom-call(f32[2,256,960]{2,1,0:T(8,128)} %fusion.22.q_ref, bf16[2,1024,1280]{2,1,0:T(8,128)(2,1)} %convolution_convert_fusion.2.kv_ref, bf16[2,1024,128]{2,1,0:T(8,128)(2,1)} %copy-done.8, f32[3,256,128]{2,1,0:T(8,128)} %copy-done.9, ...), custom_call_target="tpu_custom_call" | custom-call | flops 6710886400 | bytes 20000000 | tf_op jit(solution)/shard_map/pallas_call | solution.py:338
  614.0 4.2 convolution_bitcast_fusion
  628.1 5.7 convolution_convert_fusion.3
  634.9 4.0 convolution_convert_fusion.4
  650.2 7.5 collective-permute-done.91
  662.5 3.8 collective-permute-start.88
  667.8 8.4 collective-permute-done.86
  676.3 3.7 collective-permute-start.66
  680.8 3.4 collective-permute-start.68
  684.2 15.8 %collective-permute-done.87 = bf16[96,960]{1,0:T(8,128)(2,1)S(1)} collective-permute-done((bf16[96,960]{1,0:T(8,128)(2,1)S(1)}, bf16[96,960]{1,0:T(8,128)(2,1)S(1)}, u32[]{:S(2)}, u32[]{:S(2)}) %collective-permute-start.87) | collective-permute-done | bytes 184352 | tf_op jit(solution)/shard_map/ppermute | solution.py:83
  700.9 11.1 %collective-permute-done.67 = bf16[1,256,384]{2,1,0:T(8,128)(2,1)S(1)} collective-permute-done((bf16[1,256,384]{2,1,0:T(8,128)(2,1)S(1)}, bf16[1,256,384]{2,1,0:T(8,128)(2,1)S(1)}, u32[]{:S(2)}, u32[]{:S(2)}) %collective-permute-start.67) | collective-permute-done | bytes 196640 | tf_op jit(solution)/shard_map/ppermute | solution.py:83
  716.4 5.9 add_convert_fusion
  725.5 2.8 copy.410
  747.0 6.8 collective-permute-done.51
  762.0 9.3 collective-permute-done.73
  776.8 13.1 %collective-permute-done.75 = bf16[1200,320]{0,1:T(8,128)(2,1)} collective-permute-done((bf16[1200,320]{0,1:T(8,128)(2,1)}, bf16[1200,320]{0,1:T(8,128)(2,1)}, u32[]{:S(2)}, u32[]{:S(2)}) %collective-permute-start.75) | collective-permute-done | bytes 768032 | tf_op jit(solution)/shard_map/ppermute | solution.py:493
  793.3 3.8 shard_map.274
  798.5 3.1 copy.437
  837.5 5.2 multiply_reduce_fusion.4
  843.5 3.3 all-to-all-start.2
  846.9 4.3 reduce-precision_convert_fusion
  860.3 22.3 %collective-permute-done.60 = bf16[128,2560]{1,0:T(8,128)(2,1)} collective-permute-done((bf16[128,2560]{1,0:T(8,128)(2,1)}, bf16[128,2560]{1,0:T(8,128)(2,1)}, u32[]{:S(2)}, u32[]{:S(2)}) %collective-permute-start.60) | collective-permute-done | bytes 655392 | tf_op jit(solution)/shard_map/ppermute | solution.py:69
  889.9 3.7 reshape.432
  905.9 8.0 collective-permute-done.80
  913.9 6.1 collective-permute-done.79
  933.0 2.8 copy.401
  (791 shorter events, 358.5 us)
Async XLA Ops:
  7.2 225.5 %all-gather.4.cloned.1.call-start = ((), (), s32[]{:S(2)}) async-start(), calls=%async_computation.5 | async-start | bytes 3686400 | tf_op jit(solution)/shard_map/all_gather | solution.py:599
  13.6 42.4 %all-to-all-start = ((bf16[16,80,264]{2,1,0:T(8,128)(2,1)}), bf16[16,80,264]{2,1,0:T(8,128)(2,1)S(1)}, u32[]{:S(2)}, u32[]{:S(2)}) async-start(bf16[16,80,264]{2,1,0:T(8,128)(2,1)} %bitcast.5), calls=%async_computation | async-start | bytes 1966080 | tf_op jit(solution)/shard_map/all_to_all | solution.py:587
  56.9 22.7 %all-to-all-start.1 = ((bf16[32,1,192]{2,1,0:T(2,128)(2,1)}), bf16[32,1,192]{2,1,0:T(2,128)(2,1)}, u32[]{:S(2)}, u32[]{:S(2)}) async-start(bf16[32,1,192]{2,1,0:T(2,128)(2,1)} %shard_map.254), calls=%async_computation.1 | async-start | bytes 65536 | tf_op jit(solution)/shard_map/all_to_all | solution.py:588
  63.9 281.9 %all-gather.6.cloned.1.call-start = ((), (), s32[]{:S(2)}) async-start(), calls=%async_computation.8 | async-start | bytes 9216000 | tf_op jit(solution)/shard_map/all_gather | solution.py:512
  66.1 29.0 %collective-permute-start = (bf16[1280,264]{0,1:T(8,128)(2,1)}, bf16[1280,264]{0,1:T(8,128)(2,1)}, u32[]{:S(2)}, u32[]{:S(2)}) collective-permute-start(bf16[1280,264]{0,1:T(8,128)(2,1)} %copy.444), channel_id=1, source_target_pairs={{0,16},{16,0},{1,17},{17,1},{2,18},{18,2},{3,19},{19,3},{4,20},{20... | collective-permute-start | bytes 2027528 | tf_op jit(solution)/shard_map/ppermute | solution.py:118
  76.2 69.8 %collective-permute-start.7 = (bf16[1200,320]{0,1:T(8,128)(2,1)}, bf16[1200,320]{0,1:T(8,128)(2,1)}, u32[]{:S(2)}, u32[]{:S(2)}) collective-permute-start(bf16[1200,320]{0,1:T(8,128)(2,1)} %bitcast.29), channel_id=1, source_target_pairs={{0,4},{4,0},{8,12},{12,8},{16,20},{20,16},{24,28},{28,24},{1,5},{5... | collective-permute-start | bytes 2304008 | tf_op jit(solution)/shard_map/ppermute | solution.py:493
  77.7 70.7 %collective-permute-start.8 = (bf16[1200,320]{0,1:T(8,128)(2,1)}, bf16[1200,320]{0,1:T(8,128)(2,1)}, u32[]{:S(2)}, u32[]{:S(2)}) collective-permute-start(bf16[1200,320]{0,1:T(8,128)(2,1)} %bitcast.484), channel_id=1, source_target_pairs={{0,16},{4,20},{8,24},{12,28},{16,0},{20,4},{24,8},{28,12},{1,17},{... | collective-permute-start | bytes 2304008 | tf_op jit(solution)/shard_map/ppermute | solution.py:493
  78.3 73.5 %collective-permute-start.9 = (bf16[1200,320]{0,1:T(8,128)(2,1)}, bf16[1200,320]{0,1:T(8,128)(2,1)}, u32[]{:S(2)}, u32[]{:S(2)}) collective-permute-start(bf16[1200,320]{0,1:T(8,128)(2,1)} %bitcast.483), channel_id=1, source_target_pairs={{0,20},{4,16},{8,28},{12,24},{16,4},{20,0},{24,12},{28,8},{1,21},{... | collective-permute-start | bytes 2304008 | tf_op jit(solution)/shard_map/ppermute | solution.py:493
  101.8 28.2 %collective-permute-start.15 = (bf16[32,1280]{1,0:T(8,128)(2,1)}, bf16[32,1280]{1,0:T(8,128)(2,1)S(1)}, u32[]{:S(2)}, u32[]{:S(2)}) collective-permute-start(bf16[32,1280]{1,0:T(8,128)(2,1)} %shard_map.260), channel_id=1, source_target_pairs={{8,0},{12,4},{0,8},{4,12},{9,1},{13,5},{1,9},{5,13},{10,2},{14,6},... | collective-permute-start | bytes 245768 | tf_op jit(solution)/shard_map/ppermute | solution.py:74
  104.3 24.3 %collective-permute-start.14 = (bf16[32,1280]{1,0:T(8,128)(2,1)}, bf16[32,1280]{1,0:T(8,128)(2,1)S(1)}, u32[]{:S(2)}, u32[]{:S(2)}) collective-permute-start(bf16[32,1280]{1,0:T(8,128)(2,1)} %shard_map.260), channel_id=1, source_target_pairs={{4,0},{8,4},{12,8},{0,12},{5,1},{9,5},{13,9},{1,13},{6,2},{10,6},{... | collective-permute-start | bytes 245768 | tf_op jit(solution)/shard_map/ppermute | solution.py:74
  145.9 21.8 %collective-permute-start.2 = (f32[2,512,264]{1,2,0:T(8,128)}, f32[2,512,264]{1,2,0:T(8,128)}, u32[]{:S(2)}, u32[]{:S(2)}) collective-permute-start(f32[2,512,264]{1,2,0:T(8,128)} %pad_maximum_fusion.14), channel_id=1, source_target_pairs={{0,1},{1,0},{2,3},{3,2},{4,5},{5,4},{6,7},{7,6},{8,9},{9,8},{10,11... | collective-permute-start | bytes 3244040 | tf_op jit(solution)/shard_map/ppermute | solution.py:69
  146.7 19.5 %collective-permute-start.5 = (bf16[96,960]{1,0:T(8,128)(2,1)}, bf16[96,960]{1,0:T(8,128)(2,1)}, u32[]{:S(2)}, u32[]{:S(2)}) collective-permute-start(bf16[96,960]{1,0:T(8,128)(2,1)} %shard_map.255), channel_id=1, source_target_pairs={{12,0},{0,4},{4,8},{8,12},{13,1},{1,5},{5,9},{9,13},{14,2},{2,6},{... | collective-permute-start | bytes 552968 | tf_op jit(solution)/shard_map/ppermute | solution.py:74
  176.8 23.4 %collective-permute-start.12 = (bf16[1,256,384]{2,1,0:T(8,128)(2,1)}, bf16[1,256,384]{2,1,0:T(8,128)(2,1)S(1)}, u32[]{:S(2)}, u32[]{:S(2)}) collective-permute-start(bf16[1,256,384]{2,1,0:T(8,128)(2,1)} %shard_map.259), channel_id=1, source_target_pairs={{12,0},{0,4},{4,8},{8,12},{13,1},{1,5},{5,9},{9,13},{14,2},{2,6},{... | collective-permute-start | bytes 589832 | tf_op jit(solution)/shard_map/ppermute | solution.py:74
  176.8 22.4 %collective-permute-start.11 = (bf16[1,256,384]{2,1,0:T(8,128)(2,1)}, bf16[1,256,384]{2,1,0:T(8,128)(2,1)}, u32[]{:S(2)}, u32[]{:S(2)}) collective-permute-start(bf16[1,256,384]{2,1,0:T(8,128)(2,1)} %shard_map.259), channel_id=1, source_target_pairs={{8,0},{12,4},{0,8},{4,12},{9,1},{13,5},{1,9},{5,13},{10,2},{14,6},... | collective-permute-start | bytes 589832 | tf_op jit(solution)/shard_map/ppermute | solution.py:74
  177.9 20.3 %collective-permute-start.10 = (bf16[1,256,384]{2,1,0:T(8,128)(2,1)}, bf16[1,256,384]{2,1,0:T(8,128)(2,1)}, u32[]{:S(2)}, u32[]{:S(2)}) collective-permute-start(bf16[1,256,384]{2,1,0:T(8,128)(2,1)} %shard_map.259), channel_id=1, source_target_pairs={{4,0},{8,4},{12,8},{0,12},{5,1},{9,5},{13,9},{1,13},{6,2},{10,6},{... | collective-permute-start | bytes 589832 | tf_op jit(solution)/shard_map/ppermute | solution.py:74
  182.6 18.7 %collective-permute-start.17 = (bf16[128,1280]{1,0:T(8,128)(2,1)S(1)}, bf16[128,1280]{1,0:T(8,128)(2,1)}, u32[]{:S(2)}, u32[]{:S(2)}) collective-permute-start(bf16[128,1280]{1,0:T(8,128)(2,1)S(1)} %copy-done.73), channel_id=1, source_target_pairs={{0,16},{16,0},{1,17},{17,1},{2,18},{18,2},{3,19},{19,3},{4,20},{20... | collective-permute-start | bytes 983048 | tf_op jit(solution)/shard_map/ppermute | solution.py:118
  185.5 22.1 %collective-permute-start.6 = (bf16[384,960]{0,1:T(8,128)(2,1)}, bf16[384,960]{0,1:T(8,128)(2,1)}, u32[]{:S(2)}, u32[]{:S(2)}) collective-permute-start(bf16[384,960]{0,1:T(8,128)(2,1)} %copy.375), channel_id=1, source_target_pairs={{0,16},{16,0},{1,17},{17,1},{2,18},{18,2},{3,19},{19,3},{4,20},{20... | collective-permute-start | bytes 2211848 | tf_op jit(solution)/shard_map/ppermute | solution.py:118
  201.2 530.3 %reduce-scatter.3.cloned.1.call-start = ((), (), s32[]{:S(2)}) async-start(), calls=%async_computation.6 | async-start | bytes 9216000 | tf_op jit(solution)/shard_map/reduce_scatter | solution.py:714
  263.7 85.1 %collective-permute-start.36 = (bf16[1,1,1,128,768]{4,3,2,1,0:T(8,128)(2,1)S(1)}, bf16[1,1,1,128,768]{4,3,2,1,0:T(8,128)(2,1)S(1)}, u32[]{:S(2)}, u32[]{:S(2)}) collective-permute-start(bf16[1,1,1,128,768]{4,3,2,1,0:T(8,128)(2,1)S(1)} %slice_bitcast_fusion.18), channel_id=1, source_target_pairs={{0,4},{4,0},{8,12},{12,8},{1,5},{5,1},{9,13},{13,9},{2,6},{6,2},{1... | collective-permute-start | bytes 589832 | tf_op jit(solution)/shard_map/ppermute | solution.py:188
  275.0 85.9 %collective-permute-start.27 = (bf16[1,1,2,128,768]{4,3,2,1,0:T(8,128)(2,1)}, bf16[1,1,2,128,768]{4,3,2,1,0:T(8,128)(2,1)}, u32[]{:S(2)}, u32[]{:S(2)}) collective-permute-start(bf16[1,1,2,128,768]{4,3,2,1,0:T(8,128)(2,1)} %pad_maximum_fusion.33), channel_id=1, source_target_pairs={{0,2},{1,3},{2,0},{3,1},{4,6},{5,7},{6,4},{7,5},{8,10},{9,11},{10,... | collective-permute-start | bytes 1179656 | tf_op jit(solution)/shard_map/ppermute | solution.py:188
  277.3 72.2 %collective-permute-start.24 = (bf16[1,2,1,128,896]{4,3,2,1,0:T(8,128)(2,1)}, bf16[1,2,1,128,896]{4,3,2,1,0:T(8,128)(2,1)S(1)}, u32[]{:S(2)}, u32[]{:S(2)}) collective-permute-start(bf16[1,2,1,128,896]{4,3,2,1,0:T(8,128)(2,1)} %pad_maximum_fusion.27), channel_id=1, source_target_pairs={{0,4},{4,0},{8,12},{12,8},{1,5},{5,1},{9,13},{13,9},{2,6},{6,2},{1... | collective-permute-start | bytes 1376264 | tf_op jit(solution)/shard_map/ppermute | solution.py:188
  359.4 34.8 %collective-permute-start.25 = (bf16[1,2,2,128,896]{4,3,2,1,0:T(8,128)(2,1)S(1)}, bf16[1,2,2,128,896]{4,3,2,1,0:T(8,128)(2,1)S(1)}, u32[]{:S(2)}, u32[]{:S(2)}) collective-permute-start(bf16[1,2,2,128,896]{4,3,2,1,0:T(8,128)(2,1)S(1)} %pad_maximum_fusion.18), channel_id=1, source_target_pairs={{0,2},{1,3},{2,0},{3,1},{4,6},{5,7},{6,4},{7,5},{8,10},{9,11},{10,... | collective-permute-start | bytes 2752520 | tf_op jit(solution)/shard_map/ppermute | solution.py:188
  361.0 33.2 %collective-permute-start.22 = (bf16[2,2,1,128,896]{4,3,2,1,0:T(8,128)(2,1)S(1)}, bf16[2,2,1,128,896]{4,3,2,1,0:T(8,128)(2,1)S(1)}, u32[]{:S(2)}, u32[]{:S(2)}) collective-permute-start(bf16[2,2,1,128,896]{4,3,2,1,0:T(8,128)(2,1)S(1)} %pad_maximum_fusion.17), channel_id=1, source_target_pairs={{0,4},{4,0},{8,12},{12,8},{1,5},{5,1},{9,13},{13,9},{2,6},{6,2},{1... | collective-permute-start | bytes 2752520 | tf_op jit(solution)/shard_map/ppermute | solution.py:188
  362.2 31.4 %collective-permute-start.28 = (bf16[2,1,2,128,768]{4,3,2,1,0:T(8,128)(2,1)S(1)}, bf16[2,1,2,128,768]{4,3,2,1,0:T(8,128)(2,1)S(1)}, u32[]{:S(2)}, u32[]{:S(2)}) collective-permute-start(bf16[2,1,2,128,768]{4,3,2,1,0:T(8,128)(2,1)S(1)} %pad_maximum_fusion.21), channel_id=1, source_target_pairs={{0,16},{16,0},{1,17},{17,1},{2,18},{18,2},{3,19},{19,3},{4,20},{20... | collective-permute-start | bytes 2359304 | tf_op jit(solution)/shard_map/ppermute | solution.py:188
  363.9 25.9 %collective-permute-start.31 = (bf16[2,1,1,128,896]{4,3,2,1,0:T(8,128)(2,1)S(1)}, bf16[2,1,1,128,896]{4,3,2,1,0:T(8,128)(2,1)S(1)}, u32[]{:S(2)}, u32[]{:S(2)}) collective-permute-start(bf16[2,1,1,128,896]{4,3,2,1,0:T(8,128)(2,1)S(1)} %pad_maximum_fusion.28), channel_id=1, source_target_pairs={{0,16},{16,0},{1,17},{17,1},{2,18},{18,2},{3,19},{19,3},{4,20},{20... | collective-permute-start | bytes 1376264 | tf_op jit(solution)/shard_map/ppermute | solution.py:188
  365.4 25.9 %collective-permute-start.34 = (bf16[1,2,1,128,896]{4,3,2,1,0:T(8,128)(2,1)S(1)}, bf16[1,2,1,128,896]{4,3,2,1,0:T(8,128)(2,1)S(1)}, u32[]{:S(2)}, u32[]{:S(2)}) collective-permute-start(bf16[1,2,1,128,896]{4,3,2,1,0:T(8,128)(2,1)S(1)} %pad_maximum_fusion.29), channel_id=1, source_target_pairs={{0,4},{4,0},{8,12},{12,8},{1,5},{5,1},{9,13},{13,9},{2,6},{6,2},{1... | collective-permute-start | bytes 1376264 | tf_op jit(solution)/shard_map/ppermute | solution.py:188
  391.4 19.4 %collective-permute-start.32 = (bf16[2,2,1,128,896]{4,3,2,1,0:T(8,128)(2,1)S(1)}, bf16[2,2,1,128,896]{4,3,2,1,0:T(8,128)(2,1)S(1)}, u32[]{:S(2)}, u32[]{:S(2)}) collective-permute-start(bf16[2,2,1,128,896]{4,3,2,1,0:T(8,128)(2,1)S(1)} %pad_maximum_fusion.19), channel_id=1, source_target_pairs={{0,4},{4,0},{8,12},{12,8},{1,5},{5,1},{9,13},{13,9},{2,6},{6,2},{1... | collective-permute-start | bytes 2752520 | tf_op jit(solution)/shard_map/ppermute | solution.py:188
  393.5 18.1 %collective-permute-start.35 = (bf16[1,2,2,128,896]{4,3,2,1,0:T(8,128)(2,1)S(1)}, bf16[1,2,2,128,896]{4,3,2,1,0:T(8,128)(2,1)S(1)}, u32[]{:S(2)}, u32[]{:S(2)}) collective-permute-start(bf16[1,2,2,128,896]{4,3,2,1,0:T(8,128)(2,1)S(1)} %pad_maximum_fusion.20), channel_id=1, source_target_pairs={{0,2},{1,3},{2,0},{3,1},{4,6},{5,7},{6,4},{7,5},{8,10},{9,11},{10,... | collective-permute-start | bytes 2752520 | tf_op jit(solution)/shard_map/ppermute | solution.py:188
  397.0 17.6 %collective-permute-start.29 = (bf16[1024,2560]{1,0:T(8,128)(2,1)S(1)}, bf16[1024,2560]{1,0:T(8,128)(2,1)S(1)}, u32[]{:S(2)}, u32[]{:S(2)}) collective-permute-start(bf16[1024,2560]{1,0:T(8,128)(2,1)S(1)} %bitcast.434), channel_id=1, source_target_pairs={{0,1},{1,0},{2,3},{3,2},{4,5},{5,4},{6,7},{7,6},{8,9},{9,8},{10,11... | collective-permute-start | bytes 15728648 | tf_op jit(solution)/shard_map/ppermute | solution.py:188
  468.7 25.3 %collective-permute-start.47 = (bf16[2,1,2,128,768]{4,3,2,1,0:T(8,128)(2,1)}, bf16[2,1,2,128,768]{4,3,2,1,0:T(8,128)(2,1)}, u32[]{:S(2)}, u32[]{:S(2)}) collective-permute-start(bf16[2,1,2,128,768]{4,3,2,1,0:T(8,128)(2,1)} %slice.519), channel_id=1, source_target_pairs={{0,16},{16,0},{1,17},{17,1},{2,18},{18,2},{3,19},{19,3},{4,20},{20... | collective-permute-start | bytes 2359304 | tf_op jit(solution)/shard_map/ppermute | solution.py:188
  469.2 26.7 %collective-permute-start.41 = (bf16[2,2,1,128,896]{4,3,2,1,0:T(8,128)(2,1)S(1)}, bf16[2,2,1,128,896]{4,3,2,1,0:T(8,128)(2,1)}, u32[]{:S(2)}, u32[]{:S(2)}) collective-permute-start(bf16[2,2,1,128,896]{4,3,2,1,0:T(8,128)(2,1)S(1)} %slice.507), channel_id=1, source_target_pairs={{0,4},{4,0},{8,12},{12,8},{1,5},{5,1},{9,13},{13,9},{2,6},{6,2},{1... | collective-permute-start | bytes 2752520 | tf_op jit(solution)/shard_map/ppermute | solution.py:188
  471.0 28.3 %collective-permute-start.44 = (bf16[1,2,2,128,896]{4,3,2,1,0:T(8,128)(2,1)S(1)}, bf16[1,2,2,128,896]{4,3,2,1,0:T(8,128)(2,1)}, u32[]{:S(2)}, u32[]{:S(2)}) collective-permute-start(bf16[1,2,2,128,896]{4,3,2,1,0:T(8,128)(2,1)S(1)} %slice.513), channel_id=1, source_target_pairs={{0,2},{1,3},{2,0},{3,1},{4,6},{5,7},{6,4},{7,5},{8,10},{9,11},{10,... | collective-permute-start | bytes 2752520 | tf_op jit(solution)/shard_map/ppermute | solution.py:188
  492.6 436.6 %reduce-scatter.5.cloned.1.call-start = ((), (), s32[]{:S(2)}) async-start(), calls=%async_computation.7 | async-start | bytes 3686400 | tf_op jit(solution)/shard_map/reduce_scatter | solution.py:727
  501.0 23.2 %collective-permute-start.45 = (bf16[1,2,1,128,896]{4,3,2,1,0:T(8,128)(2,1)S(1)}, bf16[1,2,1,128,896]{4,3,2,1,0:T(8,128)(2,1)S(1)}, u32[]{:S(2)}, u32[]{:S(2)}) collective-permute-start(bf16[1,2,1,128,896]{4,3,2,1,0:T(8,128)(2,1)S(1)} %slice.515), channel_id=1, source_target_pairs={{0,4},{4,0},{8,12},{12,8},{1,5},{5,1},{9,13},{13,9},{2,6},{6,2},{1... | collective-permute-start | bytes 1376264 | tf_op jit(solution)/shard_map/ppermute | solution.py:188
  506.3 23.8 %collective-permute-start.49 = (bf16[1,1,1,128,768]{4,3,2,1,0:T(8,128)(2,1)S(1)}, bf16[1,1,1,128,768]{4,3,2,1,0:T(8,128)(2,1)S(1)}, u32[]{:S(2)}, u32[]{:S(2)}) collective-permute-start(bf16[1,1,1,128,768]{4,3,2,1,0:T(8,128)(2,1)S(1)} %slice.523), channel_id=1, source_target_pairs={{0,4},{4,0},{8,12},{12,8},{1,5},{5,1},{9,13},{13,9},{2,6},{6,2},{1... | collective-permute-start | bytes 589832 | tf_op jit(solution)/shard_map/ppermute | solution.py:188
  509.6 20.6 %collective-permute-start.43 = (bf16[1,1,1,128,896]{4,3,2,1,0:T(8,128)(2,1)S(1)}, bf16[1,1,1,128,896]{4,3,2,1,0:T(8,128)(2,1)S(1)}, u32[]{:S(2)}, u32[]{:S(2)}) collective-permute-start(bf16[1,1,1,128,896]{4,3,2,1,0:T(8,128)(2,1)S(1)} %slice.511), channel_id=1, source_target_pairs={{0,2},{1,3},{2,0},{3,1},{4,6},{5,7},{6,4},{7,5},{8,10},{9,11},{10,... | collective-permute-start | bytes 688136 | tf_op jit(solution)/shard_map/ppermute | solution.py:188
  534.4 18.0 %collective-permute-start.62 = (bf16[128,2560]{1,0:T(8,128)(2,1)}, bf16[128,2560]{1,0:T(8,128)(2,1)}, u32[]{:S(2)}, u32[]{:S(2)}) collective-permute-start(bf16[128,2560]{1,0:T(8,128)(2,1)} %shard_map.267), channel_id=1, source_target_pairs={{0,2},{1,3},{2,0},{3,1},{4,6},{5,7},{6,4},{7,5},{8,10},{9,11},{10,... | collective-permute-start | bytes 1966088 | tf_op jit(solution)/shard_map/ppermute | solution.py:69
  543.5 35.1 %collective-permute-start.71 = (bf16[264,2560]{1,0:T(8,128)(2,1)}, bf16[264,2560]{1,0:T(8,128)(2,1)}, u32[]{:S(2)}, u32[]{:S(2)}) collective-permute-start(bf16[264,2560]{1,0:T(8,128)(2,1)} %shard_map.271), channel_id=1, source_target_pairs={{0,2},{1,3},{2,0},{3,1},{4,6},{5,7},{6,4},{7,5},{8,10},{9,11},{10,... | collective-permute-start | bytes 4055048 | tf_op jit(solution)/shard_map/ppermute | solution.py:69
  554.7 27.8 %collective-permute-start.63 = (bf16[2,128,2560]{2,1,0:T(8,128)(2,1)}, bf16[2,128,2560]{2,1,0:T(8,128)(2,1)}, u32[]{:S(2)}, u32[]{:S(2)}) collective-permute-start(bf16[2,128,2560]{2,1,0:T(8,128)(2,1)} %pad_maximum_fusion.11), channel_id=1, source_target_pairs={{0,1},{1,0},{2,3},{3,2},{4,5},{5,4},{6,7},{7,6},{8,9},{9,8},{10,11... | collective-permute-start | bytes 3932168 | tf_op jit(solution)/shard_map/ppermute | solution.py:69
  562.6 152.7 %collective-permute-start.50 = (bf16[1024,2560]{1,0:T(8,128)(2,1)}, bf16[1024,2560]{1,0:T(8,128)(2,1)}, u32[]{:S(2)}, u32[]{:S(2)}) collective-permute-start(bf16[1024,2560]{1,0:T(8,128)(2,1)} %shard_map.265), channel_id=1, source_target_pairs={{0,1},{1,0},{2,3},{3,2},{4,5},{5,4},{6,7},{7,6},{8,9},{9,8},{10,11... | collective-permute-start | bytes 15728648 | tf_op jit(solution)/shard_map/ppermute | solution.py:188
  582.5 130.5 %collective-permute-start.72 = (bf16[2,264,2560]{2,1,0:T(8,128)(2,1)}, bf16[2,264,2560]{2,1,0:T(8,128)(2,1)}, u32[]{:S(2)}, u32[]{:S(2)}) collective-permute-start(bf16[2,264,2560]{2,1,0:T(8,128)(2,1)} %pad_maximum_fusion.2), channel_id=1, source_target_pairs={{0,1},{1,0},{2,3},{3,2},{4,5},{5,4},{6,7},{7,6},{8,9},{9,8},{10,11... | collective-permute-start | bytes 8110088 | tf_op jit(solution)/shard_map/ppermute | solution.py:69
  619.0 20.0 %collective-permute-start.89 = (bf16[128,1280]{1,0:T(8,128)(2,1)}, bf16[128,1280]{1,0:T(8,128)(2,1)S(1)}, u32[]{:S(2)}, u32[]{:S(2)}) collective-permute-start(bf16[128,1280]{1,0:T(8,128)(2,1)} %select_convert_fusion.4), channel_id=1, source_target_pairs={{0,16},{16,0},{1,17},{17,1},{2,18},{18,2},{3,19},{19,3},{4,20},{20... | collective-permute-start | bytes 983048 | tf_op jit(solution)/shard_map/ppermute | solution.py:132
  621.2 21.2 %collective-permute-start.64 = (bf16[1,256,768]{2,1,0:T(8,128)(2,1)}, bf16[1,256,768]{2,1,0:T(8,128)(2,1)}, u32[]{:S(2)}, u32[]{:S(2)}) collective-permute-start(bf16[1,256,768]{2,1,0:T(8,128)(2,1)} %constant_dynamic-slice_fusion.10), channel_id=1, source_target_pairs={{0,1},{1,0},{2,3},{3,2},{4,5},{5,4},{6,7},{7,6},{8,9},{9,8},{10,11... | collective-permute-start | bytes 1179656 | tf_op jit(solution)/shard_map/ppermute | solution.py:69
  626.4 32.0 %collective-permute-start.85 = (bf16[384,960]{0,1:T(8,128)(2,1)}, bf16[384,960]{0,1:T(8,128)(2,1)}, u32[]{:S(2)}, u32[]{:S(2)}) collective-permute-start(bf16[384,960]{0,1:T(8,128)(2,1)} %copy.430), channel_id=1, source_target_pairs={{0,16},{16,0},{1,17},{17,1},{2,18},{18,2},{3,19},{19,3},{4,20},{20... | collective-permute-start | bytes 2211848 | tf_op jit(solution)/shard_map/ppermute | solution.py:132
  662.5 18.3 %collective-permute-start.88 = (bf16[96,960]{1,0:T(8,128)(2,1)S(1)}, bf16[96,960]{1,0:T(8,128)(2,1)S(1)}, u32[]{:S(2)}, u32[]{:S(2)}) collective-permute-start(bf16[96,960]{1,0:T(8,128)(2,1)S(1)} %get-tuple-element.202), channel_id=1, source_target_pairs={{0,12},{4,0},{8,4},{12,8},{1,13},{5,1},{9,5},{13,9},{2,14},{6,2},{... | collective-permute-start | bytes 552968 | tf_op jit(solution)/shard_map/ppermute | solution.py:83
  666.4 33.7 %collective-permute-start.87 = (bf16[96,960]{1,0:T(8,128)(2,1)S(1)}, bf16[96,960]{1,0:T(8,128)(2,1)S(1)}, u32[]{:S(2)}, u32[]{:S(2)}) collective-permute-start(bf16[96,960]{1,0:T(8,128)(2,1)S(1)} %get-tuple-element.203), channel_id=1, source_target_pairs={{0,8},{4,12},{8,0},{12,4},{1,9},{5,13},{9,1},{13,5},{2,10},{6,14},... | collective-permute-start | bytes 552968 | tf_op jit(solution)/shard_map/ppermute | solution.py:83
  676.3 24.6 %collective-permute-start.66 = (bf16[1,256,384]{2,1,0:T(8,128)(2,1)S(1)}, bf16[1,256,384]{2,1,0:T(8,128)(2,1)S(1)}, u32[]{:S(2)}, u32[]{:S(2)}) collective-permute-start(bf16[1,256,384]{2,1,0:T(8,128)(2,1)S(1)} %get-tuple-element.208), channel_id=1, source_target_pairs={{0,4},{4,8},{8,12},{12,0},{1,5},{5,9},{9,13},{13,1},{2,6},{6,10},{... | collective-permute-start | bytes 589832 | tf_op jit(solution)/shard_map/ppermute | solution.py:83
  680.8 20.1 %collective-permute-start.68 = (bf16[1,256,384]{2,1,0:T(8,128)(2,1)S(1)}, bf16[1,256,384]{2,1,0:T(8,128)(2,1)S(1)}, u32[]{:S(2)}, u32[]{:S(2)}) collective-permute-start(bf16[1,256,384]{2,1,0:T(8,128)(2,1)S(1)} %get-tuple-element.209), channel_id=1, source_target_pairs={{0,12},{4,0},{8,4},{12,8},{1,13},{5,1},{9,5},{13,9},{2,14},{6,2},{... | collective-permute-start | bytes 589832 | tf_op jit(solution)/shard_map/ppermute | solution.py:83
  724.8 19.7 %collective-permute-start.57 = (bf16[2,1,2,128,768]{4,3,2,1,0:T(8,128)(2,1)}, bf16[2,1,2,128,768]{4,3,2,1,0:T(8,128)(2,1)}, u32[]{:S(2)}, u32[]{:S(2)}) collective-permute-start(bf16[2,1,2,128,768]{4,3,2,1,0:T(8,128)(2,1)} %slice.537), channel_id=1, source_target_pairs={{0,16},{16,0},{1,17},{17,1},{2,18},{18,2},{3,19},{19,3},{4,20},{20... | collective-permute-start | bytes 2359304 | tf_op jit(solution)/shard_map/ppermute | solution.py:188
  725.0 28.8 %collective-permute-start.51 = (bf16[2,2,1,128,896]{4,3,2,1,0:T(8,128)(2,1)}, bf16[2,2,1,128,896]{4,3,2,1,0:T(8,128)(2,1)}, u32[]{:S(2)}, u32[]{:S(2)}) collective-permute-start(bf16[2,2,1,128,896]{4,3,2,1,0:T(8,128)(2,1)} %slice.525), channel_id=1, source_target_pairs={{0,4},{4,0},{8,12},{12,8},{1,5},{5,1},{9,13},{13,9},{2,6},{6,2},{1... | collective-permute-start | bytes 2752520 | tf_op jit(solution)/shard_map/ppermute | solution.py:188
  729.3 28.7 %collective-permute-start.54 = (bf16[1,2,2,128,896]{4,3,2,1,0:T(8,128)(2,1)}, bf16[1,2,2,128,896]{4,3,2,1,0:T(8,128)(2,1)}, u32[]{:S(2)}, u32[]{:S(2)}) collective-permute-start(bf16[1,2,2,128,896]{4,3,2,1,0:T(8,128)(2,1)} %slice.531), channel_id=1, source_target_pairs={{0,2},{1,3},{2,0},{3,1},{4,6},{5,7},{6,4},{7,5},{8,10},{9,11},{10,... | collective-permute-start | bytes 2752520 | tf_op jit(solution)/shard_map/ppermute | solution.py:188
  741.0 30.4 %collective-permute-start.73 = (bf16[1200,320]{0,1:T(8,128)(2,1)}, bf16[1200,320]{0,1:T(8,128)(2,1)}, u32[]{:S(2)}, u32[]{:S(2)}) collective-permute-start(bf16[1200,320]{0,1:T(8,128)(2,1)} %bitcast.123), channel_id=1, source_target_pairs={{0,4},{4,0},{8,12},{12,8},{16,20},{20,16},{24,28},{28,24},{1,5},{5... | collective-permute-start | bytes 2304008 | tf_op jit(solution)/shard_map/ppermute | solution.py:493
  743.1 30.1 %collective-permute-start.74 = (bf16[1200,320]{0,1:T(8,128)(2,1)}, bf16[1200,320]{0,1:T(8,128)(2,1)}, u32[]{:S(2)}, u32[]{:S(2)}) collective-permute-start(bf16[1200,320]{0,1:T(8,128)(2,1)} %bitcast.486), channel_id=1, source_target_pairs={{0,16},{4,20},{8,24},{12,28},{16,0},{20,4},{24,8},{28,12},{1,17},{... | collective-permute-start | bytes 2304008 | tf_op jit(solution)/shard_map/ppermute | solution.py:493
  744.5 45.3 %collective-permute-start.75 = (bf16[1200,320]{0,1:T(8,128)(2,1)}, bf16[1200,320]{0,1:T(8,128)(2,1)}, u32[]{:S(2)}, u32[]{:S(2)}) collective-permute-start(bf16[1200,320]{0,1:T(8,128)(2,1)} %bitcast.485), channel_id=1, source_target_pairs={{0,20},{4,16},{8,28},{12,24},{16,4},{20,0},{24,12},{28,8},{1,21},{... | collective-permute-start | bytes 2304008 | tf_op jit(solution)/shard_map/ppermute | solution.py:493
  753.8 47.8 %collective-permute-start.58 = (bf16[1,1,2,128,768]{4,3,2,1,0:T(8,128)(2,1)}, bf16[1,1,2,128,768]{4,3,2,1,0:T(8,128)(2,1)}, u32[]{:S(2)}, u32[]{:S(2)}) collective-permute-start(bf16[1,1,2,128,768]{4,3,2,1,0:T(8,128)(2,1)} %slice.539), channel_id=1, source_target_pairs={{0,2},{1,3},{2,0},{3,1},{4,6},{5,7},{6,4},{7,5},{8,10},{9,11},{10,... | collective-permute-start | bytes 1179656 | tf_op jit(solution)/shard_map/ppermute | solution.py:188
  758.0 46.2 %collective-permute-start.52 = (bf16[2,1,1,128,896]{4,3,2,1,0:T(8,128)(2,1)}, bf16[2,1,1,128,896]{4,3,2,1,0:T(8,128)(2,1)}, u32[]{:S(2)}, u32[]{:S(2)}) collective-permute-start(bf16[2,1,1,128,896]{4,3,2,1,0:T(8,128)(2,1)} %slice.527), channel_id=1, source_target_pairs={{0,16},{16,0},{1,17},{17,1},{2,18},{18,2},{3,19},{19,3},{4,20},{20... | collective-permute-start | bytes 1376264 | tf_op jit(solution)/shard_map/ppermute | solution.py:188
  771.4 35.5 %collective-permute-start.55 = (bf16[1,2,1,128,896]{4,3,2,1,0:T(8,128)(2,1)}, bf16[1,2,1,128,896]{4,3,2,1,0:T(8,128)(2,1)}, u32[]{:S(2)}, u32[]{:S(2)}) collective-permute-start(bf16[1,2,1,128,896]{4,3,2,1,0:T(8,128)(2,1)} %slice.533), channel_id=1, source_target_pairs={{0,4},{4,0},{8,12},{12,8},{1,5},{5,1},{9,13},{13,9},{2,6},{6,2},{1... | collective-permute-start | bytes 1376264 | tf_op jit(solution)/shard_map/ppermute | solution.py:188
  773.2 35.5 %collective-permute-start.69 = (bf16[1,256,1152]{2,1,0:T(8,128)(2,1)}, bf16[1,256,1152]{2,1,0:T(8,128)(2,1)}, u32[]{:S(2)}, u32[]{:S(2)}) collective-permute-start(bf16[1,256,1152]{2,1,0:T(8,128)(2,1)} %shard_map.269), channel_id=1, source_target_pairs={{0,2},{1,3},{2,0},{3,1},{4,6},{5,7},{6,4},{7,5},{8,10},{9,11},{10,... | collective-permute-start | bytes 1769480 | tf_op jit(solution)/shard_map/ppermute | solution.py:69
  851.2 34.0 %collective-permute-start.76 = (bf16[128,2560]{1,0:T(8,128)(2,1)}, bf16[128,2560]{1,0:T(8,128)(2,1)}, u32[]{:S(2)}, u32[]{:S(2)}) collective-permute-start(bf16[128,2560]{1,0:T(8,128)(2,1)} %get-tuple-element.188), channel_id=1, source_target_pairs={{0,2},{1,3},{2,0},{3,1},{4,6},{5,7},{6,4},{7,5},{8,10},{9,11},{10,... | collective-permute-start | bytes 1966088 | tf_op jit(solution)/shard_map/ppermute | solution.py:69
  853.1 29.5 %collective-permute-start.60 = (bf16[128,2560]{1,0:T(8,128)(2,1)}, bf16[128,2560]{1,0:T(8,128)(2,1)}, u32[]{:S(2)}, u32[]{:S(2)}) collective-permute-start(bf16[128,2560]{1,0:T(8,128)(2,1)} %get-tuple-element.189), channel_id=1, source_target_pairs={{0,2},{1,3},{2,0},{3,1},{4,6},{5,7},{6,4},{7,5},{8,10},{9,11},{10,... | collective-permute-start | bytes 1966088 | tf_op jit(solution)/shard_map/ppermute | solution.py:69
  856.6 30.9 %collective-permute-start.78 = (bf16[1280,264]{0,1:T(8,128)(2,1)}, bf16[1280,264]{0,1:T(8,128)(2,1)}, u32[]{:S(2)}, u32[]{:S(2)}) collective-permute-start(bf16[1280,264]{0,1:T(8,128)(2,1)} %select_convert_fusion.2), channel_id=1, source_target_pairs={{0,16},{16,0},{1,17},{17,1},{2,18},{18,2},{3,19},{19,3},{4,20},{20... | collective-permute-start | bytes 2027528 | tf_op jit(solution)/shard_map/ppermute | solution.py:132
  885.2 45.9 %collective-permute-start.61 = (bf16[2,128,2560]{2,1,0:T(8,128)(2,1)}, bf16[2,128,2560]{2,1,0:T(8,128)(2,1)}, u32[]{:S(2)}, u32[]{:S(2)}) collective-permute-start(bf16[2,128,2560]{2,1,0:T(8,128)(2,1)} %pad_maximum_fusion.10), channel_id=1, source_target_pairs={{0,1},{1,0},{2,3},{3,2},{4,5},{5,4},{6,7},{7,6},{8,9},{9,8},{10,11... | collective-permute-start | bytes 3932168 | tf_op jit(solution)/shard_map/ppermute | solution.py:69
  902.6 17.3 %collective-permute-start.79 = (bf16[4,80,264]{2,1,0:T(8,128)(2,1)}, bf16[4,80,264]{2,1,0:T(8,128)(2,1)}, u32[]{:S(2)}, u32[]{:S(2)}) collective-permute-start(bf16[4,80,264]{2,1,0:T(8,128)(2,1)} %bitcast.493), channel_id=1, source_target_pairs={{0,4},{4,8},{8,12},{12,0},{1,5},{5,9},{9,13},{13,1},{2,6},{6,10},{... | collective-permute-start | bytes 506888 | tf_op jit(solution)/shard_map/ppermute | solution.py:83
  905.5 30.3 %collective-permute-start.77 = (bf16[2,128,2560]{2,1,0:T(8,128)(2,1)}, bf16[2,128,2560]{2,1,0:T(8,128)(2,1)}, u32[]{:S(2)}, u32[]{:S(2)}) collective-permute-start(bf16[2,128,2560]{2,1,0:T(8,128)(2,1)} %pad_maximum_fusion.12), channel_id=1, source_target_pairs={{0,1},{1,0},{2,3},{3,2},{4,5},{5,4},{6,7},{7,6},{8,9},{9,8},{10,11... | collective-permute-start | bytes 3932168 | tf_op jit(solution)/shard_map/ppermute | solution.py:69
  (189 other events, 2580.5 us)
Sparse Core Ops, SparseCore 0:
  10.5 99.2 all-gather.3
  201.3 144.4 all-gather.5
  492.8 140.7 reduce-scatter.2
  637.4 101.5 reduce-scatter.4
